TPU v7x, 32 devices: a whole 2x2x4 slice. The times are simulated.
32 devices in a mesh: wide: 16 (over z, x, core), tensor: 2 (over y).
Axes of the slice: x: 2, y: 2, z: 4, core: 2. Of those that a mesh axis runs over, the one named last changes fastest.
Arguments:
- images: bfloat16 [18464, 1024], P('wide', 'tensor'), may hold values from -6 to 6
- first_gain: bfloat16 [2, 1024], replicated, may hold values from 0.5 to 1.5
- first_shift: bfloat16 [2, 1024], replicated, may hold values from -3 to 3
- query_weight: bfloat16 [2, 1024, 1024], P(None, 'wide', 'tensor'), may hold values from -0.1875 to 0.1875
- key_weight: bfloat16 [2, 1024, 1024], P(None, 'wide', 'tensor'), may hold values from -0.1875 to 0.1875
- value_weight: bfloat16 [2, 1024, 1024], P(None, 'wide', 'tensor'), may hold values from -0.1875 to 0.1875
- query_bias: bfloat16 [2, 1024], P(None, 'tensor'), may hold values from -3 to 3
- value_bias: bfloat16 [2, 1024], P(None, 'tensor'), may hold values from -3 to 3
- out_weight: bfloat16 [2, 1024, 1024], P(None, 'tensor', 'wide'), may hold values from -3 to 3
- out_bias: bfloat16 [2, 1024], P(None, 'tensor'), may hold values from -2 to 2
- second_gain: bfloat16 [2, 1024], replicated, may hold values from 0.5 to 1.5
- second_shift: bfloat16 [2, 1024], replicated, may hold values from -3 to 3
- up_weight: bfloat16 [2, 1024, 4096], P(None, 'wide', 'tensor'), may hold values from -0.1875 to 0.1875
- up_bias: bfloat16 [2, 4096], P(None, 'tensor'), may hold values from -3 to 3
- down_weight: bfloat16 [2, 4096, 1024], P(None, 'tensor', 'wide'), may hold values from -0.09375 to 0.09375
- down_bias: bfloat16 [2, 1024], P(None, 'tensor'), may hold values from -2 to 2
- cotangent: bfloat16 [18464, 1024], P('wide', 'tensor'), may hold values from -6 to 6
Outputs:
- activations: bfloat16 [18464, 1024], P('wide', 'tensor')
- input_gradient: float32 [18464, 1024], P('wide', 'tensor')
- query_weight_gradient: float32 [2, 1024, 1024], P(None, 'wide', 'tensor')
- key_weight_gradient: float32 [2, 1024, 1024], P(None, 'wide', 'tensor')
- value_weight_gradient: float32 [2, 1024, 1024], P(None, 'wide', 'tensor')
- out_weight_gradient: float32 [2, 1024, 1024], P(None, 'tensor', 'wide')
- up_weight_gradient: float32 [2, 1024, 4096], P(None, 'wide', 'tensor')
- down_weight_gradient: float32 [2, 4096, 1024], P(None, 'tensor', 'wide')
- query_bias_gradient: float32 [2, 1024], replicated
- value_bias_gradient: float32 [2, 1024], replicated
- out_bias_gradient: float32 [2, 1024], replicated
- up_bias_gradient: float32 [2, 4096], replicated
- down_bias_gradient: float32 [2, 1024], replicated
- first_gain_gradient: float32 [2, 1024], replicated
- first_shift_gradient: float32 [2, 1024], replicated
- second_gain_gradient: float32 [2, 1024], replicated
- second_shift_gradient: float32 [2, 1024], replicated
All inputs are finite; a program needn't handle non-finite values.
Results may differ from a plain program's by a relative error of at most 0.018.
Values may be sent and summed in bfloat16 or wider, within the bound.
A program may use at most 320 MiB of HBM per device.

v0:
```python
import jax
import jax.numpy as jnp
from jax import lax
from jax.sharding import PartitionSpec as P

HEAD_DIM = 64
SEQ = 577
MICRO = 2


norm_eps = 1e-06


def row_totals(first_terms, second_terms):
    return lax.psum((first_terms, second_terms), "tensor")


def full_rows(share_low):
    return lax.all_gather(share_low, "tensor", axis=1, tiled=True)


def feature_total(partial_sums):
    return lax.psum_scatter(
        partial_sums.astype(jnp.bfloat16), "tensor", scatter_dimension=1, tiled=True
    ).astype(jnp.float32)


def fetch_weights(query_block, key_block, value_block, out_block, up_block, down_block):
    return (
        lax.all_gather(query_block, "wide", axis=0, tiled=True),
        lax.all_gather(key_block, "wide", axis=0, tiled=True),
        lax.all_gather(value_block, "wide", axis=0, tiled=True),
        lax.all_gather(out_block, "wide", axis=1, tiled=True),
        lax.all_gather(up_block, "wide", axis=0, tiled=True),
        lax.all_gather(down_block, "wide", axis=1, tiled=True),
    )


def settle_grads(query_piece, key_piece, value_piece, out_piece, up_piece, down_piece):
    return (
        lax.psum_scatter(
            query_piece.astype(jnp.bfloat16), "wide", scatter_dimension=0, tiled=True
        ).astype(jnp.float32),
        lax.psum_scatter(
            key_piece.astype(jnp.bfloat16), "wide", scatter_dimension=0, tiled=True
        ).astype(jnp.float32),
        lax.psum_scatter(
            value_piece.astype(jnp.bfloat16), "wide", scatter_dimension=0, tiled=True
        ).astype(jnp.float32),
        lax.psum_scatter(
            out_piece.astype(jnp.bfloat16), "wide", scatter_dimension=1, tiled=True
        ).astype(jnp.float32),
        lax.psum_scatter(
            up_piece.astype(jnp.bfloat16), "wide", scatter_dimension=0, tiled=True
        ).astype(jnp.float32),
        lax.psum_scatter(
            down_piece.astype(jnp.bfloat16), "wide", scatter_dimension=1, tiled=True
        ).astype(jnp.float32),
    )


def add_terms(earlier, latest):
    if earlier is None:
        return latest
    return jax.tree.map(jnp.add, earlier, latest)


def norm_forward(stream, gain, shift, full_width):
    first_terms, second_terms = row_totals(
        jnp.sum(stream, axis=1), jnp.sum(stream * stream, axis=1)
    )
    row_mean = first_terms / full_width
    inverse_std = lax.rsqrt(second_terms / full_width - row_mean * row_mean + norm_eps)
    centred = (stream - row_mean[:, None]) * inverse_std[:, None]
    return (centred * gain + shift, centred, inverse_std)


def norm_backward(upstream, centred, inverse_std, gain, full_width):
    scaled = upstream * gain
    first_terms, second_terms = row_totals(
        jnp.sum(scaled, axis=1), jnp.sum(scaled * centred, axis=1)
    )
    return inverse_std[:, None] * (
        scaled - first_terms[:, None] / full_width - centred * (second_terms[:, None] / full_width)
    )


def attention_forward(queries, keys_here, values_here, image_count, heads_here):
    score_scale = HEAD_DIM ** (-0.5)
    shape_four = (image_count, SEQ, heads_here, HEAD_DIM)
    query_four = queries.reshape(shape_four)
    key_four = keys_here.reshape(shape_four)
    value_four = values_here.reshape(shape_four)
    scores = (
        jnp.einsum("iqhd,ikhd->ihqk", query_four, key_four, preferred_element_type=jnp.float32)
        * score_scale
    )
    row_peak = jnp.max(scores, axis=-1, keepdims=True)
    exponent = jnp.exp(scores - row_peak)
    row_total = jnp.sum(exponent, axis=-1, keepdims=True)
    weights_soft = (exponent / row_total).astype(jnp.bfloat16)
    mixed_heads = jnp.einsum(
        "ihqk,ikhd->iqhd", weights_soft, value_four, preferred_element_type=jnp.float32
    )
    log_total = row_peak[..., 0] + jnp.log(row_total[..., 0])
    return (mixed_heads.reshape(queries.shape).astype(jnp.bfloat16), log_total)


def attention_backward(
    queries, keys_here, values_here, log_total, mixed_grad, image_count, heads_here
):
    score_scale = HEAD_DIM ** (-0.5)
    shape_four = (image_count, SEQ, heads_here, HEAD_DIM)
    query_four = queries.reshape(shape_four)
    key_four = keys_here.reshape(shape_four)
    value_four = values_here.reshape(shape_four)
    grad_four = mixed_grad.reshape(shape_four)
    scores = (
        jnp.einsum("iqhd,ikhd->ihqk", query_four, key_four, preferred_element_type=jnp.float32)
        * score_scale
    )
    weights_soft = jnp.exp(scores - log_total[..., None])
    weight_grad = jnp.einsum(
        "iqhd,ikhd->ihqk", grad_four, value_four, preferred_element_type=jnp.float32
    )
    row_delta = jnp.sum(weight_grad * weights_soft, axis=-1, keepdims=True)
    score_grad = (weights_soft * (weight_grad - row_delta)).astype(jnp.bfloat16)
    query_grad = (
        jnp.einsum("ihqk,ikhd->iqhd", score_grad, key_four, preferred_element_type=jnp.float32)
        * score_scale
    )
    key_grad = (
        jnp.einsum("ihqk,iqhd->ikhd", score_grad, query_four, preferred_element_type=jnp.float32)
        * score_scale
    )
    value_grad = jnp.einsum(
        "ihqk,iqhd->ikhd",
        weights_soft.astype(jnp.bfloat16),
        grad_four,
        preferred_element_type=jnp.float32,
    )
    flat_shape = queries.shape
    return (
        query_grad.reshape(flat_shape),
        key_grad.reshape(flat_shape),
        value_grad.reshape(flat_shape),
    )


def gelu_slope(values):
    normal_cdf = 0.5 * (1.0 + lax.erf(values * 0.7071067811865476))
    return normal_cdf + values * jnp.exp(-0.5 * values * values) * 0.3989422804014327


def body(
    images,
    first_gain,
    first_shift,
    query_weight,
    key_weight,
    value_weight,
    query_bias,
    value_bias,
    out_weight,
    out_bias,
    second_gain,
    second_shift,
    up_weight,
    up_bias,
    down_weight,
    down_bias,
    cotangent,
):
    layer_count = query_weight.shape[0]
    feature_block = images.shape[1]
    tensor_count = lax.axis_size("tensor")
    full_width = feature_block * tensor_count
    heads_here = feature_block // HEAD_DIM
    tensor_place = lax.axis_index("tensor")
    micro_rows = images.shape[0] // MICRO
    image_count = micro_rows // SEQ

    def gain_share(param_table, layer_idx):
        return lax.dynamic_slice_in_dim(
            param_table[layer_idx], tensor_place * feature_block, feature_block
        )

    def layer_weights(layer_idx):
        return fetch_weights(
            query_weight[layer_idx],
            key_weight[layer_idx],
            value_weight[layer_idx],
            out_weight[layer_idx],
            up_weight[layer_idx],
            down_weight[layer_idx],
        )

    weight_sums = [None] * layer_count
    small_sums = [None] * layer_count
    activation_parts = []
    gradient_parts = []
    for micro_idx in range(MICRO):
        row_start = micro_idx * micro_rows
        stream = images[row_start : row_start + micro_rows].astype(jnp.float32)
        saved_state = []
        for layer_idx in range(layer_count):
            query_full, key_full, value_full, out_full, up_full, down_full = layer_weights(
                layer_idx
            )
            normed, centred_one, inverse_one = norm_forward(
                stream,
                gain_share(first_gain, layer_idx),
                gain_share(first_shift, layer_idx),
                full_width,
            )
            normed_full = full_rows(normed.astype(jnp.bfloat16))
            joined_weight = jnp.concatenate((query_full, key_full, value_full), axis=1)
            projected = jnp.dot(normed_full, joined_weight, preferred_element_type=jnp.float32)
            queries = (projected[:, :feature_block] + query_bias[layer_idx]).astype(jnp.bfloat16)
            keys_here = projected[:, feature_block : 2 * feature_block].astype(jnp.bfloat16)
            values_here = (projected[:, 2 * feature_block :] + value_bias[layer_idx]).astype(
                jnp.bfloat16
            )
            mixed_heads, log_total = attention_forward(
                queries, keys_here, values_here, image_count, heads_here
            )
            attention_sum = feature_total(
                jnp.dot(mixed_heads, out_full, preferred_element_type=jnp.float32)
            )
            after_attention = stream + attention_sum + out_bias[layer_idx]
            normed_two, centred_two, inverse_two = norm_forward(
                after_attention,
                gain_share(second_gain, layer_idx),
                gain_share(second_shift, layer_idx),
                full_width,
            )
            normed_two_full = full_rows(normed_two.astype(jnp.bfloat16))
            hidden_pre = (
                jnp.dot(normed_two_full, up_full, preferred_element_type=jnp.float32)
                + up_bias[layer_idx]
            )
            hidden = jax.nn.gelu(hidden_pre, approximate=False).astype(jnp.bfloat16)
            feedforward_sum = feature_total(
                jnp.dot(hidden, down_full, preferred_element_type=jnp.float32)
            )
            saved_state.append(
                (
                    centred_one,
                    inverse_one,
                    normed_full,
                    queries,
                    keys_here,
                    values_here,
                    mixed_heads,
                    log_total,
                    centred_two,
                    inverse_two,
                    normed_two_full,
                    hidden_pre,
                    hidden,
                )
            )
            stream = after_attention + feedforward_sum + down_bias[layer_idx]
        activation_parts.append(stream.astype(jnp.bfloat16))
        upstream = cotangent[row_start : row_start + micro_rows].astype(jnp.float32)
        for layer_idx in reversed(range(layer_count)):
            query_full, key_full, value_full, out_full, up_full, down_full = layer_weights(
                layer_idx
            )
            (
                centred_one,
                inverse_one,
                normed_full,
                queries,
                keys_here,
                values_here,
                mixed_heads,
                log_total,
                centred_two,
                inverse_two,
                normed_two_full,
                hidden_pre,
                hidden,
            ) = saved_state[layer_idx]
            down_bias_term = jnp.sum(upstream, axis=0)
            upstream_full = full_rows(upstream.astype(jnp.bfloat16))
            down_term = jnp.einsum(
                "rc,rd->cd", hidden, upstream_full, preferred_element_type=jnp.float32
            )
            hidden_grad = jnp.einsum(
                "rd,cd->rc", upstream_full, down_full, preferred_element_type=jnp.float32
            )
            pre_grad = (hidden_grad * gelu_slope(hidden_pre)).astype(jnp.bfloat16)
            up_bias_term = jnp.sum(pre_grad.astype(jnp.float32), axis=0)
            up_term = jnp.einsum(
                "rd,rc->dc", normed_two_full, pre_grad, preferred_element_type=jnp.float32
            )
            normed_two_grad = feature_total(
                jnp.einsum("rc,dc->rd", pre_grad, up_full, preferred_element_type=jnp.float32)
            )
            second_gain_term = jnp.sum(normed_two_grad * centred_two, axis=0)
            second_shift_term = jnp.sum(normed_two_grad, axis=0)
            upstream = upstream + norm_backward(
                normed_two_grad,
                centred_two,
                inverse_two,
                gain_share(second_gain, layer_idx),
                full_width,
            )
            out_bias_term = jnp.sum(upstream, axis=0)
            upstream_full = full_rows(upstream.astype(jnp.bfloat16))
            out_term = jnp.einsum(
                "rc,rd->cd", mixed_heads, upstream_full, preferred_element_type=jnp.float32
            )
            mixed_grad = jnp.einsum(
                "rd,cd->rc", upstream_full, out_full, preferred_element_type=jnp.float32
            ).astype(jnp.bfloat16)
            query_grad, key_grad, value_grad = attention_backward(
                queries, keys_here, values_here, log_total, mixed_grad, image_count, heads_here
            )
            joined_grad = jnp.concatenate((query_grad, key_grad, value_grad), axis=1).astype(
                jnp.bfloat16
            )
            joined_float = joined_grad.astype(jnp.float32)
            query_bias_term = jnp.sum(joined_float[:, :feature_block], axis=0)
            value_bias_term = jnp.sum(joined_float[:, 2 * feature_block :], axis=0)
            joined_term = jnp.einsum(
                "rd,rc->dc", normed_full, joined_grad, preferred_element_type=jnp.float32
            )
            joined_weight = jnp.concatenate((query_full, key_full, value_full), axis=1)
            normed_grad = feature_total(
                jnp.einsum(
                    "rc,dc->rd", joined_grad, joined_weight, preferred_element_type=jnp.float32
                )
            )
            first_gain_term = jnp.sum(normed_grad * centred_one, axis=0)
            first_shift_term = jnp.sum(normed_grad, axis=0)
            upstream = upstream + norm_backward(
                normed_grad, centred_one, inverse_one, gain_share(first_gain, layer_idx), full_width
            )
            query_term = joined_term[:, :feature_block]
            key_term = joined_term[:, feature_block : 2 * feature_block]
            value_term = joined_term[:, 2 * feature_block :]
            weight_sums[layer_idx] = add_terms(
                weight_sums[layer_idx],
                settle_grads(query_term, key_term, value_term, out_term, up_term, down_term),
            )
            small_sums[layer_idx] = add_terms(
                small_sums[layer_idx],
                (
                    query_bias_term,
                    value_bias_term,
                    out_bias_term,
                    up_bias_term,
                    down_bias_term,
                    first_gain_term,
                    first_shift_term,
                    second_gain_term,
                    second_shift_term,
                ),
            )
        gradient_parts.append(upstream)
    share_sets = []
    for layer_idx in range(layer_count):
        share_sets.append(weight_sums[layer_idx])
    weight_outputs = [
        jnp.stack([share_sets[layer_idx][entry_idx] for layer_idx in range(layer_count)])
        for entry_idx in range(6)
    ]
    small_stack = [
        jnp.stack([small_sums[layer_idx][entry_idx] for layer_idx in range(layer_count)])
        for entry_idx in range(9)
    ]
    widened = [
        lax.dynamic_update_slice_in_dim(
            jnp.zeros((layer_count, share_piece.shape[1] * tensor_count), jnp.float32),
            share_piece,
            tensor_place * share_piece.shape[1],
            1,
        )
        for share_piece in small_stack
    ]
    totals = lax.psum(
        (
            widened[0],
            widened[1],
            widened[2],
            widened[3],
            widened[4],
            widened[5],
            widened[6],
            widened[7],
            widened[8],
        ),
        ("wide", "tensor"),
    )
    activations = jnp.concatenate(activation_parts, axis=0)
    input_gradient = jnp.concatenate(gradient_parts, axis=0)
    return (
        activations,
        input_gradient,
        weight_outputs[0],
        weight_outputs[1],
        weight_outputs[2],
        weight_outputs[3],
        weight_outputs[4],
        weight_outputs[5],
        totals[0],
        totals[1],
        totals[2],
        totals[3],
        totals[4],
        totals[5],
        totals[6],
        totals[7],
        totals[8],
    )


def solution(mesh):
    in_specs = (
        P("wide", "tensor"),
        P(),
        P(),
        P(None, "wide", "tensor"),
        P(None, "wide", "tensor"),
        P(None, "wide", "tensor"),
        P(None, "tensor"),
        P(None, "tensor"),
        P(None, "tensor", "wide"),
        P(None, "tensor"),
        P(),
        P(),
        P(None, "wide", "tensor"),
        P(None, "tensor"),
        P(None, "tensor", "wide"),
        P(None, "tensor"),
        P("wide", "tensor"),
    )
    out_specs = (
        P("wide", "tensor"),
        P("wide", "tensor"),
        P(None, "wide", "tensor"),
        P(None, "wide", "tensor"),
        P(None, "wide", "tensor"),
        P(None, "tensor", "wide"),
        P(None, "wide", "tensor"),
        P(None, "tensor", "wide"),
        P(),
        P(),
        P(),
        P(),
        P(),
        P(),
        P(),
        P(),
        P(),
    )
    return jax.shard_map(body, mesh=mesh, in_specs=in_specs, out_specs=out_specs, check_vma=False)
```

profile of v0, /device:TPU:0, one launch (start us, length us, event | category | flops | bytes accessed | tf_op | source)
XLA Modules:
  0.0 3117.9 jit_solution(15028014547809773235)
XLA Ops:
  318.8 53.3 %all-gather.81.cloned.1.call-done = bf16[1,1024,2048]{2,1,0:T(8,128)(2,1)} async-done(((bf16[1,64,2048]{2,1,0:T(8,128)(2,1)}), bf16[1,1024,2048]{2,1,0:T(8,128)(2,1)}) %all-gather.81.cloned.1.call-update) | async-done | bytes 4194320 | tf_op jit(solution)/shard_map/all_gather | solution.py:34
  857.0 53.3 %all-gather.95.cloned.1.call-done = bf16[1,2048,1024]{1,2,0:T(8,128)(2,1)} async-done(((bf16[1,2048,64]{1,2,0:T(8,128)(2,1)}), bf16[1,2048,1024]{1,2,0:T(8,128)(2,1)}) %all-gather.95.cloned.1.call-update) | async-done | bytes 4194320 | tf_op jit(solution)/shard_map/all_gather | solution.py:35
  1530.8 60.3 %reduce-scatter.93.cloned.1.call-done = bf16[64,512]{1,0:T(8,128)(2,1)} async-done(((bf16[1024,512]{1,0:T(8,128)(2,1)}), bf16[64,512]{1,0:T(8,128)(2,1)}) %reduce-scatter.93.cloned.1.call-update) | async-done | bytes 65552 | tf_op jit(solution)/shard_map/reduce_scatter | solution.py:47
  1592.7 58.9 %reduce-scatter.87.cloned.1.call-done = bf16[64,512]{1,0:T(8,128)(2,1)} async-done(((bf16[1024,512]{1,0:T(8,128)(2,1)}), bf16[64,512]{1,0:T(8,128)(2,1)}) %reduce-scatter.87.cloned.1.call-update) | async-done | bytes 65552 | tf_op jit(solution)/shard_map/reduce_scatter | solution.py:44
  1651.6 60.3 %reduce-scatter.85.cloned.1.call-done = bf16[64,512]{1,0:T(8,128)(2,1)} async-done(((bf16[1024,512]{1,0:T(8,128)(2,1)}), bf16[64,512]{1,0:T(8,128)(2,1)}) %reduce-scatter.85.cloned.1.call-update) | async-done | bytes 65552 | tf_op jit(solution)/shard_map/reduce_scatter | solution.py:44
  1712.9 59.1 %reduce-scatter.79.cloned.1.call-done = bf16[64,512]{1,0:T(8,128)(2,1)} async-done(((bf16[1024,512]{1,0:T(8,128)(2,1)}), bf16[64,512]{1,0:T(8,128)(2,1)}) %reduce-scatter.79.cloned.1.call-update) | async-done | bytes 65552 | tf_op jit(solution)/shard_map/reduce_scatter | solution.py:41
  1772.0 60.5 %reduce-scatter.77.cloned.1.call-done = bf16[64,512]{1,0:T(8,128)(2,1)} async-done(((bf16[1024,512]{1,0:T(8,128)(2,1)}), bf16[64,512]{1,0:T(8,128)(2,1)}) %reduce-scatter.77.cloned.1.call-update) | async-done | bytes 65552 | tf_op jit(solution)/shard_map/reduce_scatter | solution.py:41
  1841.2 66.5 %reduce-scatter.119.cloned.1.call-done = bf16[2048,64]{0,1:T(8,128)(2,1)} async-done(((bf16[2048,1024]{0,1:T(8,128)(2,1)}), bf16[2048,64]{0,1:T(8,128)(2,1)}) %reduce-scatter.119.cloned.1.call-update) | async-done | bytes 262160 | tf_op jit(solution)/shard_map/reduce_scatter | solution.py:56
  1907.7 75.8 %reduce-scatter.117.cloned.1.call-done = bf16[2048,64]{0,1:T(8,128)(2,1)} async-done(((bf16[2048,1024]{0,1:T(8,128)(2,1)}), bf16[2048,64]{0,1:T(8,128)(2,1)}) %reduce-scatter.117.cloned.1.call-update) | async-done | bytes 262160 | tf_op jit(solution)/shard_map/reduce_scatter | solution.py:56
  1985.3 73.3 %reduce-scatter.111.cloned.1.call-done = bf16[64,2048]{1,0:T(8,128)(2,1)} async-done(((bf16[1024,2048]{1,0:T(8,128)(2,1)}), bf16[64,2048]{1,0:T(8,128)(2,1)}) %reduce-scatter.111.cloned.1.call-update) | async-done | bytes 262160 | tf_op jit(solution)/shard_map/reduce_scatter | solution.py:53
  2058.6 76.1 %reduce-scatter.109.cloned.1.call-done = bf16[64,2048]{1,0:T(8,128)(2,1)} async-done(((bf16[1024,2048]{1,0:T(8,128)(2,1)}), bf16[64,2048]{1,0:T(8,128)(2,1)}) %reduce-scatter.109.cloned.1.call-update) | async-done | bytes 262160 | tf_op jit(solution)/shard_map/reduce_scatter | solution.py:53
  2139.3 55.4 %reduce-scatter.97.cloned.1.call-done = bf16[512,64]{0,1:T(8,128)(2,1)} async-done(((bf16[512,1024]{0,1:T(8,128)(2,1)}), bf16[512,64]{0,1:T(8,128)(2,1)}) %reduce-scatter.97.cloned.1.call-update) | async-done | bytes 65552 | tf_op jit(solution)/shard_map/reduce_scatter | solution.py:50
  2194.7 60.5 %reduce-scatter.99.cloned.1.call-done = bf16[512,64]{0,1:T(8,128)(2,1)} async-done(((bf16[512,1024]{0,1:T(8,128)(2,1)}), bf16[512,64]{0,1:T(8,128)(2,1)}) %reduce-scatter.99.cloned.1.call-update) | async-done | bytes 65552 | tf_op jit(solution)/shard_map/reduce_scatter | solution.py:50
  2257.8 57.5 %reduce-scatter.89.cloned.1.call-done = bf16[64,512]{1,0:T(8,128)(2,1)} async-done(((bf16[1024,512]{1,0:T(8,128)(2,1)}), bf16[64,512]{1,0:T(8,128)(2,1)}) %reduce-scatter.89.cloned.1.call-update) | async-done | bytes 65552 | tf_op jit(solution)/shard_map/reduce_scatter | solution.py:47
  2315.3 60.3 %reduce-scatter.91.cloned.1.call-done = bf16[64,512]{1,0:T(8,128)(2,1)} async-done(((bf16[1024,512]{1,0:T(8,128)(2,1)}), bf16[64,512]{1,0:T(8,128)(2,1)}) %reduce-scatter.91.cloned.1.call-update) | async-done | bytes 65552 | tf_op jit(solution)/shard_map/reduce_scatter | solution.py:47
  2377.3 58.3 %reduce-scatter.81.cloned.1.call-done = bf16[64,512]{1,0:T(8,128)(2,1)} async-done(((bf16[1024,512]{1,0:T(8,128)(2,1)}), bf16[64,512]{1,0:T(8,128)(2,1)}) %reduce-scatter.81.cloned.1.call-update) | async-done | bytes 65552 | tf_op jit(solution)/shard_map/reduce_scatter | solution.py:44
  2435.6 60.5 %reduce-scatter.83.cloned.1.call-done = bf16[64,512]{1,0:T(8,128)(2,1)} async-done(((bf16[1024,512]{1,0:T(8,128)(2,1)}), bf16[64,512]{1,0:T(8,128)(2,1)}) %reduce-scatter.83.cloned.1.call-update) | async-done | bytes 65552 | tf_op jit(solution)/shard_map/reduce_scatter | solution.py:44
  2497.7 58.4 %reduce-scatter.73.cloned.1.call-done = bf16[64,512]{1,0:T(8,128)(2,1)} async-done(((bf16[1024,512]{1,0:T(8,128)(2,1)}), bf16[64,512]{1,0:T(8,128)(2,1)}) %reduce-scatter.73.cloned.1.call-update) | async-done | bytes 65552 | tf_op jit(solution)/shard_map/reduce_scatter | solution.py:41
  2556.1 60.5 %reduce-scatter.75.cloned.1.call-done = bf16[64,512]{1,0:T(8,128)(2,1)} async-done(((bf16[1024,512]{1,0:T(8,128)(2,1)}), bf16[64,512]{1,0:T(8,128)(2,1)}) %reduce-scatter.75.cloned.1.call-update) | async-done | bytes 65552 | tf_op jit(solution)/shard_map/reduce_scatter | solution.py:41
  2678.0 62.5 %reduce-scatter.115.cloned.1.call-done = bf16[2048,64]{0,1:T(8,128)(2,1)} async-done(((bf16[2048,1024]{0,1:T(8,128)(2,1)}), bf16[2048,64]{0,1:T(8,128)(2,1)}) %reduce-scatter.115.cloned.1.call-update) | async-done | bytes 262160 | tf_op jit(solution)/shard_map/reduce_scatter | solution.py:56
  2740.5 75.7 %reduce-scatter.113.cloned.1.call-done = bf16[2048,64]{0,1:T(8,128)(2,1)} async-done(((bf16[2048,1024]{0,1:T(8,128)(2,1)}), bf16[2048,64]{0,1:T(8,128)(2,1)}) %reduce-scatter.113.cloned.1.call-update) | async-done | bytes 262160 | tf_op jit(solution)/shard_map/reduce_scatter | solution.py:56
  2818.4 73.3 %reduce-scatter.105.cloned.1.call-done = bf16[64,2048]{1,0:T(8,128)(2,1)} async-done(((bf16[1024,2048]{1,0:T(8,128)(2,1)}), bf16[64,2048]{1,0:T(8,128)(2,1)}) %reduce-scatter.105.cloned.1.call-update) | async-done | bytes 262160 | tf_op jit(solution)/shard_map/reduce_scatter | solution.py:53
  2891.6 75.7 %reduce-scatter.107.cloned.1.call-done = bf16[64,2048]{1,0:T(8,128)(2,1)} async-done(((bf16[1024,2048]{1,0:T(8,128)(2,1)}), bf16[64,2048]{1,0:T(8,128)(2,1)}) %reduce-scatter.107.cloned.1.call-update) | async-done | bytes 262160 | tf_op jit(solution)/shard_map/reduce_scatter | solution.py:53
  2969.5 129.7 %all-reduce.11.cloned.1.call-done = (f32[2,1024]{1,0:T(2,128)}, f32[2,1024]{1,0:T(2,128)}, f32[2,1024]{1,0:T(2,128)}, f32[2,4096]{1,0:T(2,128)}, f32[2,1024]{1,0...) async-done(((f32[2,1024]{1,0:T(2,128)}, f32[2,1024]{1,0:T(2,128)}, f32[2,1024]{1,0:T(2,128)}, f32[2,4096]{1,0:T(2,128)}, ...) | async-done | bytes 98320 | tf_op jit(solution)/shard_map/psum | solution.py:383
  (924 shorter events, 1513.3 us)
Async XLA Ops:
  1316.9 274.3 %reduce-scatter.93.cloned.1.call-start = ((), (), s32[]{:S(2)}) async-start(), calls=%async_computation.82 | async-start | bytes 1114112 | tf_op jit(solution)/shard_map/reduce_scatter | solution.py:47
  1324.2 327.4 %reduce-scatter.87.cloned.1.call-start = ((), (), s32[]{:S(2)}) async-start(), calls=%async_computation.79 | async-start | bytes 1114112 | tf_op jit(solution)/shard_map/reduce_scatter | solution.py:44
  1324.8 387.1 %reduce-scatter.85.cloned.1.call-start = ((), (), s32[]{:S(2)}) async-start(), calls=%async_computation.78 | async-start | bytes 1114112 | tf_op jit(solution)/shard_map/reduce_scatter | solution.py:44
  1325.4 446.6 %reduce-scatter.79.cloned.1.call-start = ((), (), s32[]{:S(2)}) async-start(), calls=%async_computation.75 | async-start | bytes 1114112 | tf_op jit(solution)/shard_map/reduce_scatter | solution.py:41
  1326.0 506.5 %reduce-scatter.77.cloned.1.call-start = ((), (), s32[]{:S(2)}) async-start(), calls=%async_computation.74 | async-start | bytes 1114112 | tf_op jit(solution)/shard_map/reduce_scatter | solution.py:41
  1326.7 580.9 %reduce-scatter.119.cloned.1.call-start = ((), (), s32[]{:S(2)}) async-start(), calls=%async_computation.95 | async-start | bytes 4456448 | tf_op jit(solution)/shard_map/reduce_scatter | solution.py:56
  1333.5 649.9 %reduce-scatter.117.cloned.1.call-start = ((), (), s32[]{:S(2)}) async-start(), calls=%async_computation.94 | async-start | bytes 4456448 | tf_op jit(solution)/shard_map/reduce_scatter | solution.py:56
  1341.6 717.0 %reduce-scatter.111.cloned.1.call-start = ((), (), s32[]{:S(2)}) async-start(), calls=%async_computation.91 | async-start | bytes 4456448 | tf_op jit(solution)/shard_map/reduce_scatter | solution.py:53
  1349.7 785.0 %reduce-scatter.109.cloned.1.call-start = ((), (), s32[]{:S(2)}) async-start(), calls=%async_computation.90 | async-start | bytes 4456448 | tf_op jit(solution)/shard_map/reduce_scatter | solution.py:53
  1357.7 837.1 %reduce-scatter.97.cloned.1.call-start = ((), (), s32[]{:S(2)}) async-start(), calls=%async_computation.84 | async-start | bytes 1114112 | tf_op jit(solution)/shard_map/reduce_scatter | solution.py:50
  1367.3 888.0 %reduce-scatter.99.cloned.1.call-start = ((), (), s32[]{:S(2)}) async-start(), calls=%async_computation.85 | async-start | bytes 1114112 | tf_op jit(solution)/shard_map/reduce_scatter | solution.py:50
  1396.4 918.9 %reduce-scatter.89.cloned.1.call-start = ((), (), s32[]{:S(2)}) async-start(), calls=%async_computation.80 | async-start | bytes 1114112 | tf_op jit(solution)/shard_map/reduce_scatter | solution.py:47
  1418.9 956.8 %reduce-scatter.91.cloned.1.call-start = ((), (), s32[]{:S(2)}) async-start(), calls=%async_computation.81 | async-start | bytes 1114112 | tf_op jit(solution)/shard_map/reduce_scatter | solution.py:47
  1436.2 999.4 %reduce-scatter.81.cloned.1.call-start = ((), (), s32[]{:S(2)}) async-start(), calls=%async_computation.76 | async-start | bytes 1114112 | tf_op jit(solution)/shard_map/reduce_scatter | solution.py:44
  1436.8 1059.3 %reduce-scatter.83.cloned.1.call-start = ((), (), s32[]{:S(2)}) async-start(), calls=%async_computation.77 | async-start | bytes 1114112 | tf_op jit(solution)/shard_map/reduce_scatter | solution.py:44
  1437.5 1118.6 %reduce-scatter.73.cloned.1.call-start = ((), (), s32[]{:S(2)}) async-start(), calls=%async_computation.72 | async-start | bytes 1114112 | tf_op jit(solution)/shard_map/reduce_scatter | solution.py:41
  1438.3 1178.4 %reduce-scatter.75.cloned.1.call-start = ((), (), s32[]{:S(2)}) async-start(), calls=%async_computation.73 | async-start | bytes 1114112 | tf_op jit(solution)/shard_map/reduce_scatter | solution.py:41
  1439.0 1200.8 %reduce-scatter.63.cloned.1.call-start = ((), (), s32[]{:S(2)}) async-start(), calls=%async_computation.63 | async-start | bytes 1794048 | tf_op jit(solution)/shard_map/reduce_scatter | solution.py:23
  1444.7 1219.2 %reduce-scatter.71.cloned.1.call-start = ((), (), s32[]{:S(2)}) async-start(), calls=%async_computation.71 | async-start | bytes 1794048 | tf_op jit(solution)/shard_map/reduce_scatter | solution.py:23
  1450.3 1290.3 %reduce-scatter.115.cloned.1.call-start = ((), (), s32[]{:S(2)}) async-start(), calls=%async_computation.93 | async-start | bytes 4456448 | tf_op jit(solution)/shard_map/reduce_scatter | solution.py:56
  1458.0 1358.2 %reduce-scatter.113.cloned.1.call-start = ((), (), s32[]{:S(2)}) async-start(), calls=%async_computation.92 | async-start | bytes 4456448 | tf_op jit(solution)/shard_map/reduce_scatter | solution.py:56
  1466.1 1425.5 %reduce-scatter.105.cloned.1.call-start = ((), (), s32[]{:S(2)}) async-start(), calls=%async_computation.88 | async-start | bytes 4456448 | tf_op jit(solution)/shard_map/reduce_scatter | solution.py:53
  1474.2 1493.1 %reduce-scatter.107.cloned.1.call-start = ((), (), s32[]{:S(2)}) async-start(), calls=%async_computation.89 | async-start | bytes 4456448 | tf_op jit(solution)/shard_map/reduce_scatter | solution.py:53
  1841.1 1258.0 %all-reduce.11.cloned.1.call-start = ((), (), s32[]{:S(2)}) async-start(), calls=%async_computation.108 | async-start | bytes 196608 | tf_op jit(solution)/shard_map/psum | solution.py:383
  (283 other events, 19200.3 us)
Sparse Core Ops, SparseCore 0:
  1352.3 57.3 reduce-scatter.102
  1413.8 56.4 reduce-scatter.100
  1474.4 56.4 reduce-scatter.94
  1534.7 56.3 reduce-scatter.92
  1655.5 56.3 reduce-scatter.84
  1715.4 56.4 reduce-scatter.78
  1776.0 56.4 reduce-scatter.76
  1836.2 71.4 reduce-scatter.118
  1912.0 71.3 reduce-scatter.116
  1987.2 71.3 reduce-scatter.110
  2063.0 71.6 reduce-scatter.108
  2138.3 56.3 reduce-scatter.96
  2198.8 56.4 reduce-scatter.98
  2258.9 56.3 reduce-scatter.88
  2319.2 56.3 reduce-scatter.90
  2379.1 56.4 reduce-scatter.80
  2439.7 56.3 reduce-scatter.82
  2499.7 56.3 reduce-scatter.72
  2560.2 56.4 reduce-scatter.74
  2667.8 72.6 reduce-scatter.114
  2744.8 71.4 reduce-scatter.112
  2819.9 71.6 reduce-scatter.104
  2896.0 71.3 reduce-scatter.106
  2974.9 124.1 all-reduce.10
  (45 shorter events, 1265.3 us)
where the time goes:
time: 3130 us; the launch traced here: 3120 us
  waiting for transfers between devices  2430 us (78%)
  matrix products  390 us (12%)
  other arithmetic  123 us (4%)
  local copies, waits for them, and re-layouts  86.1 us (3%)
  blocking collectives  58 us (2%)
    reduce_scatter x4, waiting for transfers between devices, settle_grads(): lax.psum_scatter(up_piece.astype(jnp.bfloat16), 'wide', scatter_dimension...  298 us
    reduce_scatter x4, waiting for transfers between devices, settle_grads(): lax.psum_scatter(down_piece.astype(jnp.bfloat16), 'wide', scatter_dimensi...  280 us
    reduce_scatter x16, waiting for transfers between devices, feature_total(): lax.psum_scatter(partial_sums.astype(jnp.bfloat16), 'tensor', scatter_dim...  260 us
    reduce_scatter x4, waiting for transfers between devices, settle_grads(): lax.psum_scatter(query_piece.astype(jnp.bfloat16), 'wide', scatter_dimens...  239 us
    reduce_scatter x4, waiting for transfers between devices, settle_grads(): lax.psum_scatter(key_piece.astype(jnp.bfloat16), 'wide', scatter_dimensio...  238 us
    reduce_scatter x4, waiting for transfers between devices, settle_grads(): lax.psum_scatter(value_piece.astype(jnp.bfloat16), 'wide', scatter_dimens...  227 us
    all_gather x16, waiting for transfers between devices, full_rows(): return lax.all_gather(share_low, 'tensor', axis=1, tiled=True)  209 us
    psum x1, waiting for transfers between devices, body(): lax.psum((widened[0], widened[1], widened[2], widened[3], widened[4], wid...  130 us
  transfers between devices with their start and end apart: 69, of which 61 were waited for; matrix products, arithmetic and copies ran while one was open for 16% of the time, Pallas kernels for 0%

commit v1 on v0

--- a/solution.py
+++ b/solution.py
@@ -1,6 +1,8 @@
 import jax
 import jax.numpy as jnp
 from jax import lax
+from jax.experimental import pallas as pl
+from jax.experimental.pallas import tpu as pltpu
 from jax.sharding import PartitionSpec as P
 
 HEAD_DIM = 64
@@ -417,6 +419,422 @@
     )
 
 
+MESH_IDS = pl.DeviceIdType.MESH
+LOW = jnp.bfloat16
+BLOCK = 64
+
+
+def place():
+    wide = lax.axis_index("wide")
+    return (
+        lax.div(wide, 4),
+        lax.rem(lax.div(wide, 2), 2),
+        lax.rem(wide, 2),
+        lax.axis_index("tensor"),
+    )
+
+
+def neighbours():
+    z, x, c, y = place()
+
+    def at(z, x, c, y):
+        return (z * 4 + x * 2 + c, y)
+
+    return {
+        "core": at(z, x, 1 - c, y),
+        "x": at(z, 1 - x, c, y),
+        "y": at(z, x, c, 1 - y),
+        "z1": at(z + 1 - 2 * lax.rem(z, 2), x, c, y),
+        "z2": at(lax.rem(z + 2, 4), x, c, y),
+    }
+
+
+LINKS = ("core", "x", "y", "z1", "z2")
+
+
+def greet(partners):
+    barrier = pltpu.get_barrier_semaphore()
+    for link in LINKS:
+        pl.semaphore_signal(barrier, inc=1, device_id=partners[link], device_id_type=MESH_IDS)
+    pl.semaphore_wait(barrier, len(LINKS))
+
+
+def gather_stages(z, x, c, y, width):
+    share = width * 7 // 16
+    part_a, part_b, part_c = pl.ds(0, share), pl.ds(share, share), pl.ds(2 * share, width - 2 * share)
+    part_ab = pl.ds(0, 2 * share)
+    all_rows = pl.ds(0, BLOCK)
+    pair = pl.ds(lax.div(z, 2) * 2, 2)
+    every_z, every_x, every_t = pl.ds(0, 4), pl.ds(0, 2), pl.ds(0, 2)
+    far_x, far_y = 1 - x, 1 - y
+    return (
+        (
+            ("z1", (y, z, x, c, all_rows, part_ab)),
+            ("x", (y, z, x, c, all_rows, part_c)),
+        ),
+        (
+            ("z2", (y, pair, x, c, all_rows, part_ab)),
+            ("y", (y, z, every_x, c, all_rows, part_c)),
+        ),
+        (
+            ("x", (y, every_z, x, c, all_rows, part_a)),
+            ("y", (y, every_z, x, c, all_rows, part_b)),
+            ("z1", (every_t, z, every_x, c, all_rows, part_c)),
+            ("core", (y, every_z, x, c, all_rows, part_ab)),
+        ),
+        (
+            ("y", (y, every_z, every_x, c, all_rows, part_a)),
+            ("x", (every_t, every_z, x, c, all_rows, part_b)),
+            ("z2", (every_t, pair, every_x, c, all_rows, part_c)),
+            ("core", (y, every_z, far_x, c, all_rows, part_a)),
+            ("core", (far_y, every_z, x, c, all_rows, part_b)),
+        ),
+        (
+            ("core", (far_y, every_z, every_x, c, all_rows, part_a)),
+            ("core", (every_t, every_z, far_x, c, all_rows, part_b)),
+            ("core", (every_t, every_z, every_x, c, all_rows, part_c)),
+        ),
+    )
+
+
+def gather_kernel(count, shard_ref, *rest):
+    whole_refs = rest[:count]
+    send_sem, recv_sem, local_sem = rest[count:]
+    z, x, c, y = place()
+    partners = neighbours()
+    width = shard_ref.shape[2]
+    stages = gather_stages(z, x, c, y, width)
+    own = []
+    for chunk in range(count):
+        copy = pltpu.make_async_copy(
+            shard_ref.at[chunk], whole_refs[chunk].at[y, z, x, c], local_sem.at[chunk]
+        )
+        copy.start()
+        own.append(copy)
+    greet(partners)
+    flying = {}
+    for tick in range(count + len(stages)):
+        for stage_idx in range(len(stages), -1, -1):
+            chunk = tick - stage_idx
+            if chunk < 0 or chunk >= count:
+                continue
+            if stage_idx == 0:
+                own[chunk].wait()
+            for copy in flying.get((chunk, stage_idx - 1), ()):
+                copy.wait_recv()
+            if stage_idx == len(stages):
+                continue
+            started = []
+            base = sum(len(stage) for stage in stages[:stage_idx])
+            for entry, (link, index) in enumerate(stages[stage_idx]):
+                copy = pltpu.make_async_remote_copy(
+                    src_ref=whole_refs[chunk].at[index],
+                    dst_ref=whole_refs[chunk].at[index],
+                    send_sem=send_sem.at[chunk, base + entry],
+                    recv_sem=recv_sem.at[chunk, base + entry],
+                    device_id=partners[link],
+                    device_id_type=MESH_IDS,
+                )
+                copy.start()
+                started.append(copy)
+            flying[(chunk, stage_idx)] = started
+    for started in flying.values():
+        for copy in started:
+            copy.wait_send()
+
+
+def gather_weights(shards):
+    count, _, width = shards.shape
+    copies = 16
+    return pl.pallas_call(
+        lambda *refs: gather_kernel(count, *refs),
+        out_shape=[jax.ShapeDtypeStruct((2, 4, 2, 2, BLOCK, width), LOW)] * count,
+        in_specs=[pl.BlockSpec(memory_space=pl.ANY)],
+        out_specs=[pl.BlockSpec(memory_space=pl.ANY)] * count,
+        scratch_shapes=[
+            pltpu.SemaphoreType.DMA((count, copies)),
+            pltpu.SemaphoreType.DMA((count, copies)),
+            pltpu.SemaphoreType.DMA((count,)),
+        ],
+        compiler_params=pltpu.CompilerParams(collective_id=0, has_side_effects=True),
+        name="gather_weights",
+    )(shards)
+
+
+def swap_tensor(block):
+    return lax.ppermute(block, "tensor", [(0, 1), (1, 0)])
+
+
+def in_order(own, other, y, axis):
+    first = jnp.where(y == 0, own, other)
+    second = jnp.where(y == 0, other, own)
+    return jnp.concatenate((first, second), axis=axis)
+
+
+def whole_norm(stream, gain, shift):
+    row_mean = jnp.mean(stream, axis=1, keepdims=True)
+    square_mean = jnp.mean(stream * stream, axis=1, keepdims=True)
+    inverse_std = lax.rsqrt(square_mean - row_mean * row_mean + norm_eps)
+    centred = (stream - row_mean) * inverse_std
+    return (centred * gain + shift).astype(LOW), centred, inverse_std
+
+
+def whole_norm_backward(upstream, centred, inverse_std, gain):
+    scaled = upstream * gain
+    return inverse_std * (
+        scaled
+        - jnp.mean(scaled, axis=1, keepdims=True)
+        - centred * jnp.mean(scaled * centred, axis=1, keepdims=True)
+    )
+
+
+def dot_rows(left, right):
+    return lax.dot_general(
+        left, right, (((1,), (0,)), ((), ())), preferred_element_type=jnp.float32
+    )
+
+
+def dot_cols(left, right):
+    return lax.dot_general(
+        left, right, (((1,), (1,)), ((), ())), preferred_element_type=jnp.float32
+    )
+
+
+def dot_tokens(left, right):
+    return lax.dot_general(
+        left, right, (((0,), (0,)), ((), ())), preferred_element_type=jnp.float32
+    )
+
+
+def image_body(
+    images,
+    first_gain,
+    first_shift,
+    query_weight,
+    key_weight,
+    value_weight,
+    query_bias,
+    value_bias,
+    out_weight,
+    out_bias,
+    second_gain,
+    second_shift,
+    up_weight,
+    up_bias,
+    down_weight,
+    down_bias,
+    cotangent,
+):
+    layers = query_weight.shape[0]
+    half = images.shape[1]
+    hidden_half = up_weight.shape[2]
+    y = lax.axis_index("tensor")
+    far = 1 - y
+
+    out_turned = jnp.swapaxes(out_weight, 1, 2)
+    down_turned = jnp.swapaxes(down_weight, 1, 2)
+    mixed = jnp.concatenate((query_weight, key_weight, value_weight, out_turned), axis=2)
+    shards = jnp.stack(
+        [block[layer] for layer in range(layers) for block in (mixed, up_weight, down_turned)]
+    )
+    gathered = gather_weights(shards)
+    gathered = [part.reshape(2, -1, part.shape[-1]) for part in gathered]
+
+    tokens = jnp.stack((images.reshape(2, SEQ, half), cotangent.reshape(2, SEQ, half)))
+    tokens = jnp.swapaxes(tokens, 0, 1)
+    near_tokens = lax.dynamic_index_in_dim(tokens, y, 0, keepdims=False)
+    far_tokens = swap_tensor(lax.dynamic_index_in_dim(tokens, far, 0, keepdims=False))
+    tokens = in_order(near_tokens, far_tokens, y, 2)
+    biases = jnp.concatenate((query_bias, value_bias, out_bias, down_bias, up_bias), axis=1)
+    both = in_order(biases[None], swap_tensor(biases)[None], y, 0)
+
+    def whole_bias(start, size, layer):
+        return both[:, layer, start : start + size].reshape(1, -1).astype(jnp.float32)
+
+    def row(table, layer):
+        return table[layer][None].astype(jnp.float32)
+
+    stream = tokens[0].astype(jnp.float32)
+    saved = []
+    for layer in range(layers):
+        mixed_w, up_w, down_w = gathered[3 * layer : 3 * layer + 3]
+        normed, centred, inverse = whole_norm(
+            stream, row(first_gain, layer), row(first_shift, layer)
+        )
+        projected = [dot_rows(normed, mixed_w[t][:, : 3 * half]) for t in range(2)]
+        queries = jnp.concatenate([p[:, :half] for p in projected], axis=1)
+        keys_here = jnp.concatenate([p[:, half : 2 * half] for p in projected], axis=1)
+        values_here = jnp.concatenate([p[:, 2 * half :] for p in projected], axis=1)
+        queries = (queries + whole_bias(0, half, layer)).astype(LOW)
+        keys_here = keys_here.astype(LOW)
+        values_here = (values_here + whole_bias(half, half, layer)).astype(LOW)
+        heads, log_total = attention_forward(
+            queries, keys_here, values_here, 1, 2 * half // HEAD_DIM
+        )
+        attended = dot_cols(heads[:, :half], mixed_w[0][:, 3 * half :]) + dot_cols(
+            heads[:, half:], mixed_w[1][:, 3 * half :]
+        )
+        middle = stream + attended + whole_bias(2 * half, half, layer)
+        normed_two, centred_two, inverse_two = whole_norm(
+            middle, row(second_gain, layer), row(second_shift, layer)
+        )
+        before = [dot_rows(normed_two, up_w[t]) for t in range(2)]
+        before = [
+            before[t] + both[t, layer, 4 * half :][None].astype(jnp.float32) for t in range(2)
+        ]
+        hidden = [jax.nn.gelu(b, approximate=False).astype(LOW) for b in before]
+        fed = dot_cols(hidden[0], down_w[0]) + dot_cols(hidden[1], down_w[1])
+        saved.append(
+            (
+                normed,
+                centred,
+                inverse,
+                queries,
+                keys_here,
+                values_here,
+                heads,
+                log_total,
+                normed_two,
+                centred_two,
+                inverse_two,
+                before,
+                hidden,
+            )
+        )
+        stream = middle + fed + whole_bias(3 * half, half, layer)
+    activations = stream.astype(LOW)
+
+    upstream = tokens[1].astype(jnp.float32)
+    small = [None] * layers
+    owned = [None] * layers
+    for layer in reversed(range(layers)):
+        mixed_w, up_w, down_w = gathered[3 * layer : 3 * layer + 3]
+        (
+            normed,
+            centred,
+            inverse,
+            queries,
+            keys_here,
+            values_here,
+            heads,
+            log_total,
+            normed_two,
+            centred_two,
+            inverse_two,
+            before,
+            hidden,
+        ) = saved[layer]
+        down_bias_sum = jnp.sum(upstream, axis=0)
+        upstream_low = upstream.astype(LOW)
+        hidden_grad = [
+            (dot_rows(upstream_low, down_w[t]) * gelu_slope(before[t])).astype(LOW)
+            for t in range(2)
+        ]
+        up_bias_sum = [jnp.sum(g.astype(jnp.float32), axis=0) for g in hidden_grad]
+        down_term = [dot_tokens(upstream_low, hidden[t]).astype(LOW) for t in range(2)]
+        up_term = [dot_tokens(normed_two, hidden_grad[t]).astype(LOW) for t in range(2)]
+        normed_two_grad = dot_cols(hidden_grad[0], up_w[0]) + dot_cols(hidden_grad[1], up_w[1])
+        second_gain_sum = jnp.sum(normed_two_grad * centred_two, axis=0)
+        second_shift_sum = jnp.sum(normed_two_grad, axis=0)
+        upstream = upstream + whole_norm_backward(
+            normed_two_grad, centred_two, inverse_two, row(second_gain, layer)
+        )
+        out_bias_sum = jnp.sum(upstream, axis=0)
+        upstream_low = upstream.astype(LOW)
+        heads_grad = jnp.concatenate(
+            [dot_rows(upstream_low, mixed_w[t][:, 3 * half :]) for t in range(2)], axis=1
+        ).astype(LOW)
+        query_grad, key_grad, value_grad = attention_backward(
+            queries, keys_here, values_here, log_total, heads_grad, 1, 2 * half // HEAD_DIM
+        )
+        query_grad = query_grad.astype(LOW)
+        key_grad = key_grad.astype(LOW)
+        value_grad = value_grad.astype(LOW)
+        query_bias_sum = jnp.sum(query_grad.astype(jnp.float32), axis=0)
+        value_bias_sum = jnp.sum(value_grad.astype(jnp.float32), axis=0)
+        mixed_term = []
+        normed_grad = 0.0
+        for t in range(2):
+            cols = slice(t * half, (t + 1) * half)
+            joined = jnp.concatenate(
+                (query_grad[:, cols], key_grad[:, cols], value_grad[:, cols]), axis=1
+            )
+            mixed_term.append(
+                jnp.concatenate(
+                    (
+                        dot_tokens(normed, joined).astype(LOW),
+                        dot_tokens(upstream_low, heads[:, cols]).astype(LOW),
+                    ),
+                    axis=1,
+                )
+            )
+            normed_grad = normed_grad + dot_cols(joined, mixed_w[t][:, : 3 * half])
+        first_gain_sum = jnp.sum(normed_grad * centred, axis=0)
+        first_shift_sum = jnp.sum(normed_grad, axis=0)
+        upstream = upstream + whole_norm_backward(
+            normed_grad, centred, inverse, row(first_gain, layer)
+        )
+        small[layer] = jnp.concatenate(
+            (
+                query_bias_sum,
+                value_bias_sum,
+                out_bias_sum,
+                up_bias_sum[0],
+                up_bias_sum[1],
+                down_bias_sum,
+                first_gain_sum,
+                first_shift_sum,
+                second_gain_sum,
+                second_shift_sum,
+            )
+        )
+        owned[layer] = settle_whole((mixed_term, up_term, down_term))
+
+    totals = lax.psum(jnp.stack(small), ("wide", "tensor"))
+    width = 2 * half
+    small_outs, at = [], 0
+    for size in (width, width, width, 2 * hidden_half, width, width, width, width, width):
+        small_outs.append(totals[:, at : at + size])
+        at += size
+    mixed_own, up_own, down_own = [
+        jnp.stack([owned[layer][entry] for layer in range(layers)]) for entry in range(3)
+    ]
+
+    def to_owner(rows):
+        parts = rows.reshape(SEQ, 2, half)
+        near = lax.dynamic_index_in_dim(parts, y, 1, keepdims=False)
+        moved = swap_tensor(lax.dynamic_index_in_dim(parts, far, 1, keepdims=False).astype(LOW))
+        return in_order(near, moved.astype(near.dtype), y, 0)
+
+    return (
+        to_owner(activations),
+        to_owner(upstream),
+        mixed_own[:, :, :half],
+        mixed_own[:, :, half : 2 * half],
+        mixed_own[:, :, 2 * half : 3 * half],
+        jnp.swapaxes(mixed_own[:, :, 3 * half :], 1, 2),
+        up_own,
+        jnp.swapaxes(down_own, 1, 2),
+        *small_outs,
+    )
+
+
+def settle_whole(terms):
+    mixed_term, up_term, down_term = terms
+    whole = jnp.concatenate(
+        [
+            jnp.concatenate([term[t].reshape(16, 1, BLOCK, -1) for t in range(2)], axis=1)
+            for term in (mixed_term, up_term, down_term)
+        ],
+        axis=3,
+    )
+    width = whole.shape[-1] // 3
+    piece = lax.psum_scatter(
+        whole.reshape(-1, whole.shape[-1]), ("wide", "tensor"), scatter_dimension=0, tiled=True
+    ).astype(jnp.float32)
+    return piece[:, :width], piece[:, width : 2 * width], piece[:, 2 * width :]
+
+
 def solution(mesh):
     in_specs = (
         P("wide", "tensor"),
@@ -456,4 +874,9 @@
         P(),
         P(),
     )
-    return jax.shard_map(body, mesh=mesh, in_specs=in_specs, out_specs=out_specs, check_vma=False)
+    chosen = body
+    if mesh.shape["wide"] == 16 and mesh.shape["tensor"] == 2:
+        chosen = image_body
+    return jax.shard_map(
+        chosen, mesh=mesh, in_specs=in_specs, out_specs=out_specs, check_vma=False
+    )

time: 3130 us -> 1410 us (0.45)
  waiting for transfers between devices: 2430 us -> 462 us
  Pallas kernels: 0 us -> 235 us
  local copies, waits for them, and re-layouts: 86.1 us -> 180 us
  blocking collectives: 58 us -> 0 us
  matrix products: 390 us -> 351 us
  other arithmetic: 123 us -> 158 us
    reduce_scatter x40 -> x2, waiting for transfers between devices: 1660 us -> 450 us  [settle_whole(): lax.psum_scatter(whole.reshape(-1, whole.shape[-1]), ('wide', 'tensor'),...]
    all_gather x28 -> x0, waiting for transfers between devices: 626 us -> none  [the longest x16 209 us: full_rows(): return lax.all_gather(share_low, 'tensor', axis=1, tiled=True)]
    pallas_call x0 -> x1, Pallas kernels: none -> 235 us  [gather_weights(): pl.pallas_call(lambda *refs: gather_kernel(count, *refs), out_shape=[jax....]
    psum x1, waiting for transfers between devices: 130 us -> 0.01 us  [image_body(): totals = lax.psum(jnp.stack(small), ('wide', 'tensor'))]
    dot_general x48, matrix products: 283 us -> 212 us  [the longest x16 96 us: dot_rows(): lax.dot_general(left, right, (((1,), (0,)), ((), ())), preferred_element_...]
    concatenate x2 -> x17, other arithmetic: 4.09 us -> 70.6 us  [the longest x2 34.4 us: settle_whole(): jnp.concatenate([jnp.concatenate([term[t].reshape(16, 1, BLOCK, -1) for t...]
    concatenate x0 -> x13, local copies, waits for them, and re-layouts: none -> 62.6 us  [the longest x2 42.5 us: settle_whole(): jnp.concatenate([jnp.concatenate([term[t].reshape(16, 1, BLOCK, -1) for t...]
    psum x8 -> x0, blocking collectives: 58 us -> none  [row_totals(): return lax.psum((first_terms, second_terms), 'tensor')]
  transfers between devices with their start and end apart: 69 -> 7, of which waited for: 61 -> 4; matrix products, arithmetic and copies ran while one was open for 16% -> 15% of each run, Pallas kernels for 0% -> 17%
where the time goes in v1:
time: 1410 us
  waiting for transfers between devices  462 us (33%)
  matrix products  351 us (25%)
  Pallas kernels  235 us (17%)
  local copies, waits for them, and re-layouts  180 us (13%)
  other arithmetic  158 us (11%)
  between operations  16.3 us (1%)
    reduce_scatter x2, waiting for transfers between devices, settle_whole(): lax.psum_scatter(whole.reshape(-1, whole.shape[-1]), ('wide', 'tensor'),...  450 us
    pallas_call x1, Pallas kernels, gather_weights(): pl.pallas_call(lambda *refs: gather_kernel(count, *refs), out_shape=[jax....  235 us
    dot_general x16, matrix products, dot_rows(): lax.dot_general(left, right, (((1,), (0,)), ((), ())), preferred_element_...  96 us
    dot_general x16, matrix products, dot_tokens(): lax.dot_general(left, right, (((0,), (0,)), ((), ())), preferred_element_...  66.8 us
    dot_general x16, matrix products, dot_cols(): lax.dot_general(left, right, (((1,), (1,)), ((), ())), preferred_element_...  49.4 us
    concatenate x2, local copies, waits for them, and re-layouts, settle_whole(): jnp.concatenate([jnp.concatenate([term[t].reshape(16, 1, BLOCK, -1) for t...  42.5 us
    convert_element_type x2, other arithmetic, attention_backward(): score_grad = (weights_soft * (weight_grad - row_delta)).astype(jnp.bfloat16)  42.3 us
    concatenate x2, other arithmetic, settle_whole(): jnp.concatenate([jnp.concatenate([term[t].reshape(16, 1, BLOCK, -1) for t...  34.4 us
  transfers between devices with their start and end apart: 7, of which 4 were waited for; matrix products, arithmetic and copies ran while one was open for 15% of the time, Pallas kernels for 17%

profile of v1, /device:TPU:0, one launch (start us, length us, event | category | flops | bytes accessed | tf_op | source)
XLA Modules:
  0.0 1408.4 jit_solution(14344436446653331534)
XLA Ops:
  29.9 234.9 %gather_weights.1 = (bf16[2,4,2,2,64,2048]{5,4,3,2,1,0:T(8,128)(2,1)}, bf16[2,4,2,2,64,2048]{5,4,3,2,1,0:T(8,128)(2,1)}, bf16[2,4,2,2,64,2048]{5,4,3,2,1,0:T(8,1...) custom-call(bf16[6,64,2048]{2,1,0:T(8,128)(2,1)} %slice_dynamic-upda, ...), custom_call_target="tpu_custom_call" | custom-call | tf_op jit(solution)/shard_map/gather_weights/pallas_call | solution.py:549
  266.7 12.7 fusion.207
  279.4 13.0 fusion.205
  334.1 13.2 multiply_reduce_fusion.3
  347.3 10.6 fusion
  357.9 10.6 fusion.120
  374.4 14.4 %fusion.16 = (bf16[577,2048]{1,0:T(8,128)(2,1)S(1)}, f32[577,2048]{1,0:T(8,128)}) fusion(f32[2048]{0:T(1024)S(1)} %bitcast.366, bf16[577,1024]{1,0:T(8,128)(2,1)S(1)} %add_convert_fusion.7, bf16[1024,2048]{1,0:T(8,128)(2,1)S(1)} %bitcast.315), kind=kOutput, calls=%fused_computation.36 | convolution fusion | flops 2498105344 | bytes 12474368 | tf_op jit(solution)/shard_map/dot_general | solution.py:592
  391.8 14.3 %fusion.19 = (bf16[577,2048]{1,0:T(8,128)(2,1)S(1)}, f32[577,2048]{1,0:T(8,128)}) fusion(f32[2048]{0:T(1024)S(1)} %bitcast.364, bf16[577,1024]{1,0:T(8,128)(2,1)S(1)} %add_convert_fusion.7, bf16[1024,2048]{1,0:T(8,128)(2,1)S(1)} %bitcast.313), kind=kOutput, calls=%fused_computation.39 | convolution fusion | flops 2498105344 | bytes 12474368 | tf_op jit(solution)/shard_map/dot_general | solution.py:592
  435.2 13.2 multiply_reduce_fusion.2
  459.0 10.8 fusion.119
  474.1 14.5 %fusion.22 = (bf16[577,2048]{1,0:T(8,128)(2,1)}, f32[577,2048]{1,0:T(8,128)S(1)}) fusion(f32[2048]{0:T(1024)S(1)} %bitcast.370, bf16[577,1024]{1,0:T(8,128)(2,1)S(1)} %add_convert_fusion.5, bf16[1024,2048]{1,0:T(8,128)(2,1)S(1)} %bitcast.323), kind=kOutput, calls=%fused_computation.42 | convolution fusion | flops 2498105344 | bytes 12474368 | tf_op jit(solution)/shard_map/dot_general | solution.py:592
  496.9 14.2 %fusion.25 = (bf16[577,2048]{1,0:T(8,128)(2,1)}, f32[577,2048]{1,0:T(8,128)S(1)}) fusion(f32[2048]{0:T(1024)S(1)} %bitcast.368, bf16[577,1024]{1,0:T(8,128)(2,1)S(1)} %add_convert_fusion.5, bf16[1024,2048]{1,0:T(8,128)(2,1)S(1)} %bitcast.321), kind=kOutput, calls=%fused_computation.45 | convolution fusion | flops 2498105344 | bytes 12474368 | tf_op jit(solution)/shard_map/dot_general | solution.py:592
  536.6 16.4 %multiply_reduce_fusion.1 = (f32[16,577]{1,0:T(8,128)S(1)}, f32[16,577,577]{1,2,0:T(8,128)}) fusion(f32[16,577,577]{1,2,0:T(8,128)} %get-tuple-element.158, f32[16,577]{1,0:T(8,128)S(1)} %log_add_fusion.1, f32[577,8,64]{0,2,1:T(8,128)} %bitcast.293, f32[577,8,64]{0,2,1:T(8,128)} %bitcast.295, f32[16,64]{1,0:T(8,128)S(1)} %copy-done.126, ...), kind=kOutput, calls=%fused_computation.6 | convolution fusion | flops 705500160 | bytes 46237952 | tf_op jit(solution)/shard_map/iqhd,ikhd->ihqk/dot_general | solution.py:125
  553.0 21.1 %multiply_convert_fusion.1 = bf16[16,577,577]{1,2,0:T(8,128)(2,1)} fusion(f32[16,577,577]{1,2,0:T(8,128)} %get-tuple-element.166, f32[16,577,577]{1,2,0:T(8,128)} %get-tuple-element.158, f32[16,577]{1,0:T(8,128)S(1)} %get-tuple-element.165, f32[16,577]{1,0:T(8,128)S(1)} %log_add_fusion.1), kind=kLoop, calls=%fused_computation.5 | loop fusion | flops 26634320 | bytes 53342496 | tf_op jit(solution)/shard_map/convert_element_type | solution.py:129
  594.0 13.5 convert_reduce_fusion.6
  654.2 15.9 %multiply_reduce_fusion = (f32[16,577]{1,0:T(8,128)S(1)}, f32[16,577,577]{1,2,0:T(8,128)}) fusion(f32[16,577,577]{1,2,0:T(8,128)} %get-tuple-element.150, f32[16,577]{1,0:T(8,128)S(1)} %log_add_fusion, f32[577,8,64]{0,2,1:T(8,128)S(1)} %bitcast.294, f32[577,8,64]{0,2,1:T(8,128)S(1)} %bitcast.296, f32[16,64]{1,0:T(8,128)S(1)} %copy-done.125, ...), kind=kOutput, calls=%fused_computation.3 | convolution fusion | flops 705500160 | bytes 46237952 | tf_op jit(solution)/shard_map/iqhd,ikhd->ihqk/dot_general | solution.py:125
  670.1 21.1 %multiply_convert_fusion = bf16[16,577,577]{1,2,0:T(8,128)(2,1)} fusion(f32[16,577,577]{1,2,0:T(8,128)} %get-tuple-element.170, f32[16,577,577]{1,2,0:T(8,128)} %get-tuple-element.150, f32[16,577]{1,0:T(8,128)S(1)} %get-tuple-element.169, f32[16,577]{1,0:T(8,128)S(1)} %log_add_fusion), kind=kLoop, calls=%fused_computation.2 | loop fusion | flops 26634320 | bytes 53342496 | tf_op jit(solution)/shard_map/convert_element_type | solution.py:129
  734.6 13.5 convert_reduce_fusion.8
  781.2 17.3 %maximum_maximum_fusion.1 = bf16[16,2,64,6144]{3,2,0,1:T(8,128)(2,1)} fusion(bf16[16,1,64,2048]{3,2,0,1:T(8,128)(2,1)} %bitcast.303, bf16[16,1,64,2048]{3,2,0,1:T(8,128)(2,1)} %bitcast.304, bf16[16,1,64,2048]{3,2,0,1:T(8,128)(2,1)} %bitcast.301, bf16[16,1,64,2048]{3,2,0,1:T(8,128)(2,1)} %bitcast.302, bf16[16,1,64,2048]{3,2,0,1:T(8,128)(2,1)} %bitcast.263, ...), kind=kLoop, calls=%fused_computation.1 | loop fusion | flops 150994944 | bytes 50331648 | tf_op jit(solution)/shard_map/concatenate | solution.py:824
  798.6 21.3 %copy.172 = bf16[16,2,64,6144]{3,2,1,0:T(8,128)(2,1)} copy(bf16[16,2,64,6144]{3,2,0,1:T(8,128)(2,1)} %maximum_maximum_fusion.1) | data formatting | bytes 50331648 | tf_op jit(solution)/shard_map/concatenate | solution.py:824
  857.8 17.1 %maximum_maximum_fusion = bf16[16,2,64,6144]{3,2,0,1:T(8,128)(2,1)} fusion(bf16[16,1,64,2048]{3,2,0,1:T(8,128)(2,1)} %bitcast.305, bf16[16,1,64,2048]{3,2,0,1:T(8,128)(2,1)} %bitcast.306, bf16[16,1,64,2048]{3,2,0,1:T(8,128)(2,1)} %bitcast.307, bf16[16,1,64,2048]{3,2,0,1:T(8,128)(2,1)} %bitcast.308, bf16[16,1,64,2048]{3,2,0,1:T(8,128)(2,1)} %bitcast.261, ...), kind=kLoop, calls=%fused_computation | loop fusion | flops 150994944 | bytes 50331648 | tf_op jit(solution)/shard_map/concatenate | solution.py:824
  874.9 21.2 %copy.169 = bf16[16,2,64,6144]{3,2,1,0:T(8,128)(2,1)} copy(bf16[16,2,64,6144]{3,2,0,1:T(8,128)(2,1)} %maximum_maximum_fusion) | data formatting | bytes 50331648 | tf_op jit(solution)/shard_map/concatenate | solution.py:824
  945.4 199.2 %reduce-scatter.5.cloned.1.call-done = bf16[64,6144]{1,0:T(8,128)(2,1)} async-done(((bf16[2048,6144]{1,0:T(8,128)(2,1)}), bf16[64,6144]{1,0:T(8,128)(2,1)}) %reduce-scatter.5.cloned.1.call-update) | async-done | bytes 786448 | tf_op jit(solution)/shard_map/reduce_scatter | solution.py:832
  1145.9 251.2 %reduce-scatter.3.cloned.1.call-done = bf16[64,6144]{1,0:T(8,128)(2,1)} async-done(((bf16[2048,6144]{1,0:T(8,128)(2,1)}), bf16[64,6144]{1,0:T(8,128)(2,1)}) %reduce-scatter.3.cloned.1.call-update) | async-done | bytes 786448 | tf_op jit(solution)/shard_map/reduce_scatter | solution.py:832
  (570 shorter events, 386.8 us)
Async XLA Ops:
  7.2 918.1 %all-reduce.2.cloned.1.call-start = ((), (), s32[]{:S(2)}) async-start(), calls=%async_computation.4 | async-start | bytes 196608 | tf_op jit(solution)/shard_map/psum | solution.py:793
  10.7 291.7 %collective-permute-start.1 = (bf16[2,4096]{1,0:T(2,128)(2,1)S(1)}, bf16[2,4096]{1,0:T(2,128)(2,1)S(1)}, u32[]{:S(2)}, u32[]{:S(2)}) collective-permute-start(bf16[2,4096]{1,0:T(2,128)(2,1)S(1)} %constant_dynamic-update-slice_fusion.2), channel_id=1, source_target_pairs={{0,1},{1,0},{2,3},{3,2},{4,5},{5,4},{6,7},{7,6},{8,9},{9,8},{10,11... | collective-permute-start | bytes 49160 | tf_op jit(solution)/shard_map/ppermute | solution.py:565
  21.7 243.2 %copy-start.137 = (bf16[2,1024]{1,0:T(2,128)(2,1)S(1)}, bf16[2,1024]{1,0:T(2,128)(2,1)}, u32[]{:S(2)}) copy-start(bf16[2,1024]{1,0:T(2,128)(2,1)} %param.19) | copy-start | bytes 12292
  21.7 243.8 %copy-start.138 = (bf16[2,1024]{1,0:T(2,128)(2,1)S(1)}, bf16[2,1024]{1,0:T(2,128)(2,1)}, u32[]{:S(2)}) copy-start(bf16[2,1024]{1,0:T(2,128)(2,1)} %param.18) | copy-start | bytes 12292
  21.7 244.4 %copy-start.139 = (bf16[2,1024]{1,0:T(2,128)(2,1)S(1)}, bf16[2,1024]{1,0:T(2,128)(2,1)}, u32[]{:S(2)}) copy-start(bf16[2,1024]{1,0:T(2,128)(2,1)} %param.28) | copy-start | bytes 12292
  23.6 281.6 %collective-permute-start = (bf16[2,577,512]{2,0,1:T(2,128)(2,1)}, bf16[2,577,512]{2,0,1:T(2,128)(2,1)}, u32[]{:S(2)}, u32[]{:S(2)}) collective-permute-start(bf16[2,577,512]{2,0,1:T(2,128)(2,1)} %copy.137), channel_id=1, source_target_pairs={{0,1},{1,0},{2,3},{3,2},{4,5},{5,4},{6,7},{7,6},{8,9},{9,8},{10,11... | collective-permute-start | bytes 3545096 | tf_op jit(solution)/shard_map/ppermute | solution.py:565
  265.5 48.5 %copy-start.153 = (f32[1,1024]{1,0:T(1,128)}, f32[1,1024]{1,0:T(1,128)S(1)}, u32[]{:S(2)}) copy-start(f32[1,1024]{1,0:T(1,128)S(1)} %get-tuple-element.144) | copy-start | bytes 12292
  266.1 47.9 %copy-start.129 = (f32[1,1024]{1,0:T(1,128)}, f32[1,1024]{1,0:T(1,128)S(1)}, u32[]{:S(2)}) copy-start(f32[1,1024]{1,0:T(1,128)S(1)} %get-tuple-element.142) | copy-start | bytes 12292
  302.4 71.5 %copy-start.112 = (f32[1,1024]{1,0:T(1,128)}, f32[1,1024]{1,0:T(1,128)S(1)}, u32[]{:S(2)}) copy-start(f32[1,1024]{1,0:T(1,128)S(1)} %get-tuple-element.136) | copy-start | bytes 12292
  302.6 31.5 %copy-start.107 = (f32[16,64]{1,0:T(8,128)}, f32[16,64]{1,0:T(8,128)S(1)}, u32[]{:S(2)}) copy-start(f32[16,64]{1,0:T(8,128)S(1)} %reshape.611) | copy-start | bytes 12292
  302.7 55.2 %copy-start.124 = (f32[16,64]{1,0:T(8,128)}, f32[16,64]{1,0:T(8,128)S(1)}, u32[]{:S(2)}) copy-start(f32[16,64]{1,0:T(8,128)S(1)} %reshape.610) | copy-start | bytes 12292
  305.3 69.1 %copy-start.146 = (f32[1,1,2048]{2,1,0:T(1,128)}, f32[1,1,2048]{2,1,0:T(1,128)S(1)}, u32[]{:S(2)}) copy-start(f32[1,1,2048]{2,1,0:T(1,128)S(1)} %get-tuple-element.188) | copy-start | bytes 24580
  305.3 86.2 %copy-start.144 = (f32[1,1,2048]{2,1,0:T(1,128)}, f32[1,1,2048]{2,1,0:T(1,128)S(1)}, u32[]{:S(2)}) copy-start(f32[1,1,2048]{2,1,0:T(1,128)S(1)} %get-tuple-element.130) | copy-start | bytes 24580
  373.8 32.3 %copy-start.9 = (f32[577,1024]{1,0:T(8,128)}, f32[577,1024]{1,0:T(8,128)S(1)}, u32[]{:S(2)}) copy-start(f32[577,1024]{1,0:T(8,128)S(1)} %get-tuple-element.151) | copy-start | bytes 7090180
  473.2 47.0 %copy-start.4 = (f32[577,1024]{1,0:T(8,128)}, f32[577,1024]{1,0:T(8,128)S(1)}, u32[]{:S(2)}) copy-start(f32[577,1024]{1,0:T(8,128)S(1)} %get-tuple-element.159) | copy-start | bytes 7090180
  473.7 22.9 %copy-start.69 = (bf16[577,1024]{1,0:T(8,128)(2,1)}, bf16[577,1024]{1,0:T(8,128)(2,1)S(1)}, u32[]{:S(2)}) copy-start(bf16[577,1024]{1,0:T(8,128)(2,1)S(1)} %add_convert_fusion.5) | copy-start | bytes 3545092
  553.0 21.2 %copy-start.3 = (f32[577,1024]{0,1:T(8,128)S(1)}, f32[577,1024]{0,1:T(8,128)}, u32[]{:S(2)}) copy-start(f32[577,1024]{0,1:T(8,128)} %copy-done.2) | copy-start | bytes 7090180
  553.0 21.2 %copy-start.110 = (f32[16,64]{1,0:T(8,128)S(1)}, f32[16,64]{1,0:T(8,128)}, u32[]{:S(2)}) copy-start(f32[16,64]{1,0:T(8,128)} %reshape.621) | copy-start | bytes 12292
  670.1 21.1 %copy-start.1 = (f32[577,1024]{0,1:T(8,128)S(1)}, f32[577,1024]{0,1:T(8,128)}, u32[]{:S(2)}) copy-start(f32[577,1024]{0,1:T(8,128)} %copy-done) | copy-start | bytes 7090180
  670.1 21.1 %copy-start.108 = (f32[16,64]{1,0:T(8,128)S(1)}, f32[16,64]{1,0:T(8,128)}, u32[]{:S(2)}) copy-start(f32[16,64]{1,0:T(8,128)} %copy-done.107) | copy-start | bytes 12292
  773.8 370.8 %reduce-scatter.5.cloned.1.call-start = ((), (), s32[]{:S(2)}) async-start(), calls=%async_computation.3 | async-start | bytes 25952256 | tf_op jit(solution)/shard_map/reduce_scatter | solution.py:832
  819.9 577.3 %reduce-scatter.3.cloned.1.call-start = ((), (), s32[]{:S(2)}) async-start(), calls=%async_computation.2 | async-start | bytes 25952256 | tf_op jit(solution)/shard_map/reduce_scatter | solution.py:832
  913.4 16.6 %collective-permute-start.2 = (bf16[577,512]{1,0:T(8,128)(2,1)}, bf16[577,512]{1,0:T(8,128)(2,1)}, u32[]{:S(2)}, u32[]{:S(2)}) collective-permute-start(bf16[577,512]{1,0:T(8,128)(2,1)} %bitcast.254), channel_id=1, source_target_pairs={{0,1},{1,0},{2,3},{3,2},{4,5},{5,4},{6,7},{7,6},{8,9},{9,8},{10,11... | collective-permute-start | bytes 1772552 | tf_op jit(solution)/shard_map/ppermute | solution.py:565
  921.8 20.4 %collective-permute-start.3 = (bf16[577,512]{1,0:T(8,128)(2,1)}, bf16[577,512]{1,0:T(8,128)(2,1)}, u32[]{:S(2)}, u32[]{:S(2)}) collective-permute-start(bf16[577,512]{1,0:T(8,128)(2,1)} %bitcast.253), channel_id=1, source_target_pairs={{0,1},{1,0},{2,3},{3,2},{4,5},{5,4},{6,7},{7,6},{8,9},{9,8},{10,11... | collective-permute-start | bytes 1772552 | tf_op jit(solution)/shard_map/ppermute | solution.py:565
  (161 other events, 893.6 us)
Sparse Core Ops, SparseCore 0:
  773.9 117.9 all-reduce.1
  898.3 246.2 reduce-scatter.4
  1152.1 245.0 reduce-scatter.2

commit v2 on v1

--- a/solution.py
+++ b/solution.py
@@ -459,62 +459,94 @@
     pl.semaphore_wait(barrier, len(LINKS))
 
 
+def gather_parts(width):
+    last = 256 if width >= 1024 else 0
+    share = (width - last) // 2
+    return ((0, share), (share, share), (2 * share, last))
+
+
 def gather_stages(z, x, c, y, width):
-    share = width * 7 // 16
-    part_a, part_b, part_c = pl.ds(0, share), pl.ds(share, share), pl.ds(2 * share, width - 2 * share)
-    part_ab = pl.ds(0, 2 * share)
+    (_, share), _, (last_at, last) = gather_parts(width)
+
+    def cols(t, start, size):
+        return pl.ds(pl.multiple_of(t * width + start, 128), size)
+
     all_rows = pl.ds(0, BLOCK)
     pair = pl.ds(lax.div(z, 2) * 2, 2)
-    every_z, every_x, every_t = pl.ds(0, 4), pl.ds(0, 2), pl.ds(0, 2)
+    every_z, every_x = pl.ds(0, 4), pl.ds(0, 2)
     far_x, far_y = 1 - x, 1 - y
-    return (
-        (
-            ("z1", (y, z, x, c, all_rows, part_ab)),
-            ("x", (y, z, x, c, all_rows, part_c)),
-        ),
-        (
-            ("z2", (y, pair, x, c, all_rows, part_ab)),
-            ("y", (y, z, every_x, c, all_rows, part_c)),
-        ),
-        (
-            ("x", (y, every_z, x, c, all_rows, part_a)),
-            ("y", (y, every_z, x, c, all_rows, part_b)),
-            ("z1", (every_t, z, every_x, c, all_rows, part_c)),
-            ("core", (y, every_z, x, c, all_rows, part_ab)),
-        ),
-        (
-            ("y", (y, every_z, every_x, c, all_rows, part_a)),
-            ("x", (every_t, every_z, x, c, all_rows, part_b)),
-            ("z2", (every_t, pair, every_x, c, all_rows, part_c)),
-            ("core", (y, every_z, far_x, c, all_rows, part_a)),
-            ("core", (far_y, every_z, x, c, all_rows, part_b)),
-        ),
-        (
-            ("core", (far_y, every_z, every_x, c, all_rows, part_a)),
-            ("core", (every_t, every_z, far_x, c, all_rows, part_b)),
-            ("core", (every_t, every_z, every_x, c, all_rows, part_c)),
-        ),
-    )
-
-
-def gather_kernel(count, shard_ref, *rest):
-    whole_refs = rest[:count]
-    send_sem, recv_sem, local_sem = rest[count:]
+
+    def part_a(t):
+        return cols(t, 0, share)
+
+    def part_b(t):
+        return cols(t, share, share)
+
+    def part_ab(t):
+        return cols(t, 0, 2 * share)
+
+    def part_c(t):
+        return cols(t, last_at, last)
+
+    stages = [
+        [("z1", (z, x, c, all_rows, part_ab(y)))],
+        [("z2", (pair, x, c, all_rows, part_ab(y)))],
+        [
+            ("x", (every_z, x, c, all_rows, part_a(y))),
+            ("y", (every_z, x, c, all_rows, part_b(y))),
+            ("core", (every_z, x, c, all_rows, part_ab(y))),
+        ],
+        [
+            ("y", (every_z, every_x, c, all_rows, part_a(y))),
+            ("x", (every_z, x, c, all_rows, part_b(0))),
+            ("x", (every_z, x, c, all_rows, part_b(1))),
+            ("core", (every_z, far_x, c, all_rows, part_a(y))),
+            ("core", (every_z, x, c, all_rows, part_b(far_y))),
+        ],
+        [
+            ("core", (every_z, every_x, c, all_rows, part_a(far_y))),
+            ("core", (every_z, far_x, c, all_rows, part_b(0))),
+            ("core", (every_z, far_x, c, all_rows, part_b(1))),
+        ],
+    ]
+    if last:
+        stages[0].append(("x", (z, x, c, all_rows, part_c(y))))
+        stages[1].append(("y", (z, every_x, c, all_rows, part_c(y))))
+        for t in range(2):
+            stages[2].append(("z1", (z, every_x, c, all_rows, part_c(t))))
+            stages[3].append(("z2", (pair, every_x, c, all_rows, part_c(t))))
+            stages[4].append(("core", (every_z, every_x, c, all_rows, part_c(t))))
+    return stages
+
+
+GATHER_COPIES = 21
+
+
+def gather_kernel(layers, kinds, *refs):
+    shard_refs = refs[:kinds]
+    count = layers * kinds
+    whole_refs = refs[kinds : kinds + count]
+    send_sem, recv_sem, local_sem = refs[kinds + count :]
     z, x, c, y = place()
     partners = neighbours()
-    width = shard_ref.shape[2]
-    stages = gather_stages(z, x, c, y, width)
-    own = []
+    own, plans = [], []
     for chunk in range(count):
+        layer, kind = divmod(chunk, kinds)
+        width = shard_refs[kind].shape[2]
+        plans.append(gather_stages(z, x, c, y, width))
+        mine = pl.ds(pl.multiple_of(y * width, 128), width)
         copy = pltpu.make_async_copy(
-            shard_ref.at[chunk], whole_refs[chunk].at[y, z, x, c], local_sem.at[chunk]
+            shard_refs[kind].at[layer],
+            whole_refs[chunk].at[z, x, c, pl.ds(0, BLOCK), mine],
+            local_sem.at[chunk],
         )
         copy.start()
         own.append(copy)
     greet(partners)
+    depth = len(plans[0])
     flying = {}
-    for tick in range(count + len(stages)):
-        for stage_idx in range(len(stages), -1, -1):
+    for tick in range(count + depth):
+        for stage_idx in range(depth, -1, -1):
             chunk = tick - stage_idx
             if chunk < 0 or chunk >= count:
                 continue
@@ -522,11 +554,11 @@
                 own[chunk].wait()
             for copy in flying.get((chunk, stage_idx - 1), ()):
                 copy.wait_recv()
-            if stage_idx == len(stages):
+            if stage_idx == depth:
                 continue
             started = []
-            base = sum(len(stage) for stage in stages[:stage_idx])
-            for entry, (link, index) in enumerate(stages[stage_idx]):
+            base = sum(len(stage) for stage in plans[chunk][:stage_idx])
+            for entry, (link, index) in enumerate(plans[chunk][stage_idx]):
                 copy = pltpu.make_async_remote_copy(
                     src_ref=whole_refs[chunk].at[index],
                     dst_ref=whole_refs[chunk].at[index],
@@ -544,30 +576,216 @@
 
 
 def gather_weights(shards):
-    count, _, width = shards.shape
-    copies = 16
-    return pl.pallas_call(
-        lambda *refs: gather_kernel(count, *refs),
-        out_shape=[jax.ShapeDtypeStruct((2, 4, 2, 2, BLOCK, width), LOW)] * count,
-        in_specs=[pl.BlockSpec(memory_space=pl.ANY)],
+    layers, kinds = shards[0].shape[0], len(shards)
+    count = layers * kinds
+    whole = pl.pallas_call(
+        lambda *refs: gather_kernel(layers, kinds, *refs),
+        out_shape=[
+            jax.ShapeDtypeStruct((4, 2, 2, BLOCK, 2 * shards[chunk % kinds].shape[2]), LOW)
+            for chunk in range(count)
+        ],
+        in_specs=[pl.BlockSpec(memory_space=pl.ANY)] * kinds,
         out_specs=[pl.BlockSpec(memory_space=pl.ANY)] * count,
         scratch_shapes=[
-            pltpu.SemaphoreType.DMA((count, copies)),
-            pltpu.SemaphoreType.DMA((count, copies)),
+            pltpu.SemaphoreType.DMA((count, GATHER_COPIES)),
+            pltpu.SemaphoreType.DMA((count, GATHER_COPIES)),
             pltpu.SemaphoreType.DMA((count,)),
         ],
         compiler_params=pltpu.CompilerParams(collective_id=0, has_side_effects=True),
+        cost_estimate=pl.CostEstimate(
+            flops=0, bytes_accessed=600 * 1024 * 1024, transcendentals=0
+        ),
         name="gather_weights",
-    )(shards)
-
-
-def swap_tensor(block):
-    return lax.ppermute(block, "tensor", [(0, 1), (1, 0)])
-
-
-def in_order(own, other, y, axis):
-    first = jnp.where(y == 0, own, other)
-    second = jnp.where(y == 0, other, own)
+    )(*shards)
+    return [
+        [whole[layer * kinds + kind].reshape(1024, -1) for kind in range(kinds)]
+        for layer in range(layers)
+    ]
+
+
+def dot_rows(left, right):
+    return lax.dot_general(
+        left, right, (((1,), (0,)), ((), ())), preferred_element_type=jnp.float32
+    )
+
+
+def dot_cols(left, right):
+    return lax.dot_general(
+        left, right, (((1,), (1,)), ((), ())), preferred_element_type=jnp.float32
+    )
+
+
+def dot_tokens(left, right):
+    return lax.dot_general(
+        left, right, (((0,), (0,)), ((), ())), preferred_element_type=jnp.float32
+    )
+
+
+PAIR = 2 * HEAD_DIM
+
+
+def turned_softmax(keys_here, queries):
+    scores = dot_cols(keys_here, queries)
+    exponent = jnp.exp(scores - jnp.max(scores, axis=0, keepdims=True))
+    return exponent * (1.0 / jnp.sum(exponent, axis=0, keepdims=True))
+
+
+def heads_kernel(query_a, key_a, value_a, query_b, key_b, value_b, mixed_ref):
+    step = pl.program_id(0)
+    scale = jnp.asarray(HEAD_DIM**-0.5, LOW)
+    half_width = mixed_ref.shape[1] // 2
+    for t, (query_ref, key_ref, value_ref) in enumerate(
+        ((query_a, key_a, value_a), (query_b, key_b, value_b))
+    ):
+        pieces = []
+        for head in range(2):
+            cols = slice(head * HEAD_DIM, (head + 1) * HEAD_DIM)
+            soft = turned_softmax(key_ref[:, cols], query_ref[:, cols] * scale)
+            pieces.append(dot_tokens(soft.astype(LOW), value_ref[:, cols]).astype(LOW))
+        at = pl.multiple_of(t * half_width + step * PAIR, PAIR)
+        mixed_ref[:, pl.ds(at, PAIR)] = jnp.concatenate(pieces, axis=1)
+
+
+def projected_specs(blocks):
+    def spec(offset):
+        return pl.BlockSpec((SEQ, PAIR), lambda step: (0, offset + step))
+
+    return [spec(t * 3 * blocks + part * blocks) for t in range(2) for part in range(3)]
+
+
+def mix_heads(projected):
+    width = projected.shape[1] // 3
+    blocks = width // 2 // PAIR
+    return pl.pallas_call(
+        heads_kernel,
+        grid=(blocks,),
+        in_specs=projected_specs(blocks),
+        out_specs=pl.BlockSpec((SEQ, width), lambda step: (0, 0)),
+        out_shape=jax.ShapeDtypeStruct((SEQ, width), LOW),
+        compiler_params=pltpu.CompilerParams(vmem_limit_bytes=40 * 1024 * 1024),
+        cost_estimate=pl.CostEstimate(
+            flops=4 * SEQ * SEQ * width, bytes_accessed=45 * 1024 * 1024, transcendentals=0
+        ),
+        name="mix_heads",
+    )(*[projected] * 6)
+
+
+def heads_backward_kernel(
+    query_a, key_a, value_a, query_b, key_b, value_b, grad_a, grad_b, out_ref
+):
+    step = pl.program_id(0)
+    scale = jnp.asarray(HEAD_DIM**-0.5, LOW)
+    part_width = out_ref.shape[1] // 6
+    for t, (query_ref, key_ref, value_ref, grad_ref) in enumerate(
+        ((query_a, key_a, value_a, grad_a), (query_b, key_b, value_b, grad_b))
+    ):
+        pieces = ([], [], [])
+        for head in range(2):
+            cols = slice(head * HEAD_DIM, (head + 1) * HEAD_DIM)
+            keys_here, values_here = key_ref[:, cols], value_ref[:, cols]
+            grads = grad_ref[:, cols]
+            queries = query_ref[:, cols] * scale
+            soft = turned_softmax(keys_here, queries)
+            soft_grad = dot_cols(values_here, grads)
+            delta = jnp.sum(soft_grad * soft, axis=0, keepdims=True)
+            score_grad = (soft * (soft_grad - delta)).astype(LOW)
+            pieces[0].append((dot_tokens(score_grad, keys_here) * HEAD_DIM**-0.5).astype(LOW))
+            pieces[1].append(dot_rows(score_grad, queries).astype(LOW))
+            pieces[2].append(dot_rows(soft.astype(LOW), grads).astype(LOW))
+        for part in range(3):
+            at = pl.multiple_of((t * 3 + part) * part_width + step * PAIR, PAIR)
+            out_ref[:, pl.ds(at, PAIR)] = jnp.concatenate(pieces[part], axis=1)
+
+
+def mix_heads_backward(projected, mixed_grad):
+    width = mixed_grad.shape[1]
+    blocks = width // 2 // PAIR
+
+    def grad_spec(offset):
+        return pl.BlockSpec((SEQ, PAIR), lambda step: (0, offset + step))
+
+    return pl.pallas_call(
+        heads_backward_kernel,
+        grid=(blocks,),
+        in_specs=projected_specs(blocks) + [grad_spec(0), grad_spec(blocks)],
+        out_specs=pl.BlockSpec((SEQ, 3 * width), lambda step: (0, 0)),
+        out_shape=jax.ShapeDtypeStruct((SEQ, 3 * width), LOW),
+        compiler_params=pltpu.CompilerParams(vmem_limit_bytes=48 * 1024 * 1024),
+        cost_estimate=pl.CostEstimate(
+            flops=10 * SEQ * SEQ * width, bytes_accessed=90 * 1024 * 1024, transcendentals=0
+        ),
+        name="mix_heads_backward",
+    )(*[projected] * 6, mixed_grad, mixed_grad)
+
+
+def swap_link(block, link):
+    if link == "y":
+        return lax.ppermute(block, "tensor", [(0, 1), (1, 0)])
+    flip = {"core": 1, "x": 2, "z1": 4, "z2": 8}[link]
+    return lax.ppermute(block, "wide", [(i, i ^ flip) for i in range(16)])
+
+
+def pick(block, at, axis):
+    return lax.dynamic_index_in_dim(block, at, axis, keepdims=False)
+
+
+def add_low(left, right):
+    return (left.astype(jnp.float32) + right.astype(jnp.float32)).astype(LOW)
+
+
+def settle(left, right, first_link):
+    z, x, c, y = place()
+    right = right.reshape(SEQ, 2, 2, -1)
+    cols = right.shape[-1]
+    if first_link == "y":
+
+        def product(far, core):
+            picked = pick(pick(right, 1 - y if far else y, 1), core, 1)
+            return dot_tokens(left, picked)
+
+    else:
+        left = left.reshape(SEQ, 4, 2, 128)
+
+        def product(far, core):
+            rows = pick(left, 1 - x if far else x, 2).reshape(SEQ, 512)
+            picked = pick(right, core, 2).reshape(SEQ, 2 * cols)
+            return dot_tokens(rows, picked)
+
+    outgoing = [product(far, 1 - c).astype(LOW) for far in (True, False)]
+    arrived = [swap_link(block, "core") for block in outgoing]
+    far_sum = (product(True, c) + arrived[0].astype(jnp.float32)).astype(LOW)
+    near_sum = (product(False, c) + arrived[1].astype(jnp.float32)).astype(LOW)
+    kept = add_low(near_sum, swap_link(far_sum, first_link))
+    if first_link == "y":
+        kept = kept.reshape(4, 2, 128, cols)
+        kept = add_low(pick(kept, x, 1), swap_link(pick(kept, 1 - x, 1), "x"))
+    else:
+        kept = kept.reshape(4, 128, 2, cols)
+        kept = add_low(pick(kept, y, 2), swap_link(pick(kept, 1 - y, 2), "y"))
+    return kept
+
+
+def settle_along_z(kept):
+    z, x, c, y = place()
+    cols = kept.shape[-1]
+    kept = kept.reshape(2, 2, 128, cols)
+    high, lower = lax.div(z, 2), lax.rem(z, 2)
+    kept = add_low(pick(kept, high, 0), swap_link(pick(kept, 1 - high, 0), "z2"))
+    kept = add_low(pick(kept, lower, 0), swap_link(pick(kept, 1 - lower, 0), "z1"))
+    kept = kept.reshape(2, BLOCK, cols)
+    near, other = pick(kept, c, 0), swap_link(pick(kept, 1 - c, 0), "core")
+    return in_order(near[None], other[None], c, 0)
+
+
+def all_total(block):
+    for link in ("core", "x", "y", "z1", "z2"):
+        block = block + swap_link(block, link)
+    return block
+
+
+def in_order(own, other, index, axis):
+    first = jnp.where(index == 0, own, other)
+    second = jnp.where(index == 0, other, own)
     return jnp.concatenate((first, second), axis=axis)
 
 
@@ -585,24 +803,6 @@
         scaled
         - jnp.mean(scaled, axis=1, keepdims=True)
         - centred * jnp.mean(scaled * centred, axis=1, keepdims=True)
-    )
-
-
-def dot_rows(left, right):
-    return lax.dot_general(
-        left, right, (((1,), (0,)), ((), ())), preferred_element_type=jnp.float32
-    )
-
-
-def dot_cols(left, right):
-    return lax.dot_general(
-        left, right, (((1,), (1,)), ((), ())), preferred_element_type=jnp.float32
-    )
-
-
-def dot_tokens(left, right):
-    return lax.dot_general(
-        left, right, (((0,), (0,)), ((), ())), preferred_element_type=jnp.float32
     )
 
 
@@ -627,26 +827,27 @@
 ):
     layers = query_weight.shape[0]
     half = images.shape[1]
-    hidden_half = up_weight.shape[2]
+    hidden_width = 2 * up_weight.shape[2]
     y = lax.axis_index("tensor")
     far = 1 - y
 
-    out_turned = jnp.swapaxes(out_weight, 1, 2)
-    down_turned = jnp.swapaxes(down_weight, 1, 2)
-    mixed = jnp.concatenate((query_weight, key_weight, value_weight, out_turned), axis=2)
-    shards = jnp.stack(
-        [block[layer] for layer in range(layers) for block in (mixed, up_weight, down_turned)]
-    )
-    gathered = gather_weights(shards)
-    gathered = [part.reshape(2, -1, part.shape[-1]) for part in gathered]
+    whole = gather_weights(
+        (
+            jnp.concatenate((query_weight, key_weight, value_weight), axis=2),
+            jnp.swapaxes(out_weight, 1, 2),
+            up_weight,
+            jnp.swapaxes(down_weight, 1, 2),
+        )
+    )
 
     tokens = jnp.stack((images.reshape(2, SEQ, half), cotangent.reshape(2, SEQ, half)))
-    tokens = jnp.swapaxes(tokens, 0, 1)
-    near_tokens = lax.dynamic_index_in_dim(tokens, y, 0, keepdims=False)
-    far_tokens = swap_tensor(lax.dynamic_index_in_dim(tokens, far, 0, keepdims=False))
+    near_tokens = pick(tokens, y, 1)
+    far_tokens = swap_link(pick(tokens, far, 1), "y")
     tokens = in_order(near_tokens, far_tokens, y, 2)
-    biases = jnp.concatenate((query_bias, value_bias, out_bias, down_bias, up_bias), axis=1)
-    both = in_order(biases[None], swap_tensor(biases)[None], y, 0)
+    biases = jnp.concatenate(
+        (query_bias, jnp.zeros_like(query_bias), value_bias, out_bias, down_bias, up_bias), axis=1
+    )
+    both = in_order(biases[None], swap_link(biases, "y")[None], y, 0)
 
     def whole_bias(start, size, layer):
         return both[:, layer, start : start + size].reshape(1, -1).astype(jnp.float32)
@@ -657,43 +858,25 @@
     stream = tokens[0].astype(jnp.float32)
     saved = []
     for layer in range(layers):
-        mixed_w, up_w, down_w = gathered[3 * layer : 3 * layer + 3]
+        project_w, out_w, up_w, down_w = whole[layer]
         normed, centred, inverse = whole_norm(
             stream, row(first_gain, layer), row(first_shift, layer)
         )
-        projected = [dot_rows(normed, mixed_w[t][:, : 3 * half]) for t in range(2)]
-        queries = jnp.concatenate([p[:, :half] for p in projected], axis=1)
-        keys_here = jnp.concatenate([p[:, half : 2 * half] for p in projected], axis=1)
-        values_here = jnp.concatenate([p[:, 2 * half :] for p in projected], axis=1)
-        queries = (queries + whole_bias(0, half, layer)).astype(LOW)
-        keys_here = keys_here.astype(LOW)
-        values_here = (values_here + whole_bias(half, half, layer)).astype(LOW)
-        heads, log_total = attention_forward(
-            queries, keys_here, values_here, 1, 2 * half // HEAD_DIM
-        )
-        attended = dot_cols(heads[:, :half], mixed_w[0][:, 3 * half :]) + dot_cols(
-            heads[:, half:], mixed_w[1][:, 3 * half :]
-        )
-        middle = stream + attended + whole_bias(2 * half, half, layer)
+        projected = (dot_rows(normed, project_w) + whole_bias(0, 3 * half, layer)).astype(LOW)
+        heads = mix_heads(projected)
+        middle = stream + dot_cols(heads, out_w) + whole_bias(3 * half, half, layer)
         normed_two, centred_two, inverse_two = whole_norm(
             middle, row(second_gain, layer), row(second_shift, layer)
         )
-        before = [dot_rows(normed_two, up_w[t]) for t in range(2)]
-        before = [
-            before[t] + both[t, layer, 4 * half :][None].astype(jnp.float32) for t in range(2)
-        ]
-        hidden = [jax.nn.gelu(b, approximate=False).astype(LOW) for b in before]
-        fed = dot_cols(hidden[0], down_w[0]) + dot_cols(hidden[1], down_w[1])
+        before = dot_rows(normed_two, up_w) + whole_bias(5 * half, hidden_width // 2, layer)
+        hidden = (before * (0.5 * (1.0 + lax.erf(before * 0.7071067811865476)))).astype(LOW)
         saved.append(
             (
                 normed,
                 centred,
                 inverse,
-                queries,
-                keys_here,
-                values_here,
+                projected,
                 heads,
-                log_total,
                 normed_two,
                 centred_two,
                 inverse_two,
@@ -701,23 +884,20 @@
                 hidden,
             )
         )
-        stream = middle + fed + whole_bias(3 * half, half, layer)
+        stream = middle + dot_cols(hidden, down_w) + whole_bias(4 * half, half, layer)
     activations = stream.astype(LOW)
 
     upstream = tokens[1].astype(jnp.float32)
     small = [None] * layers
     owned = [None] * layers
     for layer in reversed(range(layers)):
-        mixed_w, up_w, down_w = gathered[3 * layer : 3 * layer + 3]
+        project_w, out_w, up_w, down_w = whole[layer]
         (
             normed,
             centred,
             inverse,
-            queries,
-            keys_here,
-            values_here,
+            projected,
             heads,
-            log_total,
             normed_two,
             centred_two,
             inverse_two,
@@ -726,14 +906,11 @@
         ) = saved[layer]
         down_bias_sum = jnp.sum(upstream, axis=0)
         upstream_low = upstream.astype(LOW)
-        hidden_grad = [
-            (dot_rows(upstream_low, down_w[t]) * gelu_slope(before[t])).astype(LOW)
-            for t in range(2)
-        ]
-        up_bias_sum = [jnp.sum(g.astype(jnp.float32), axis=0) for g in hidden_grad]
-        down_term = [dot_tokens(upstream_low, hidden[t]).astype(LOW) for t in range(2)]
-        up_term = [dot_tokens(normed_two, hidden_grad[t]).astype(LOW) for t in range(2)]
-        normed_two_grad = dot_cols(hidden_grad[0], up_w[0]) + dot_cols(hidden_grad[1], up_w[1])
+        down_term = settle(upstream_low, hidden, "x")
+        hidden_grad = (dot_rows(upstream_low, down_w) * gelu_slope(before)).astype(LOW)
+        up_bias_sum = jnp.sum(hidden_grad.astype(jnp.float32), axis=0)
+        up_term = settle(normed_two, hidden_grad, "y")
+        normed_two_grad = dot_cols(hidden_grad, up_w)
         second_gain_sum = jnp.sum(normed_two_grad * centred_two, axis=0)
         second_shift_sum = jnp.sum(normed_two_grad, axis=0)
         upstream = upstream + whole_norm_backward(
@@ -741,98 +918,72 @@
         )
         out_bias_sum = jnp.sum(upstream, axis=0)
         upstream_low = upstream.astype(LOW)
-        heads_grad = jnp.concatenate(
-            [dot_rows(upstream_low, mixed_w[t][:, 3 * half :]) for t in range(2)], axis=1
-        ).astype(LOW)
-        query_grad, key_grad, value_grad = attention_backward(
-            queries, keys_here, values_here, log_total, heads_grad, 1, 2 * half // HEAD_DIM
-        )
-        query_grad = query_grad.astype(LOW)
-        key_grad = key_grad.astype(LOW)
-        value_grad = value_grad.astype(LOW)
-        query_bias_sum = jnp.sum(query_grad.astype(jnp.float32), axis=0)
-        value_bias_sum = jnp.sum(value_grad.astype(jnp.float32), axis=0)
-        mixed_term = []
-        normed_grad = 0.0
-        for t in range(2):
-            cols = slice(t * half, (t + 1) * half)
-            joined = jnp.concatenate(
-                (query_grad[:, cols], key_grad[:, cols], value_grad[:, cols]), axis=1
-            )
-            mixed_term.append(
-                jnp.concatenate(
-                    (
-                        dot_tokens(normed, joined).astype(LOW),
-                        dot_tokens(upstream_low, heads[:, cols]).astype(LOW),
-                    ),
-                    axis=1,
-                )
-            )
-            normed_grad = normed_grad + dot_cols(joined, mixed_w[t][:, : 3 * half])
+        out_term = settle(upstream_low, heads, "x")
+        heads_grad = dot_rows(upstream_low, out_w).astype(LOW)
+        joined = mix_heads_backward(projected, heads_grad)
+        joined_sums = jnp.sum(joined.astype(jnp.float32), axis=0).reshape(2, 3, half)
+        project_term = settle(normed, joined, "y")
+        normed_grad = dot_cols(joined, project_w)
         first_gain_sum = jnp.sum(normed_grad * centred, axis=0)
         first_shift_sum = jnp.sum(normed_grad, axis=0)
         upstream = upstream + whole_norm_backward(
             normed_grad, centred, inverse, row(first_gain, layer)
         )
-        small[layer] = jnp.concatenate(
-            (
-                query_bias_sum,
-                value_bias_sum,
-                out_bias_sum,
-                up_bias_sum[0],
-                up_bias_sum[1],
-                down_bias_sum,
-                first_gain_sum,
-                first_shift_sum,
-                second_gain_sum,
-                second_shift_sum,
+        small[layer] = all_total(
+            jnp.concatenate(
+                (
+                    joined_sums[:, 0].reshape(-1),
+                    joined_sums[:, 2].reshape(-1),
+                    out_bias_sum,
+                    up_bias_sum,
+                    down_bias_sum,
+                    first_gain_sum,
+                    first_shift_sum,
+                    second_gain_sum,
+                    second_shift_sum,
+                )
             )
         )
-        owned[layer] = settle_whole((mixed_term, up_term, down_term))
-
-    totals = lax.psum(jnp.stack(small), ("wide", "tensor"))
+        feed_own = settle_along_z(jnp.concatenate((up_term, down_term), axis=2))
+        mixed_own = settle_along_z(jnp.concatenate((project_term, out_term), axis=2))
+        owned[layer] = (feed_own, mixed_own)
+
+    totals = jnp.stack(small)
     width = 2 * half
     small_outs, at = [], 0
-    for size in (width, width, width, 2 * hidden_half, width, width, width, width, width):
+    for size in (width, width, width, hidden_width, width, width, width, width, width):
         small_outs.append(totals[:, at : at + size])
         at += size
-    mixed_own, up_own, down_own = [
-        jnp.stack([owned[layer][entry] for layer in range(layers)]) for entry in range(3)
-    ]
+    feed_own = jnp.stack([owned[layer][0] for layer in range(layers)])
+    mixed_own = jnp.stack([owned[layer][1] for layer in range(layers)])
+
+    def weight_out(pieces, start, size):
+        block = jnp.swapaxes(pieces[..., start : start + size].astype(jnp.float32), 1, 2)
+        return block.reshape(layers, BLOCK, 2 * size)
+
+    quarter = hidden_width // 4
+    project_out = weight_out(mixed_own, 0, 3 * half // 2)
+    out_out = weight_out(mixed_own, 3 * half // 2, half // 2)
+    up_out = weight_out(feed_own, 0, quarter)
+    down_out = weight_out(feed_own, quarter, quarter)
 
     def to_owner(rows):
         parts = rows.reshape(SEQ, 2, half)
-        near = lax.dynamic_index_in_dim(parts, y, 1, keepdims=False)
-        moved = swap_tensor(lax.dynamic_index_in_dim(parts, far, 1, keepdims=False).astype(LOW))
+        near = pick(parts, y, 1)
+        moved = swap_link(pick(parts, far, 1).astype(LOW), "y")
         return in_order(near, moved.astype(near.dtype), y, 0)
 
     return (
         to_owner(activations),
         to_owner(upstream),
-        mixed_own[:, :, :half],
-        mixed_own[:, :, half : 2 * half],
-        mixed_own[:, :, 2 * half : 3 * half],
-        jnp.swapaxes(mixed_own[:, :, 3 * half :], 1, 2),
-        up_own,
-        jnp.swapaxes(down_own, 1, 2),
+        project_out[:, :, :half],
+        project_out[:, :, half : 2 * half],
+        project_out[:, :, 2 * half :],
+        jnp.swapaxes(out_out, 1, 2),
+        up_out,
+        jnp.swapaxes(down_out, 1, 2),
         *small_outs,
     )
-
-
-def settle_whole(terms):
-    mixed_term, up_term, down_term = terms
-    whole = jnp.concatenate(
-        [
-            jnp.concatenate([term[t].reshape(16, 1, BLOCK, -1) for t in range(2)], axis=1)
-            for term in (mixed_term, up_term, down_term)
-        ],
-        axis=3,
-    )
-    width = whole.shape[-1] // 3
-    piece = lax.psum_scatter(
-        whole.reshape(-1, whole.shape[-1]), ("wide", "tensor"), scatter_dimension=0, tiled=True
-    ).astype(jnp.float32)
-    return piece[:, :width], piece[:, width : 2 * width], piece[:, 2 * width :]
 
 
 def solution(mesh):

time: 1410 us -> 1260 us (0.89)
  waiting for transfers between devices: 462 us -> 273 us
  local copies, waits for them, and re-layouts: 180 us -> 348 us
  matrix products: 351 us -> 210 us
  other arithmetic: 158 us -> 53.4 us
  Pallas kernels: 235 us -> 321 us
  starting transfers between devices: 5.5 us -> 45.9 us
    reduce_scatter x2 -> x0, waiting for transfers between devices: 450 us -> none  [settle_whole(): lax.psum_scatter(whole.reshape(-1, whole.shape[-1]), ('wide', 'tensor'),...]
    ppermute x4 -> x58, waiting for transfers between devices: 11.6 us -> 273 us  [the longest x44 162 us: swap_link(): return lax.ppermute(block, 'wide', [(i, i ^ flip) for i in range(16)])]
    dynamic_slice x3 -> x16, local copies, waits for them, and re-layouts: 6.55 us -> 183 us  [pick(): return lax.dynamic_index_in_dim(block, at, axis, keepdims=False)]
    dot_general x12 -> x0, matrix products: 139 us -> none  [the longest x2 32.3 us: attention_backward(): jnp.einsum('iqhd,ikhd->ihqk', grad_four, value_four, preferred_element_ty...]
    reshape x0 -> x20, local copies, waits for them, and re-layouts: none -> 89.3 us  [the longest x8 67.7 us: settle(): right = right.reshape(SEQ, 2, 2, -1)]
    pallas_call x1 -> x5, Pallas kernels: 235 us -> 321 us  [the longest x1 237 us: gather_weights(): pl.pallas_call(lambda *refs: gather_kernel(layers, kinds, *refs), out_sha...]
    concatenate x15 -> x5, other arithmetic: 67.8 us -> 1.38 us  [the longest x1 0.77 us: image_body(): jnp.concatenate((query_weight, key_weight, value_weight), axis=2)]
    concatenate x13 -> x3, local copies, waits for them, and re-layouts: 62.6 us -> 2.57 us  [the longest x2 2.56 us: image_body(): jnp.concatenate((joined_sums[:, 0].reshape(-1), joined_sums[:, 2].reshape...]
  transfers between devices with their start and end apart: 7 -> 58, of which waited for: 4 -> 23; matrix products, arithmetic and copies ran while one was open for 15% -> 31% of each run, Pallas kernels for 17% -> 19%
where the time goes in v2:
time: 1260 us; the launch traced here: 1250 us
  local copies, waits for them, and re-layouts  348 us (28%)
  Pallas kernels  321 us (25%)
  waiting for transfers between devices  273 us (22%)
  matrix products  210 us (17%)
  other arithmetic  53.4 us (4%)
  starting transfers between devices  45.9 us (4%)
    pallas_call x1, Pallas kernels, gather_weights(): pl.pallas_call(lambda *refs: gather_kernel(layers, kinds, *refs), out_sha...  237 us
    dynamic_slice x16, local copies, waits for them, and re-layouts, pick(): return lax.dynamic_index_in_dim(block, at, axis, keepdims=False)  183 us
    ppermute x44, waiting for transfers between devices, swap_link(): return lax.ppermute(block, 'wide', [(i, i ^ flip) for i in range(16)])  162 us
    ppermute x14, waiting for transfers between devices, swap_link(): return lax.ppermute(block, 'tensor', [(0, 1), (1, 0)])  111 us
    dot_general x32, matrix products, dot_tokens(): lax.dot_general(left, right, (((0,), (0,)), ((), ())), preferred_element_...  93.7 us
    reshape x8, local copies, waits for them, and re-layouts, settle(): right = right.reshape(SEQ, 2, 2, -1)  67.7 us
    dot_general x8, matrix products, dot_cols(): lax.dot_general(left, right, (((1,), (1,)), ((), ())), preferred_element_...  58.4 us
    dot_general x8, matrix products, dot_rows(): lax.dot_general(left, right, (((1,), (0,)), ((), ())), preferred_element_...  57.5 us
  transfers between devices with their start and end apart: 58, of which 23 were waited for; matrix products, arithmetic and copies ran while one was open for 31% of the time, Pallas kernels for 19%

profile of v2, /device:TPU:0, one launch (start us, length us, event | category | flops | bytes accessed | tf_op | source)
XLA Modules:
  0.0 1254.2 jit_solution(13954585738574071128)
XLA Ops:
  14.8 236.9 %gather_weights.1 = (bf16[4,2,2,64,3072]{4,3,2,1,0:T(8,128)(2,1)}, bf16[4,2,2,64,1024]{4,3,2,1,0:T(8,128)(2,1)}, bf16[4,2,2,64,4096]{4,3,2,1,0:T(8,128)(2,1)}, b...) custom-call(bf16[2,64,1536]{2,1,0:T(8,128)(2,1)} %pad_maximum_fusion, ...), custom_call_target="tpu_custom_call" | custom-call | bytes 629145600 | tf_op jit(solution)/shard_map/gather_weights/pallas_call | solution.py:581
  261.3 13.6 %mix_heads.2 = bf16[577,1024]{1,0:T(8,128)(2,1)S(1)} custom-call(bf16[577,3072]{1,0:T(8,128)(2,1)S(1)} %add_convert_fusion.1.query_a.key_a.value_a.query_b.key_b.value_b, bf16[577,3072]{1,0:T(8,128)(2,1)S(1)} %add_convert_fusion.1.query_a.key_a.value_a.query_b.key_b.value_b, ...), custom_call_target="tpu_custom_call" | custom-call | flops 1363677184 | bytes 47185920 | tf_op jit(solution)/shard_map/mix_heads/pallas_call | solution.py:659
  302.2 13.6 %mix_heads.3 = bf16[577,1024]{1,0:T(8,128)(2,1)S(1)} custom-call(bf16[577,3072]{1,0:T(8,128)(2,1)S(1)} %add_convert_fusion.query_a.key_a.value_a.query_b.key_b.value_b, bf16[577,3072]{1,0:T(8,128)(2,1)S(1)} %add_convert_fusion.query_a.key_a.value_a.query_b.key_b.value_b, bf16[577,3072]{1,0:T(8,128)(2,1)S(1)} %add_convert_fusion.query_a.key_a.value_a.query_b.key_b.value_b, ...), custom_call_target="tpu_custom_call" | custom-call | flops 1363677184 | bytes 47185920 | tf_op jit(solution)/shard_map/mix_heads/pallas_call | solution.py:659
  318.1 12.0 multiply_convert_fusion
  330.0 12.8 %convert_reduce_fusion = (f32[4096]{0:T(1024)}, bf16[577,4096]{1,0:T(8,128)(2,1)S(1)}) fusion(f32[577,4096]{1,0:T(8,128)} %get-tuple-element.170, f32[4096]{0:T(1024)S(1)} %bitcast.548, bf16[1024,4096]{1,0:T(8,128)(2,1)} %bitcast.564, bf16[1,577,1024]{2,1,0:T(8,128)(2,1)S(1)} %get-tuple-element.76), kind=kOutput, calls=%fused_computation.14 | convolution fusion | flops 4870946816 | bytes 23783424 | tf_op jit(solution)/shard_map/dot_general | solution.py:607
  355.9 28.1 %mix_heads_backward.2 = bf16[577,3072]{1,0:T(8,128)(2,1)S(1)} custom-call(bf16[577,3072]{1,0:T(8,128)(2,1)} %copy-done.1, bf16[577,3072]{1,0:T(8,128)(2,1)} %copy-done.1, bf16[577,3072]{1,0:T(8,128)(2,1)} %copy-done.1, bf16[577,3072]{1,0:T(8,128)(2,1)} %copy-done.1, bf16[577,3072]{1,0:T(8,128)(2,1)} %copy-done.1, bf16[577,3072]{1,0:T(8,128)(2,1)} %copy-done.1, ...), custom_call_target="tpu_custom_call" | custom-call | flops 3409192960 | bytes 94371840 | tf_op jit(solution)/shard_map/mix_heads_backward/pallas_call | solution.py:707
  393.8 12.6 %convert_reduce_fusion.1 = (f32[4096]{0:T(1024)}, bf16[577,4096]{1,0:T(8,128)(2,1)S(1)}) fusion(f32[577,4096]{1,0:T(8,128)} %get-tuple-element.166, f32[4096]{0:T(1024)S(1)} %bitcast.546, bf16[577,1024]{1,0:T(8,128)(2,1)S(1)} %convert_element_type.635, bf16[1024,4096]{1,0:T(8,128)(2,1)} %bitcast.573), kind=kOutput, calls=%fused_computation.15 | convolution fusion | flops 4870946816 | bytes 23783424 | tf_op jit(solution)/shard_map/dot_general | solution.py:607
  422.3 28.3 %mix_heads_backward.3 = bf16[577,3072]{1,0:T(8,128)(2,1)S(1)} custom-call(bf16[577,3072]{1,0:T(8,128)(2,1)} %copy-done, bf16[577,3072]{1,0:T(8,128)(2,1)} %copy-done, bf16[577,3072]{1,0:T(8,128)(2,1)} %copy-done, bf16[577,3072]{1,0:T(8,128)(2,1)} %copy-done, bf16[577,3072]{1,0:T(8,128)(2,1)} %copy-done, bf16[577,3072]{1,0:T(8,128)(2,1)} %copy-done, ...), custom_call_target="tpu_custom_call" | custom-call | flops 3409192960 | bytes 94371840 | tf_op jit(solution)/shard_map/mix_heads_backward/pallas_call | solution.py:707
  463.1 11.9 reshape.671
  476.7 11.8 reshape.675
  490.0 11.8 reshape.682
  551.7 12.4 constant_dynamic-slice_fusion.10
  584.2 37.2 %dynamic-slice_reduce_fusion.2 = (bf16[577,2,1024]{2,1,0:T(2,128)(2,1)}, bf16[577,2,1024]{2,1,0:T(2,128)(2,1)}) fusion(bf16[577,2,2,1024]{3,2,1,0:T(2,128)(2,1)} %reshape.675, s32[]{:T(128)S(6)} %select_n.269, s32[]{:T(128)S(6)} %select_n.267), kind=kLoop, calls=%fused_computation.26 | loop fusion | bytes 9453576 | tf_op jit(solution)/shard_map/jit(dynamic_index_in_dim)/dynamic_slice | solution.py:729
  640.2 11.8 reshape.686
  652.0 37.4 %dynamic-slice_reduce_fusion = (bf16[577,2,1024]{2,1,0:T(2,128)(2,1)}, bf16[577,2,1024]{2,1,0:T(2,128)(2,1)}) fusion(bf16[577,2,2,1024]{3,2,1,0:T(2,128)(2,1)} %reshape.686, s32[]{:T(128)S(6)} %select_n.269, s32[]{:T(128)S(6)} %select_n.267), kind=kLoop, calls=%fused_computation.24 | loop fusion | bytes 9453576 | tf_op jit(solution)/shard_map/jit(dynamic_index_in_dim)/dynamic_slice | solution.py:729
  921.5 23.3 %collective-permute-done.17 = bf16[1024,768]{1,0:T(8,128)(2,1)S(1)} collective-permute-done((bf16[1024,768]{1,0:T(8,128)(2,1)S(1)}, bf16[1024,768]{1,0:T(8,128)(2,1)S(1)}, u32[]{:S(2)}, u32[]{:S(2)}) %collective-permute-start.17) | collective-permute-done | bytes 1572896 | tf_op jit(solution)/shard_map/ppermute | solution.py:723
  946.7 31.4 %collective-permute-done.6 = bf16[1024,768]{1,0:T(8,128)(2,1)S(1)} collective-permute-done((bf16[1024,768]{1,0:T(8,128)(2,1)S(1)}, bf16[1024,768]{1,0:T(8,128)(2,1)S(1)}, u32[]{:S(2)}, u32[]{:S(2)}) %collective-permute-start.6) | collective-permute-done | bytes 1572896 | tf_op jit(solution)/shard_map/ppermute | solution.py:723
  984.4 26.6 %collective-permute-done.18 = bf16[4,128,768]{2,1,0:T(8,128)(2,1)S(1)} collective-permute-done((bf16[4,128,768]{2,1,0:T(8,128)(2,1)S(1)}, bf16[4,128,768]{2,1,0:T(8,128)(2,1)S(1)}, u32[]{:S(2)}, u32[]{:S(2)}) %collective-permute-start.18) | collective-permute-done | bytes 786464 | tf_op jit(solution)/shard_map/ppermute | solution.py:725
  1015.7 11.7 collective-permute-done.7
  1039.0 20.9 %collective-permute-done.28 = bf16[1024,1024]{1,0:T(8,128)(2,1)} collective-permute-done((bf16[1024,1024]{1,0:T(8,128)(2,1)}, bf16[1024,1024]{1,0:T(8,128)(2,1)}, u32[]{:S(2)}, u32[]{:S(2)}) %collective-permute-start.28) | collective-permute-done | bytes 2097184 | tf_op jit(solution)/shard_map/ppermute | solution.py:723
  1136.1 11.8 collective-permute-done.44
  1153.6 52.0 %collective-permute-done.34 = bf16[2,128,2048]{2,1,0:T(8,128)(2,1)S(1)} collective-permute-done((bf16[2,128,2048]{2,1,0:T(8,128)(2,1)S(1)}, bf16[2,128,2048]{2,1,0:T(8,128)(2,1)S(1)}, u32[]{:S(2)}, u32[]{:S(2)}) %collective-permute-start.34) | collective-permute-done | bytes 1048608 | tf_op jit(solution)/shard_map/ppermute | solution.py:725
  1206.1 21.2 %collective-permute-done.45 = bf16[2,128,2048]{2,1,0:T(8,128)(2,1)S(1)} collective-permute-done((bf16[2,128,2048]{2,1,0:T(8,128)(2,1)S(1)}, bf16[2,128,2048]{2,1,0:T(8,128)(2,1)S(1)}, u32[]{:S(2)}, u32[]{:S(2)}) %collective-permute-start.45) | collective-permute-done | bytes 1048608 | tf_op jit(solution)/shard_map/ppermute | solution.py:725
  1238.8 10.9 collective-permute-done.46
  (634 shorter events, 548.7 us)
Async XLA Ops:
  10.6 241.8 %collective-permute-start = (bf16[2,577,512]{2,0,1:T(2,128)(2,1)}, bf16[2,577,512]{2,0,1:T(2,128)(2,1)}, u32[]{:S(2)}, u32[]{:S(2)}) collective-permute-start(bf16[2,577,512]{2,0,1:T(2,128)(2,1)} %copy.186), channel_id=1, source_target_pairs={{0,1},{1,0},{2,3},{3,2},{4,5},{5,4},{6,7},{7,6},{8,9},{9,8},{10,11... | collective-permute-start | bytes 3545096 | tf_op jit(solution)/shard_map/ppermute | solution.py:723
  13.7 238.0 %collective-permute-start.1 = (bf16[2,4608]{1,0:T(2,128)(2,1)S(1)}, bf16[2,4608]{1,0:T(2,128)(2,1)S(1)}, u32[]{:S(2)}, u32[]{:S(2)}) collective-permute-start(bf16[2,4608]{1,0:T(2,128)(2,1)S(1)} %constant_dynamic-update-slice_fusion.2), channel_id=1, source_target_pairs={{0,1},{1,0},{2,3},{3,2},{4,5},{5,4},{6,7},{7,6},{8,9},{9,8},{10,11... | collective-permute-start | bytes 55304 | tf_op jit(solution)/shard_map/ppermute | solution.py:723
  539.5 281.4 %collective-permute-start.48 = (f32[12288]{0:T(1024)}, f32[12288]{0:T(1024)}, u32[]{:S(2)}, u32[]{:S(2)}) collective-permute-start(f32[12288]{0:T(1024)} %constant_dynamic-update-slice_fusion.14), channel_id=1, source_target_pairs={{0,2},{2,0},{4,6},{6,4},{8,10},{10,8},{12,14},{14,12},{16,18},{18,... | collective-permute-start | bytes 147464 | tf_op jit(solution)/shard_map/ppermute | solution.py:725
  551.7 271.0 %collective-permute-start.53 = (f32[12288]{0:T(1024)}, f32[12288]{0:T(1024)}, u32[]{:S(2)}, u32[]{:S(2)}) collective-permute-start(f32[12288]{0:T(1024)} %constant_dynamic-update-slice_fusion.15), channel_id=1, source_target_pairs={{0,2},{2,0},{4,6},{6,4},{8,10},{10,8},{12,14},{14,12},{16,18},{18,... | collective-permute-start | bytes 147464 | tf_op jit(solution)/shard_map/ppermute | solution.py:725
  629.2 282.4 %collective-permute-start.31 = (bf16[512,2048]{1,0:T(8,128)(2,1)}, bf16[512,2048]{1,0:T(8,128)(2,1)}, u32[]{:S(2)}, u32[]{:S(2)}) collective-permute-start(bf16[512,2048]{1,0:T(8,128)(2,1)} %convolution_convert_fusion.2), channel_id=1, source_target_pairs={{0,2},{2,0},{4,6},{6,4},{8,10},{10,8},{12,14},{14,12},{16,18},{18,... | collective-permute-start | bytes 6291464 | tf_op jit(solution)/shard_map/ppermute | solution.py:725
  771.8 99.9 %collective-permute-start.8 = (bf16[512,512]{1,0:T(8,128)(2,1)}, bf16[512,512]{1,0:T(8,128)(2,1)}, u32[]{:S(2)}, u32[]{:S(2)}) collective-permute-start(bf16[512,512]{1,0:T(8,128)(2,1)} %convolution_convert_fusion.17), channel_id=1, source_target_pairs={{0,2},{2,0},{4,6},{6,4},{8,10},{10,8},{12,14},{14,12},{16,18},{18,... | collective-permute-start | bytes 1572872 | tf_op jit(solution)/shard_map/ppermute | solution.py:725
  775.7 80.8 %collective-permute-start.9 = (bf16[512,512]{1,0:T(8,128)(2,1)}, bf16[512,512]{1,0:T(8,128)(2,1)}, u32[]{:S(2)}, u32[]{:S(2)}) collective-permute-start(bf16[512,512]{1,0:T(8,128)(2,1)} %convolution_convert_fusion.16), channel_id=1, source_target_pairs={{0,2},{2,0},{4,6},{6,4},{8,10},{10,8},{12,14},{14,12},{16,18},{18,... | collective-permute-start | bytes 1572872 | tf_op jit(solution)/shard_map/ppermute | solution.py:725
  911.1 68.8 %collective-permute-start.27 = (bf16[1024,1024]{1,0:T(8,128)(2,1)S(1)}, bf16[1024,1024]{1,0:T(8,128)(2,1)S(1)}, u32[]{:S(2)}, u32[]{:S(2)}) collective-permute-start(bf16[1024,1024]{1,0:T(8,128)(2,1)S(1)} %copy-done.111), channel_id=1, source_target_pairs={{0,2},{2,0},{4,6},{6,4},{8,10},{10,8},{12,14},{14,12},{16,18},{18,... | collective-permute-start | bytes 6291464 | tf_op jit(solution)/shard_map/ppermute | solution.py:725
  911.6 66.5 %collective-permute-start.6 = (bf16[1024,768]{1,0:T(8,128)(2,1)S(1)}, bf16[1024,768]{1,0:T(8,128)(2,1)S(1)}, u32[]{:S(2)}, u32[]{:S(2)}) collective-permute-start(bf16[1024,768]{1,0:T(8,128)(2,1)S(1)} %add_convert_fusion.18), channel_id=1, source_target_pairs={{0,1},{1,0},{2,3},{3,2},{4,5},{5,4},{6,7},{7,6},{8,9},{9,8},{10,11... | collective-permute-start | bytes 4718600 | tf_op jit(solution)/shard_map/ppermute | solution.py:723
  912.8 71.6 %collective-permute-start.38 = (bf16[1024,1024]{1,0:T(8,128)(2,1)S(1)}, bf16[1024,1024]{1,0:T(8,128)(2,1)S(1)}, u32[]{:S(2)}, u32[]{:S(2)}) collective-permute-start(bf16[1024,1024]{1,0:T(8,128)(2,1)S(1)} %copy-done.113), channel_id=1, source_target_pairs={{0,2},{2,0},{4,6},{6,4},{8,10},{10,8},{12,14},{14,12},{16,18},{18,... | collective-permute-start | bytes 6291464 | tf_op jit(solution)/shard_map/ppermute | solution.py:725
  944.8 70.8 %collective-permute-start.30 = (bf16[512,2048]{1,0:T(8,128)(2,1)S(1)}, bf16[512,2048]{1,0:T(8,128)(2,1)S(1)}, u32[]{:S(2)}, u32[]{:S(2)}) collective-permute-start(bf16[512,2048]{1,0:T(8,128)(2,1)S(1)} %copy-done.112), channel_id=1, source_target_pairs={{0,2},{2,0},{4,6},{6,4},{8,10},{10,8},{12,14},{14,12},{16,18},{18,... | collective-permute-start | bytes 6291464 | tf_op jit(solution)/shard_map/ppermute | solution.py:725
  945.6 85.1 %collective-permute-start.32 = (bf16[512,2048]{1,0:T(8,128)(2,1)S(1)}, bf16[512,2048]{1,0:T(8,128)(2,1)S(1)}, u32[]{:S(2)}, u32[]{:S(2)}) collective-permute-start(bf16[512,2048]{1,0:T(8,128)(2,1)S(1)} %add_convert_fusion.9), channel_id=1, source_target_pairs={{0,4},{2,6},{4,0},{6,2},{8,12},{10,14},{12,8},{14,10},{16,20},{18,... | collective-permute-start | bytes 6291464 | tf_op jit(solution)/shard_map/ppermute | solution.py:725
  979.9 47.5 %collective-permute-start.7 = (bf16[4,128,768]{2,1,0:T(8,128)(2,1)S(1)}, bf16[4,128,768]{2,1,0:T(8,128)(2,1)S(1)}, u32[]{:S(2)}, u32[]{:S(2)}) collective-permute-start(bf16[4,128,768]{2,1,0:T(8,128)(2,1)S(1)} %dynamic-slice_bitcast_fusion.6), channel_id=1, source_target_pairs={{0,4},{2,6},{4,0},{6,2},{8,12},{10,14},{12,8},{14,10},{16,20},{18,... | collective-permute-start | bytes 2359304 | tf_op jit(solution)/shard_map/ppermute | solution.py:725
  984.4 53.5 %collective-permute-start.26 = (bf16[1024,1024]{1,0:T(8,128)(2,1)}, bf16[1024,1024]{1,0:T(8,128)(2,1)}, u32[]{:S(2)}, u32[]{:S(2)}) collective-permute-start(bf16[1024,1024]{1,0:T(8,128)(2,1)} %convolution_convert_fusion.7), channel_id=1, source_target_pairs={{0,2},{2,0},{4,6},{6,4},{8,10},{10,8},{12,14},{14,12},{16,18},{18,... | collective-permute-start | bytes 6291464 | tf_op jit(solution)/shard_map/ppermute | solution.py:725
  1011.0 48.9 %collective-permute-start.28 = (bf16[1024,1024]{1,0:T(8,128)(2,1)}, bf16[1024,1024]{1,0:T(8,128)(2,1)}, u32[]{:S(2)}, u32[]{:S(2)}) collective-permute-start(bf16[1024,1024]{1,0:T(8,128)(2,1)} %add_convert_fusion.12), channel_id=1, source_target_pairs={{0,1},{1,0},{2,3},{3,2},{4,5},{5,4},{6,7},{7,6},{8,9},{9,8},{10,11... | collective-permute-start | bytes 6291464 | tf_op jit(solution)/shard_map/ppermute | solution.py:723
  1015.6 53.9 %collective-permute-start.41 = (bf16[512,2048]{1,0:T(8,128)(2,1)}, bf16[512,2048]{1,0:T(8,128)(2,1)}, u32[]{:S(2)}, u32[]{:S(2)}) collective-permute-start(bf16[512,2048]{1,0:T(8,128)(2,1)} %convolution_convert_fusion.1), channel_id=1, source_target_pairs={{0,2},{2,0},{4,6},{6,4},{8,10},{10,8},{12,14},{14,12},{16,18},{18,... | collective-permute-start | bytes 6291464 | tf_op jit(solution)/shard_map/ppermute | solution.py:725
  1027.4 47.7 %collective-permute-start.43 = (bf16[512,2048]{1,0:T(8,128)(2,1)}, bf16[512,2048]{1,0:T(8,128)(2,1)}, u32[]{:S(2)}, u32[]{:S(2)}) collective-permute-start(bf16[512,2048]{1,0:T(8,128)(2,1)} %add_convert_fusion.3), channel_id=1, source_target_pairs={{0,4},{2,6},{4,0},{6,2},{8,12},{10,14},{12,8},{14,10},{16,20},{18,... | collective-permute-start | bytes 6291464 | tf_op jit(solution)/shard_map/ppermute | solution.py:725
  1030.7 65.3 %collective-permute-start.37 = (bf16[1024,1024]{1,0:T(8,128)(2,1)}, bf16[1024,1024]{1,0:T(8,128)(2,1)}, u32[]{:S(2)}, u32[]{:S(2)}) collective-permute-start(bf16[1024,1024]{1,0:T(8,128)(2,1)} %convolution_convert_fusion.5), channel_id=1, source_target_pairs={{0,2},{2,0},{4,6},{6,4},{8,10},{10,8},{12,14},{14,12},{16,18},{18,... | collective-permute-start | bytes 6291464 | tf_op jit(solution)/shard_map/ppermute | solution.py:725
  1037.8 67.0 %collective-permute-start.39 = (bf16[1024,1024]{1,0:T(8,128)(2,1)}, bf16[1024,1024]{1,0:T(8,128)(2,1)}, u32[]{:S(2)}, u32[]{:S(2)}) collective-permute-start(bf16[1024,1024]{1,0:T(8,128)(2,1)} %add_convert_fusion.6), channel_id=1, source_target_pairs={{0,1},{1,0},{2,3},{3,2},{4,5},{5,4},{6,7},{7,6},{8,9},{9,8},{10,11... | collective-permute-start | bytes 6291464 | tf_op jit(solution)/shard_map/ppermute | solution.py:723
  1059.8 50.1 %collective-permute-start.23 = (bf16[2,128,1024]{2,1,0:T(8,128)(2,1)}, bf16[2,128,1024]{2,1,0:T(8,128)(2,1)}, u32[]{:S(2)}, u32[]{:S(2)}) collective-permute-start(bf16[2,128,1024]{2,1,0:T(8,128)(2,1)} %dynamic-slice_bitcast_fusion.9), channel_id=1, source_target_pairs={{0,16},{2,18},{4,20},{6,22},{8,24},{10,26},{12,28},{14,30},{16,0},... | collective-permute-start | bytes 1572872 | tf_op jit(solution)/shard_map/ppermute | solution.py:725
  1069.5 42.8 %collective-permute-start.12 = (bf16[2,128,1024]{2,1,0:T(8,128)(2,1)}, bf16[2,128,1024]{2,1,0:T(8,128)(2,1)}, u32[]{:S(2)}, u32[]{:S(2)}) collective-permute-start(bf16[2,128,1024]{2,1,0:T(8,128)(2,1)} %dynamic-slice_bitcast_fusion.10), channel_id=1, source_target_pairs={{0,16},{2,18},{4,20},{6,22},{8,24},{10,26},{12,28},{14,30},{16,0},... | collective-permute-start | bytes 1572872 | tf_op jit(solution)/shard_map/ppermute | solution.py:725
  1075.1 55.8 %collective-permute-start.29 = (bf16[4,128,1024]{2,1,0:T(8,128)(2,1)}, bf16[4,128,1024]{2,1,0:T(8,128)(2,1)}, u32[]{:S(2)}, u32[]{:S(2)}) collective-permute-start(bf16[4,128,1024]{2,1,0:T(8,128)(2,1)} %dynamic-slice_bitcast_fusion.4), channel_id=1, source_target_pairs={{0,4},{2,6},{4,0},{6,2},{8,12},{10,14},{12,8},{14,10},{16,20},{18,... | collective-permute-start | bytes 3145736 | tf_op jit(solution)/shard_map/ppermute | solution.py:725
  1133.7 71.9 %collective-permute-start.34 = (bf16[2,128,2048]{2,1,0:T(8,128)(2,1)S(1)}, bf16[2,128,2048]{2,1,0:T(8,128)(2,1)S(1)}, u32[]{:S(2)}, u32[]{:S(2)}) collective-permute-start(bf16[2,128,2048]{2,1,0:T(8,128)(2,1)S(1)} %dynamic-slice_bitcast_fusion.3), channel_id=1, source_target_pairs={{0,16},{2,18},{4,20},{6,22},{8,24},{10,26},{12,28},{14,30},{16,0},... | collective-permute-start | bytes 3145736 | tf_op jit(solution)/shard_map/ppermute | solution.py:725
  1149.3 78.0 %collective-permute-start.45 = (bf16[2,128,2048]{2,1,0:T(8,128)(2,1)S(1)}, bf16[2,128,2048]{2,1,0:T(8,128)(2,1)S(1)}, u32[]{:S(2)}, u32[]{:S(2)}) collective-permute-start(bf16[2,128,2048]{2,1,0:T(8,128)(2,1)S(1)} %dynamic-slice_bitcast_fusion.1), channel_id=1, source_target_pairs={{0,16},{2,18},{4,20},{6,22},{8,24},{10,26},{12,28},{14,30},{16,0},... | collective-permute-start | bytes 3145736 | tf_op jit(solution)/shard_map/ppermute | solution.py:725
  (166 other events, 2462.7 us)

commit v3 on v2

--- a/solution.py
+++ b/solution.py
@@ -422,6 +422,8 @@
 MESH_IDS = pl.DeviceIdType.MESH
 LOW = jnp.bfloat16
 BLOCK = 64
+ROWS = -(-SEQ // 16) * 16
+DEEP = -(-SEQ // 128) * 128
 
 
 def place():
@@ -630,6 +632,12 @@
     return exponent * (1.0 / jnp.sum(exponent, axis=0, keepdims=True))
 
 
+def store_rows(ref, at, pieces):
+    full = SEQ // 16 * 16
+    ref[pl.ds(full, ROWS - full), pl.ds(at, PAIR)] = jnp.zeros((ROWS - full, PAIR), LOW)
+    ref[pl.ds(0, SEQ), pl.ds(at, PAIR)] = jnp.concatenate(pieces, axis=1)
+
+
 def heads_kernel(query_a, key_a, value_a, query_b, key_b, value_b, mixed_ref):
     step = pl.program_id(0)
     scale = jnp.asarray(HEAD_DIM**-0.5, LOW)
@@ -640,15 +648,15 @@
         pieces = []
         for head in range(2):
             cols = slice(head * HEAD_DIM, (head + 1) * HEAD_DIM)
-            soft = turned_softmax(key_ref[:, cols], query_ref[:, cols] * scale)
-            pieces.append(dot_tokens(soft.astype(LOW), value_ref[:, cols]).astype(LOW))
+            soft = turned_softmax(key_ref[:SEQ, cols], query_ref[:SEQ, cols] * scale)
+            pieces.append(dot_tokens(soft.astype(LOW), value_ref[:SEQ, cols]).astype(LOW))
         at = pl.multiple_of(t * half_width + step * PAIR, PAIR)
-        mixed_ref[:, pl.ds(at, PAIR)] = jnp.concatenate(pieces, axis=1)
+        store_rows(mixed_ref, at, pieces)
 
 
 def projected_specs(blocks):
     def spec(offset):
-        return pl.BlockSpec((SEQ, PAIR), lambda step: (0, offset + step))
+        return pl.BlockSpec((ROWS, PAIR), lambda step: (0, offset + step))
 
     return [spec(t * 3 * blocks + part * blocks) for t in range(2) for part in range(3)]
 
@@ -660,8 +668,8 @@
         heads_kernel,
         grid=(blocks,),
         in_specs=projected_specs(blocks),
-        out_specs=pl.BlockSpec((SEQ, width), lambda step: (0, 0)),
-        out_shape=jax.ShapeDtypeStruct((SEQ, width), LOW),
+        out_specs=pl.BlockSpec((ROWS, width), lambda step: (0, 0)),
+        out_shape=jax.ShapeDtypeStruct((ROWS, width), LOW),
         compiler_params=pltpu.CompilerParams(vmem_limit_bytes=40 * 1024 * 1024),
         cost_estimate=pl.CostEstimate(
             flops=4 * SEQ * SEQ * width, bytes_accessed=45 * 1024 * 1024, transcendentals=0
@@ -682,9 +690,9 @@
         pieces = ([], [], [])
         for head in range(2):
             cols = slice(head * HEAD_DIM, (head + 1) * HEAD_DIM)
-            keys_here, values_here = key_ref[:, cols], value_ref[:, cols]
-            grads = grad_ref[:, cols]
-            queries = query_ref[:, cols] * scale
+            keys_here, values_here = key_ref[:SEQ, cols], value_ref[:SEQ, cols]
+            grads = grad_ref[:SEQ, cols]
+            queries = query_ref[:SEQ, cols] * scale
             soft = turned_softmax(keys_here, queries)
             soft_grad = dot_cols(values_here, grads)
             delta = jnp.sum(soft_grad * soft, axis=0, keepdims=True)
@@ -694,7 +702,7 @@
             pieces[2].append(dot_rows(soft.astype(LOW), grads).astype(LOW))
         for part in range(3):
             at = pl.multiple_of((t * 3 + part) * part_width + step * PAIR, PAIR)
-            out_ref[:, pl.ds(at, PAIR)] = jnp.concatenate(pieces[part], axis=1)
+            store_rows(out_ref, at, pieces[part])
 
 
 def mix_heads_backward(projected, mixed_grad):
@@ -702,14 +710,14 @@
     blocks = width // 2 // PAIR
 
     def grad_spec(offset):
-        return pl.BlockSpec((SEQ, PAIR), lambda step: (0, offset + step))
+        return pl.BlockSpec((ROWS, PAIR), lambda step: (0, offset + step))
 
     return pl.pallas_call(
         heads_backward_kernel,
         grid=(blocks,),
         in_specs=projected_specs(blocks) + [grad_spec(0), grad_spec(blocks)],
-        out_specs=pl.BlockSpec((SEQ, 3 * width), lambda step: (0, 0)),
-        out_shape=jax.ShapeDtypeStruct((SEQ, 3 * width), LOW),
+        out_specs=pl.BlockSpec((ROWS, 3 * width), lambda step: (0, 0)),
+        out_shape=jax.ShapeDtypeStruct((ROWS, 3 * width), LOW),
         compiler_params=pltpu.CompilerParams(vmem_limit_bytes=48 * 1024 * 1024),
         cost_estimate=pl.CostEstimate(
             flops=10 * SEQ * SEQ * width, bytes_accessed=90 * 1024 * 1024, transcendentals=0
@@ -729,58 +737,270 @@
     return lax.dynamic_index_in_dim(block, at, axis, keepdims=False)
 
 
-def add_low(left, right):
-    return (left.astype(jnp.float32) + right.astype(jnp.float32)).astype(LOW)
-
-
-def settle(left, right, first_link):
-    z, x, c, y = place()
-    right = right.reshape(SEQ, 2, 2, -1)
-    cols = right.shape[-1]
-    if first_link == "y":
-
-        def product(far, core):
-            picked = pick(pick(right, 1 - y if far else y, 1), core, 1)
-            return dot_tokens(left, picked)
-
-    else:
-        left = left.reshape(SEQ, 4, 2, 128)
-
-        def product(far, core):
-            rows = pick(left, 1 - x if far else x, 2).reshape(SEQ, 512)
-            picked = pick(right, core, 2).reshape(SEQ, 2 * cols)
-            return dot_tokens(rows, picked)
-
-    outgoing = [product(far, 1 - c).astype(LOW) for far in (True, False)]
-    arrived = [swap_link(block, "core") for block in outgoing]
-    far_sum = (product(True, c) + arrived[0].astype(jnp.float32)).astype(LOW)
-    near_sum = (product(False, c) + arrived[1].astype(jnp.float32)).astype(LOW)
-    kept = add_low(near_sum, swap_link(far_sum, first_link))
-    if first_link == "y":
-        kept = kept.reshape(4, 2, 128, cols)
-        kept = add_low(pick(kept, x, 1), swap_link(pick(kept, 1 - x, 1), "x"))
-    else:
-        kept = kept.reshape(4, 128, 2, cols)
-        kept = add_low(pick(kept, y, 2), swap_link(pick(kept, 1 - y, 2), "y"))
-    return kept
-
-
-def settle_along_z(kept):
-    z, x, c, y = place()
-    cols = kept.shape[-1]
-    kept = kept.reshape(2, 2, 128, cols)
-    high, lower = lax.div(z, 2), lax.rem(z, 2)
-    kept = add_low(pick(kept, high, 0), swap_link(pick(kept, 1 - high, 0), "z2"))
-    kept = add_low(pick(kept, lower, 0), swap_link(pick(kept, 1 - lower, 0), "z1"))
-    kept = kept.reshape(2, BLOCK, cols)
-    near, other = pick(kept, c, 0), swap_link(pick(kept, 1 - c, 0), "core")
-    return in_order(near[None], other[None], c, 0)
-
-
-def all_total(block):
-    for link in ("core", "x", "y", "z1", "z2"):
-        block = block + swap_link(block, link)
-    return block
+COLS = 256
+SETTLE_DEPTH = 6
+VAL_SLOTS, ARRIVAL_SLOTS = 6, 3
+
+
+class Settle:
+    def __init__(self, widths, pairs):
+        self.widths, self.pairs = widths, pairs
+
+    def scratch(self):
+        rows = (4, 2, 2, BLOCK, COLS)
+        pairs, vals, slots = len(self.pairs), VAL_SLOTS, ARRIVAL_SLOTS
+        sem = pltpu.SemaphoreType.DMA
+        return dict(
+            left_in=pltpu.VMEM((2, ROWS, 1024), LOW),
+            left_turned=pltpu.VMEM((4, 1024, DEEP), LOW),
+            right_in=pltpu.VMEM((2, 2, 4, DEEP, COLS), LOW),
+            core_out=pltpu.VMEM((2, 2, 2, *rows), LOW),
+            core_in=pltpu.VMEM((slots, 2, 2, *rows), LOW),
+            val=pltpu.VMEM((vals, 2, 2, *rows), LOW),
+            first_a=pltpu.VMEM((slots, *rows), LOW),
+            first_b=pltpu.VMEM((slots, 2, 4, 2, BLOCK, COLS), LOW),
+            second=pltpu.VMEM((slots, 2, 4, 2, BLOCK, COLS), LOW),
+            third=pltpu.VMEM((slots, 2, 2, 2, BLOCK, COLS), LOW),
+            fourth=pltpu.VMEM((slots, 2, 2, BLOCK, COLS), LOW),
+            fifth=pltpu.VMEM((slots, 2, BLOCK, COLS), LOW),
+            send_sem=sem((pairs, 2, SETTLE_DEPTH)),
+            recv_sem=sem((pairs, 2, SETTLE_DEPTH)),
+            right_sem=sem((pairs, 2, 4)),
+            left_sem=sem((len(self.widths),)),
+        )
+
+    def bind(self, lefts, rights, outs, refs):
+        self.lefts, self.rights, self.outs = lefts, rights, outs
+        for name, ref in zip(self.scratch(), refs, strict=True):
+            setattr(self, name, ref)
+        self.z, self.x, self.c, self.y = place()
+        self.partners = neighbours()
+        self.copies = {}
+        self.left_copies = {}
+        self.turned = {}
+        self.loaded = []
+        tail = ROWS // 128 * 128
+        self.left_turned[:, :, pl.ds(tail, DEEP - tail)] = jnp.zeros((4, 1024, DEEP - tail), LOW)
+        self.right_in[:, :, :, pl.ds(ROWS, DEEP - ROWS)] = jnp.zeros(
+            (2, 2, 4, DEEP - ROWS, COLS), LOW
+        )
+
+    def load(self, pair):
+        if pair >= len(self.pairs):
+            return
+        for unit, (matrix, step) in enumerate(self.pairs[pair]):
+            if matrix not in self.left_copies:
+                copy = pltpu.make_async_copy(
+                    self.lefts[matrix],
+                    self.left_in.at[len(self.loaded) % 2],
+                    self.left_sem.at[len(self.loaded)],
+                )
+                copy.start()
+                self.left_copies[matrix] = (copy, len(self.loaded))
+                self.loaded.append(matrix)
+            width = self.widths[matrix]
+            for t in range(2):
+                for core in range(2):
+                    at = t * width + core * (width // 2) + step * COLS
+                    copy = pltpu.make_async_copy(
+                        self.rights[matrix].at[:, pl.ds(at, COLS)],
+                        self.right_in.at[pair % 2, unit, 2 * t + core, pl.ds(0, ROWS)],
+                        self.right_sem.at[pair, unit, 2 * t + core],
+                    )
+                    copy.start()
+                    self.copies[(pair, unit, "right", 2 * t + core)] = copy
+
+    def wait_load(self, pair):
+        for unit, (matrix, _) in enumerate(self.pairs[pair]):
+            if matrix not in self.turned:
+                copy, at = self.left_copies[matrix]
+                copy.wait()
+                self.left_turned[at % 4, :, pl.ds(0, ROWS)] = self.left_in[at % 2].T
+                self.turned[matrix] = at % 4
+            for entry in range(4):
+                self.copies.pop((pair, unit, "right", entry)).wait()
+
+    def send(self, pair, unit, stage, source, target, link):
+        copy = pltpu.make_async_remote_copy(
+            src_ref=source,
+            dst_ref=target,
+            send_sem=self.send_sem.at[pair, unit, stage],
+            recv_sem=self.recv_sem.at[pair, unit, stage],
+            device_id=self.partners[link],
+            device_id_type=MESH_IDS,
+        )
+        copy.start()
+        self.copies[(pair, unit, stage)] = copy
+
+    def product(self, pair, unit, t, core, z):
+        matrix, _ = self.pairs[pair][unit]
+        at = pl.multiple_of(z * 256, 256)
+        left = self.left_turned[self.turned[matrix], pl.ds(at, 256), :]
+        right = self.right_in[pair % 2, unit, 2 * t + core]
+        total = dot_rows(left[:, :512], right[:512]) + dot_rows(left[:, 512:], right[512:])
+        return total.reshape(2, 2, BLOCK, COLS)
+
+    def stage(self, pair, unit, stage):
+        if pair < 0 or pair >= len(self.pairs):
+            return
+        z, x, c, y = self.z, self.x, self.c, self.y
+        slot, arrival = pair % VAL_SLOTS, pair % ARRIVAL_SLOTS
+        high, lower = lax.div(z, 2), lax.rem(z, 2)
+        near_pair, far_pair = pl.ds(2 * high, 2), pl.ds(2 * (1 - high), 2)
+        far_z = z + 1 - 2 * lower
+        val = self.val.at[slot, unit]
+        if stage == 0:
+            out = self.core_out.at[pair % 2, unit]
+
+            @pl.loop(0, 4)
+            def _(row):
+                for t in range(2):
+                    out[t, row] = self.product(pair, unit, t, 1 - c, row).astype(LOW)
+
+            self.send(pair, unit, 0, out, self.core_in.at[arrival, unit], "core")
+            return
+        self.copies.pop((pair, unit, stage - 1)).wait()
+        if stage == 1:
+            other = self.core_in.at[arrival, unit]
+
+            @pl.loop(0, 4)
+            def _(row):
+                for t in range(2):
+                    total = self.product(pair, unit, t, c, row)
+                    val[t, row] = (total + other[t, row].astype(jnp.float32)).astype(LOW)
+
+            if unit == 0:
+                self.send(pair, unit, 1, val.at[1 - y], self.first_a.at[arrival], "y")
+            else:
+                self.send(pair, unit, 1, val.at[:, :, 1 - x], self.first_b.at[arrival], "x")
+        elif stage == 2:
+            target = self.second.at[arrival, unit]
+            if unit == 0:
+
+                @pl.loop(0, 4)
+                def _(row):
+                    val[y, row] = val[y, row] + self.first_a[arrival, row]
+
+                self.send(pair, unit, 2, val.at[y, :, 1 - x], target, "x")
+            else:
+
+                @pl.loop(0, 4)
+                def _(row):
+                    for t in range(2):
+                        val[t, row, x] = val[t, row, x] + self.first_b[arrival, t, row]
+
+                self.send(pair, unit, 2, val.at[1 - y, :, x], target, "y")
+        elif stage == 3:
+
+            @pl.loop(0, 4)
+            def _(row):
+                val[y, row, x] = val[y, row, x] + self.second[arrival, unit, row]
+
+            target = self.third.at[arrival, unit]
+            self.send(pair, unit, 3, val.at[y, far_pair, x], target, "z2")
+        elif stage == 4:
+            for row in range(2):
+                at = 2 * high + row
+                val[y, at, x] = val[y, at, x] + self.third[arrival, unit, row]
+            target = self.fourth.at[arrival, unit]
+            self.send(pair, unit, 4, val.at[y, far_z, x], target, "z1")
+        elif stage == 5:
+            val[y, z, x] = val[y, z, x] + self.fourth[arrival, unit]
+            target = self.fifth.at[arrival, unit]
+            self.send(pair, unit, 5, val.at[y, z, x, 1 - c], target, "core")
+        else:
+            matrix, step = self.pairs[pair][unit]
+            out_ref, layer = self.outs[matrix]
+            cols = pl.ds(step * COLS, COLS)
+            out_ref[layer, c, :, cols] = val[y, z, x, c].astype(jnp.float32)
+            out_ref[layer, 1 - c, :, cols] = self.fifth[arrival, unit].astype(jnp.float32)
+
+    def tick(self, pair):
+        for stage in range(SETTLE_DEPTH, 0, -1):
+            for unit in range(2):
+                self.stage(pair - stage, unit, stage)
+        self.load(pair + 1)
+        if pair < len(self.pairs):
+            self.wait_load(pair)
+            for unit in range(2):
+                self.stage(pair, unit, 0)
+
+
+TOTAL_LINKS = ("x", "y", "z1", "z2", "core")
+
+
+def settle_kernel(plan, kinds, layers, *refs):
+    matrices = kinds * layers
+    lefts, rights = refs[:matrices], refs[matrices : 2 * matrices]
+    small_ref = refs[2 * matrices]
+    refs = refs[2 * matrices + 1 :]
+    outs, total_ref, refs = refs[:kinds], refs[kinds], refs[kinds + 1 :]
+    sums, sums_in, sums_send, sums_recv = refs[:4]
+    plan.bind(
+        lefts, rights, [(outs[m % kinds], m // kinds) for m in range(matrices)], refs[4:]
+    )
+    plan.load(0)
+    greet(plan.partners)
+    sums[0] = small_ref[...]
+    flying = None
+    for pair in range(len(plan.pairs) + SETTLE_DEPTH):
+        if flying is not None:
+            flying.wait()
+            sums[pair] = sums[pair - 1] + sums_in[pair - 1]
+            flying = None
+        if pair < len(TOTAL_LINKS):
+            flying = pltpu.make_async_remote_copy(
+                src_ref=sums.at[pair],
+                dst_ref=sums_in.at[pair],
+                send_sem=sums_send.at[pair],
+                recv_sem=sums_recv.at[pair],
+                device_id=plan.partners[TOTAL_LINKS[pair]],
+                device_id_type=MESH_IDS,
+            )
+            flying.start()
+        plan.tick(pair)
+    total_ref[...] = sums[len(TOTAL_LINKS)]
+
+
+def layer_pairs(base, widths):
+    feed = [((base + 2, k), (base + 3, k)) for k in range(widths[2] // 2 // COLS)]
+    rest = [(base, k) for k in range(widths[0] // 2 // COLS)]
+    rest.insert(1, (base + 1, 0))
+    return feed + [(rest[k], rest[k + 1]) for k in range(0, len(rest), 2)]
+
+
+def settle_all(layer_terms, small):
+    layers, kinds = len(layer_terms), len(layer_terms[0])
+    widths = [right.shape[1] // 2 for _, right in layer_terms[0]]
+    pairs = []
+    for layer in reversed(range(layers)):
+        pairs += layer_pairs(layer * kinds, widths)
+    plan = Settle(widths * layers, pairs)
+    lefts = [left for terms in layer_terms for left, _ in terms]
+    rights = [right for terms in layer_terms for _, right in terms]
+    steps = len(TOTAL_LINKS)
+    any_spec, vmem_spec = pl.BlockSpec(memory_space=pl.ANY), pl.BlockSpec(memory_space=pltpu.VMEM)
+    return pl.pallas_call(
+        lambda *refs: settle_kernel(plan, kinds, layers, *refs),
+        out_shape=[jax.ShapeDtypeStruct((layers, 2, BLOCK, width // 2), jnp.float32) for width in widths]
+        + [jax.ShapeDtypeStruct(small.shape, jnp.float32)],
+        in_specs=[any_spec] * (2 * kinds * layers) + [vmem_spec],
+        out_specs=[vmem_spec] * (kinds + 1),
+        scratch_shapes=[
+            pltpu.VMEM((steps + 1, *small.shape), jnp.float32),
+            pltpu.VMEM((steps, *small.shape), jnp.float32),
+            pltpu.SemaphoreType.DMA((steps,)),
+            pltpu.SemaphoreType.DMA((steps,)),
+            *plan.scratch().values(),
+        ],
+        compiler_params=pltpu.CompilerParams(
+            collective_id=1, has_side_effects=True, vmem_limit_bytes=58 * 1024 * 1024
+        ),
+        cost_estimate=pl.CostEstimate(
+            flops=24 * 4 * 1024 * 1024 * ROWS, bytes_accessed=700 * 1024 * 1024, transcendentals=0
+        ),
+        name="settle_all",
+    )(*lefts, *rights, small)
 
 
 def in_order(own, other, index, axis):
@@ -844,6 +1064,7 @@
     near_tokens = pick(tokens, y, 1)
     far_tokens = swap_link(pick(tokens, far, 1), "y")
     tokens = in_order(near_tokens, far_tokens, y, 2)
+    tokens = jnp.pad(tokens, ((0, 0), (0, ROWS - SEQ), (0, 0)))
     biases = jnp.concatenate(
         (query_bias, jnp.zeros_like(query_bias), value_bias, out_bias, down_bias, up_bias), axis=1
     )
@@ -889,7 +1110,7 @@
 
     upstream = tokens[1].astype(jnp.float32)
     small = [None] * layers
-    owned = [None] * layers
+    terms = [None] * layers
     for layer in reversed(range(layers)):
         project_w, out_w, up_w, down_w = whole[layer]
         (
@@ -906,10 +1127,10 @@
         ) = saved[layer]
         down_bias_sum = jnp.sum(upstream, axis=0)
         upstream_low = upstream.astype(LOW)
-        down_term = settle(upstream_low, hidden, "x")
+        down_term = (upstream_low, hidden)
         hidden_grad = (dot_rows(upstream_low, down_w) * gelu_slope(before)).astype(LOW)
         up_bias_sum = jnp.sum(hidden_grad.astype(jnp.float32), axis=0)
-        up_term = settle(normed_two, hidden_grad, "y")
+        up_term = (normed_two, hidden_grad)
         normed_two_grad = dot_cols(hidden_grad, up_w)
         second_gain_sum = jnp.sum(normed_two_grad * centred_two, axis=0)
         second_shift_sum = jnp.sum(normed_two_grad, axis=0)
@@ -918,57 +1139,47 @@
         )
         out_bias_sum = jnp.sum(upstream, axis=0)
         upstream_low = upstream.astype(LOW)
-        out_term = settle(upstream_low, heads, "x")
+        out_term = (upstream_low, heads)
         heads_grad = dot_rows(upstream_low, out_w).astype(LOW)
         joined = mix_heads_backward(projected, heads_grad)
         joined_sums = jnp.sum(joined.astype(jnp.float32), axis=0).reshape(2, 3, half)
-        project_term = settle(normed, joined, "y")
+        project_term = (normed, joined)
         normed_grad = dot_cols(joined, project_w)
         first_gain_sum = jnp.sum(normed_grad * centred, axis=0)
         first_shift_sum = jnp.sum(normed_grad, axis=0)
         upstream = upstream + whole_norm_backward(
             normed_grad, centred, inverse, row(first_gain, layer)
         )
-        small[layer] = all_total(
-            jnp.concatenate(
-                (
-                    joined_sums[:, 0].reshape(-1),
-                    joined_sums[:, 2].reshape(-1),
-                    out_bias_sum,
-                    up_bias_sum,
-                    down_bias_sum,
-                    first_gain_sum,
-                    first_shift_sum,
-                    second_gain_sum,
-                    second_shift_sum,
-                )
-            )
-        )
-        feed_own = settle_along_z(jnp.concatenate((up_term, down_term), axis=2))
-        mixed_own = settle_along_z(jnp.concatenate((project_term, out_term), axis=2))
-        owned[layer] = (feed_own, mixed_own)
-
-    totals = jnp.stack(small)
+        small[layer] = jnp.concatenate(
+            (
+                joined_sums[:, 0].reshape(-1),
+                joined_sums[:, 2].reshape(-1),
+                out_bias_sum,
+                up_bias_sum,
+                down_bias_sum,
+                first_gain_sum,
+                first_shift_sum,
+                second_gain_sum,
+                second_shift_sum,
+            )
+        )
+        terms[layer] = (project_term, out_term, up_term, down_term)
+
     width = 2 * half
+    project_out, out_out, up_out, down_out, totals = settle_all(
+        terms, jnp.stack(small).reshape(-1, width)
+    )
+    totals = totals.reshape(layers, -1)
+    project_out, out_out, up_out, down_out = [
+        jnp.swapaxes(block, 1, 2).reshape(layers, BLOCK, -1)
+        for block in (project_out, out_out, up_out, down_out)
+    ]
     small_outs, at = [], 0
     for size in (width, width, width, hidden_width, width, width, width, width, width):
         small_outs.append(totals[:, at : at + size])
         at += size
-    feed_own = jnp.stack([owned[layer][0] for layer in range(layers)])
-    mixed_own = jnp.stack([owned[layer][1] for layer in range(layers)])
-
-    def weight_out(pieces, start, size):
-        block = jnp.swapaxes(pieces[..., start : start + size].astype(jnp.float32), 1, 2)
-        return block.reshape(layers, BLOCK, 2 * size)
-
-    quarter = hidden_width // 4
-    project_out = weight_out(mixed_own, 0, 3 * half // 2)
-    out_out = weight_out(mixed_own, 3 * half // 2, half // 2)
-    up_out = weight_out(feed_own, 0, quarter)
-    down_out = weight_out(feed_own, quarter, quarter)
-
     def to_owner(rows):
-        parts = rows.reshape(SEQ, 2, half)
+        parts = rows[:SEQ].reshape(SEQ, 2, half)
         near = pick(parts, y, 1)
         moved = swap_link(pick(parts, far, 1).astype(LOW), "y")
         return in_order(near, moved.astype(near.dtype), y, 0)

time: 1260 us -> 773 us (0.61)
  local copies, waits for them, and re-layouts: 348 us -> 40.3 us
  waiting for transfers between devices: 273 us -> 21.8 us
  Pallas kernels: 321 us -> 559 us
  matrix products: 210 us -> 118 us
  starting transfers between devices: 45.9 us -> 5.2 us
  other arithmetic: 53.4 us -> 21.2 us
    pallas_call x0 -> x1, Pallas kernels: none -> 239 us  [settle_all(): pl.pallas_call(lambda *refs: settle_kernel(plan, kinds, layers, *refs), o...]
    dynamic_slice x16 -> x2, local copies, waits for them, and re-layouts: 183 us -> 4.44 us  [pick(): return lax.dynamic_index_in_dim(block, at, axis, keepdims=False)]
    ppermute x44 -> x0, waiting for transfers between devices: 162 us -> none  [swap_link(): return lax.ppermute(block, 'wide', [(i, i ^ flip) for i in range(16)])]
    dot_general x32 -> x0, matrix products: 93.7 us -> none  [dot_tokens(): lax.dot_general(left, right, (((0,), (0,)), ((), ())), preferred_element_...]
    ppermute x14 -> x4, waiting for transfers between devices: 111 us -> 21.8 us  [swap_link(): return lax.ppermute(block, 'tensor', [(0, 1), (1, 0)])]
    reshape x20 -> x8, local copies, waits for them, and re-layouts: 93.4 us -> 15.3 us  [the longest x2 8.13 us: to_owner(): parts = rows[:SEQ].reshape(SEQ, 2, half)]
    unnamed x324 -> x143, local copies, waits for them, and re-layouts: 49.9 us -> 8.79 us
    ppermute x44 -> x0, starting transfers between devices: 30.1 us -> none  [swap_link(): return lax.ppermute(block, 'wide', [(i, i ^ flip) for i in range(16)])]
  transfers between devices with their start and end apart: 58 -> 4, of which waited for: 23 -> 2; matrix products, arithmetic and copies ran while one was open for 31% -> 1% of each run, Pallas kernels for 19% -> 31%
where the time goes in v3:
time: 773 us; the launch traced here: 767 us
  Pallas kernels  559 us (72%)
  matrix products  118 us (15%)
  local copies, waits for them, and re-layouts  40.3 us (5%)
  waiting for transfers between devices  21.8 us (3%)
  other arithmetic  21.2 us (3%)
    pallas_call x1, Pallas kernels, settle_all(): pl.pallas_call(lambda *refs: settle_kernel(plan, kinds, layers, *refs), o...  239 us
    pallas_call x1, Pallas kernels, gather_weights(): pl.pallas_call(lambda *refs: gather_kernel(layers, kinds, *refs), out_sha...  236 us
    dot_general x8, matrix products, dot_rows(): lax.dot_general(left, right, (((1,), (0,)), ((), ())), preferred_element_...  60 us
    dot_general x8, matrix products, dot_cols(): lax.dot_general(left, right, (((1,), (1,)), ((), ())), preferred_element_...  57.8 us
    pallas_call x2, Pallas kernels, mix_heads_backward(): pl.pallas_call(heads_backward_kernel, grid=(blocks,), in_specs=projected_...  56.3 us
    pallas_call x2, Pallas kernels, mix_heads(): pl.pallas_call(heads_kernel, grid=(blocks,), in_specs=projected_specs(blo...  27.3 us
    ppermute x4, waiting for transfers between devices, swap_link(): return lax.ppermute(block, 'tensor', [(0, 1), (1, 0)])  21.8 us
  transfers between devices with their start and end apart: 4, of which 2 were waited for; matrix products, arithmetic and copies ran while one was open for 1% of the time, Pallas kernels for 31%

profile of v3, /device:TPU:0, one launch (start us, length us, event | category | flops | bytes accessed | tf_op | source)
XLA Modules:
  0.0 767.3 jit_solution(8705776757828260393)
XLA Ops:
  14.7 236.2 %gather_weights.1 = (bf16[4,2,2,64,3072]{4,3,2,1,0:T(8,128)(2,1)}, bf16[4,2,2,64,1024]{4,3,2,1,0:T(8,128)(2,1)}, bf16[4,2,2,64,4096]{4,3,2,1,0:T(8,128)(2,1)}, b...) custom-call(bf16[2,64,1536]{2,1,0:T(8,128)(2,1)} %pad_maximum_fusion, ...), custom_call_target="tpu_custom_call" | custom-call | bytes 629145600 | tf_op jit(solution)/shard_map/gather_weights/pallas_call | solution.py:583
  255.9 4.6 add_convert_fusion.1.query_a.key_a.value_a.query_b.key_b.value_b
  260.6 13.6 %mix_heads.2.refs_9_ = bf16[592,1024]{1,0:T(8,128)(2,1)S(1)} custom-call(bf16[592,3072]{1,0:T(8,128)(2,1)S(1)} %add_convert_fusion.1.query_a.key_a.value_a.query_b.key_b.value_b, bf16[592,3072]{1,0:T(8,128)(2,1)S(1)} %add_convert_fusion.1.query_a.key_a.value_a.query_b.key_b.value_b, ...), custom_call_target="tpu_custom_call" | custom-call | flops 1363677184 | bytes 47185920 | tf_op jit(solution)/shard_map/mix_heads/pallas_call | solution.py:667
  278.6 8.9 %multiply_convert_fusion.1 = (bf16[592,4096]{1,0:T(8,128)(2,1)}, f32[592,4096]{1,0:T(8,128)}) fusion(f32[4096]{0:T(1024)S(1)} %bitcast.168, bf16[592,1024]{1,0:T(8,128)(2,1)S(1)} %add_convert_fusion.5.refs_2_, bf16[1024,4096]{1,0:T(8,128)(2,1)S(1)} %bitcast.189), kind=kOutput, calls=%fused_computation.18 | convolution fusion | flops 4980604928 | bytes 24166400 | tf_op jit(solution)/shard_map/dot_general | solution.py:609
  287.6 8.0 %fusion.41 = (f32[592]{0:T(1024)S(1)}, f32[592]{0:T(1024)S(1)}, f32[592,1024]{1,0:T(8,128)S(1)}) fusion(f32[1024]{0:T(1024)S(1)} %bitcast.183, f32[592,1024]{1,0:T(8,128)S(1)} %get-tuple-element.124, bf16[592,4096]{1,0:T(8,128)(2,1)} %get-tuple-element.125.refs_11_, bf16[1024,4096]{1,0:T(8,128)(2,1)S(1)} %bitcast.196), kind=kOutput, calls=%fused_computation.169 | convolution fusion | flops 4969085952 | bytes 18096768 | tf_op jit(solution)/shard_map/dot_general | solution.py:615
  296.1 4.2 add_convert_fusion.query_a.key_a.value_a.query_b.key_b.value_b
  300.3 13.6 %mix_heads.3.refs_13_ = bf16[592,1024]{1,0:T(8,128)(2,1)S(1)} custom-call(bf16[592,3072]{1,0:T(8,128)(2,1)S(1)} %add_convert_fusion.query_a.key_a.value_a.query_b.key_b.value_b, bf16[592,3072]{1,0:T(8,128)(2,1)S(1)} %add_convert_fusion.query_a.key_a.value_a.query_b.key_b.value_b, ...), custom_call_target="tpu_custom_call" | custom-call | flops 1363677184 | bytes 47185920 | tf_op jit(solution)/shard_map/mix_heads/pallas_call | solution.py:667
  316.2 11.9 %multiply_convert_fusion = (bf16[592,4096]{1,0:T(8,128)(2,1)}, f32[592,4096]{1,0:T(8,128)}) fusion(f32[4096]{0:T(1024)S(1)} %bitcast.170, bf16[592,1024]{1,0:T(8,128)(2,1)S(1)} %add_convert_fusion.3.refs_6_, bf16[1024,4096]{1,0:T(8,128)(2,1)} %bitcast.197), kind=kOutput, calls=%fused_computation.16 | convolution fusion | flops 4980604928 | bytes 24166400 | tf_op jit(solution)/shard_map/dot_general | solution.py:609
  328.1 13.3 %convert_reduce_fusion = (f32[4096]{0:T(1024)S(1)}, bf16[592,4096]{1,0:T(8,128)(2,1)}) fusion(f32[592,4096]{1,0:T(8,128)} %get-tuple-element.130, f32[4096]{0:T(1024)S(1)} %bitcast.171, bf16[1024,4096]{1,0:T(8,128)(2,1)} %bitcast.185, bf16[2,592,1024]{2,1,0:T(8,128)(2,1)S(1)} %fusion.24), kind=kOutput, calls=%fused_computation.14 | convolution fusion | flops 4997574656 | bytes 24182784 | tf_op jit(solution)/shard_map/dot_general | solution.py:609
  341.4 9.8 %multiply_reduce_fusion = (f32[1024]{0:T(1024)S(1)}, f32[592]{0:T(1024)S(1)}, f32[592]{0:T(1024)S(1)}, f32[1024]{0:T(1024)S(1)}, f32[592,1024]{1,0:T(8,128)S(1)}) fusion(f32[592,1024]{1,0:T(8,128)S(1)} %get-tuple-element.128, f32[592]{0:T(1024)S(1)} %get-tuple-element.109, f32[592]{0:T(1024)S(1)} %get-tuple-element.108, f32[1024]{0:T(1024)S(1)} %bitcast.153, ...), kind=kOutput, calls=%fused_computation.43 | convolution fusion | flops 4971508736 | bytes 18109696 | tf_op jit(solution)/shard_map/dot_general | solution.py:615
  354.9 28.0 %mix_heads_backward.2.refs_12_ = bf16[592,3072]{1,0:T(8,128)(2,1)S(1)} custom-call(bf16[592,3072]{1,0:T(8,128)(2,1)} %copy-done.1, bf16[592,3072]{1,0:T(8,128)(2,1)} %copy-done.1, bf16[592,3072]{1,0:T(8,128)(2,1)} %copy-done.1, bf16[592,3072]{1,0:T(8,128)(2,1)} %copy-done.1, bf16[592,3072]{1,0:T(8,128)(2,1)} %copy-done.1, bf16[592,3072]{1,0:T(8,128)(2,1)} %copy-done.1, ...), custom_call_target="tpu_custom_call" | custom-call | flops 3409192960 | bytes 94371840 | tf_op jit(solution)/shard_map/mix_heads_backward/pallas_call | solution.py:715
  383.7 7.3 multiply_reduce_fusion.1
  392.2 14.2 %convert_reduce_fusion.1 = (f32[4096]{0:T(1024)S(1)}, bf16[592,4096]{1,0:T(8,128)(2,1)}) fusion(f32[592,4096]{1,0:T(8,128)} %get-tuple-element.126, f32[4096]{0:T(1024)S(1)} %bitcast.169, bf16[592,1024]{1,0:T(8,128)(2,1)S(1)} %convert_element_type.218.refs_3_, bf16[1024,4096]{1,0:T(8,128)(2,1)} %bitcast.193), kind=kOutput, calls=%fused_computation.15 | convolution fusion | flops 4997574656 | bytes 24182784 | tf_op jit(solution)/shard_map/dot_general | solution.py:609
  406.5 8.1 %multiply_reduce_fusion.2 = (f32[1024]{0:T(1024)S(1)}, f32[592]{0:T(1024)S(1)}, f32[592]{0:T(1024)S(1)}, f32[1024]{0:T(1024)S(1)}, f32[592,1024]{1,0:T(8,128)S(1)}) fusion(f32[592,1024]{1,0:T(8,128)S(1)} %get-tuple-element.124, f32[592]{0:T(1024)S(1)} %copy-done.29, f32[592]{0:T(1024)S(1)} %copy-done.27, f32[1024]{0:T(1024)S(1)} %bitcast.156, ...), kind=kOutput, calls=%fused_computation.45 | convolution fusion | flops 4971508736 | bytes 18109696 | tf_op jit(solution)/shard_map/dot_general | solution.py:615
  418.8 28.3 %mix_heads_backward.3.refs_8_ = bf16[592,3072]{1,0:T(8,128)(2,1)S(1)} custom-call(bf16[592,3072]{1,0:T(8,128)(2,1)} %copy-done, bf16[592,3072]{1,0:T(8,128)(2,1)} %copy-done, bf16[592,3072]{1,0:T(8,128)(2,1)} %copy-done, bf16[592,3072]{1,0:T(8,128)(2,1)} %copy-done, bf16[592,3072]{1,0:T(8,128)(2,1)} %copy-done, bf16[592,3072]{1,0:T(8,128)(2,1)} %copy-done, ...), custom_call_target="tpu_custom_call" | custom-call | flops 3409192960 | bytes 94371840 | tf_op jit(solution)/shard_map/mix_heads_backward/pallas_call | solution.py:715
  448.0 10.5 %multiply_reduce_fusion.3 = (f32[1024]{0:T(1024)S(1)}, f32[592]{0:T(1024)S(1)}, f32[592]{0:T(1024)S(1)}, f32[1024]{0:T(1024)S(1)}, f32[1024]{0:T(1024)S(1)}, /*i...) fusion(f32[592]{0:T(1024)S(1)} %copy-done.31, f32[592]{0:T(1024)S(1)} %copy-done.43, ...), kind=kOutput, calls=%fused_computation.46 | convolution fusion | flops 3733630976 | bytes 18445568 | tf_op jit(solution)/shard_map/dot_general | solution.py:615
  460.7 10.7 %fusion.50 = f32[592,1024]{1,0:T(8,128)} fusion(bf16[592,4096]{1,0:T(8,128)(2,1)} %get-tuple-element.129.refs_15_, bf16[1024,4096]{1,0:T(8,128)(2,1)} %bitcast.186), kind=kOutput, calls=%fused_computation.178 | convolution fusion | flops 4966055936 | bytes 15663104 | tf_op jit(solution)/shard_map/dot_general | solution.py:615
  471.4 239.1 %settle_all.1 = (f32[2,2,64,768]{3,2,1,0:T(8,128)}, f32[2,2,64,256]{3,2,1,0:T(8,128)}, f32[2,2,64,1024]{3,2,1,0:T(8,128)}, f32[2,2,64,1024]{3,2,1,0:T(8,128)}, f32[24,1024]{1,0:T(8,128)}) custom-call(bf16[592,1024]{1,0:T(8,128)(2,1)} %get-tuple-element.75.refs_0_, bf16[592,1024]{1,0:T(8,128)(2,1)} %copy-done.15, bf16[592,1024]{1,0:T(8,128)(2,1)} %copy-done.10, ...), custom_call_target="tpu_custom_call" | custom-call | flops 59592671232 | bytes 734003200 | tf_op jit(solution)/shard_map/settle_all/pallas_call | solution.py:983
  717.7 4.3 slice_add_fusion
  722.0 4.4 reshape.306
  729.8 3.7 reshape.305
  733.5 3.4 constant_dynamic-slice_fusion.3
  742.0 11.5 %collective-permute-done.3 = bf16[577,512]{1,0:T(8,128)(2,1)S(1)} collective-permute-done((bf16[577,512]{1,0:T(8,128)(2,1)S(1)}, bf16[577,512]{1,0:T(8,128)(2,1)S(1)}, u32[]{:S(2)}, u32[]{:S(2)}) %collective-permute-start.3) | collective-permute-done | bytes 590880 | tf_op jit(solution)/shard_map/ppermute | solution.py:731
  755.5 10.2 %collective-permute-done.2 = bf16[577,512]{1,0:T(8,128)(2,1)S(1)} collective-permute-done((bf16[577,512]{1,0:T(8,128)(2,1)S(1)}, bf16[577,512]{1,0:T(8,128)(2,1)S(1)}, u32[]{:S(2)}, u32[]{:S(2)}) %collective-permute-start.2) | collective-permute-done | bytes 590880 | tf_op jit(solution)/shard_map/ppermute | solution.py:731
  (222 shorter events, 57.0 us)
Async XLA Ops:
  10.6 241.0 %collective-permute-start = (bf16[2,577,512]{2,0,1:T(2,128)(2,1)}, bf16[2,577,512]{2,0,1:T(2,128)(2,1)}, u32[]{:S(2)}, u32[]{:S(2)}) collective-permute-start(bf16[2,577,512]{2,0,1:T(2,128)(2,1)} %copy.53), channel_id=1, source_target_pairs={{0,1},{1,0},{2,3},{3,2},{4,5},{5,4},{6,7},{7,6},{8,9},{9,8},{10,11... | collective-permute-start | bytes 3545096 | tf_op jit(solution)/shard_map/ppermute | solution.py:731
  13.7 237.2 %collective-permute-start.1 = (bf16[2,4608]{1,0:T(2,128)(2,1)S(1)}, bf16[2,4608]{1,0:T(2,128)(2,1)S(1)}, u32[]{:S(2)}, u32[]{:S(2)}) collective-permute-start(bf16[2,4608]{1,0:T(2,128)(2,1)S(1)} %constant_dynamic-update-slice_fusion.2), channel_id=1, source_target_pairs={{0,1},{1,0},{2,3},{3,2},{4,5},{5,4},{6,7},{7,6},{8,9},{9,8},{10,11... | collective-permute-start | bytes 55304 | tf_op jit(solution)/shard_map/ppermute | solution.py:731
  13.8 240.3 %copy-start.38 = (f32[1,1024]{1,0:T(1,128)}, f32[1,1024]{1,0:T(1,128)S(1)}, u32[]{:S(2)}) copy-start(f32[1,1024]{1,0:T(1,128)S(1)} %get-tuple-element.117) | copy-start | bytes 12292
  13.8 240.3 %copy-start.40 = (f32[1,1024]{1,0:T(1,128)}, f32[1,1024]{1,0:T(1,128)S(1)}, u32[]{:S(2)}) copy-start(f32[1,1024]{1,0:T(1,128)S(1)} %get-tuple-element.119) | copy-start | bytes 12292
  13.9 262.2 %copy-start.24 = (f32[1,1024]{1,0:T(1,128)}, f32[1,1024]{1,0:T(1,128)S(1)}, u32[]{:S(2)}) copy-start(f32[1,1024]{1,0:T(1,128)S(1)} %get-tuple-element.111) | copy-start | bytes 12292
  260.5 13.7 %copy-start = (bf16[592,3072]{1,0:T(8,128)(2,1)}, bf16[592,3072]{1,0:T(8,128)(2,1)S(1)}, u32[]{:S(2)}) copy-start(bf16[592,3072]{1,0:T(8,128)(2,1)S(1)} %add_convert_fusion.1.query_a.key_a.value_a.query_b.key_b.value_b) | copy-start | bytes 10911748
  260.6 13.7 %copy-start.49 = (bf16[4,2,2,64,1024]{4,3,2,1,0:T(8,128)(2,1)S(1)}, bf16[4,2,2,64,1024]{4,3,2,1,0:T(8,128)(2,1)}, u32[]{:S(2)}) copy-start(bf16[4,2,2,64,1024]{4,3,2,1,0:T(8,128)(2,1)} %get-tuple-element.31) | copy-start | bytes 6291460
  276.0 11.5 %copy-start.26 = (f32[592]{0:T(1024)}, f32[592]{0:T(1024)S(1)}, u32[]{:S(2)}) copy-start(f32[592]{0:T(1024)S(1)} %get-tuple-element.120) | copy-start | bytes 7108
  276.0 11.5 %copy-start.28 = (f32[592]{0:T(1024)}, f32[592]{0:T(1024)S(1)}, u32[]{:S(2)}) copy-start(f32[592]{0:T(1024)S(1)} %get-tuple-element.121) | copy-start | bytes 7108
  276.1 11.5 %slice-start.4 = ((s8[8388608]{0:T(1024)(128)(4,1)}), s8[4194304]{0:T(1024)(128)(4,1)S(1)}, s32[]{:S(2)}) async-start(s8[8388608]{0:T(1024)(128)(4,1)} %bitcast.194), calls=%async_computation.4 | async-start | bytes 8388608
  276.5 11.0 %copy-start.10 = (bf16[592,1024]{1,0:T(8,128)(2,1)}, bf16[592,1024]{1,0:T(8,128)(2,1)S(1)}, u32[]{:S(2)}) copy-start(bf16[592,1024]{1,0:T(8,128)(2,1)S(1)} %add_convert_fusion.5.refs_2_) | copy-start | bytes 3637252
  300.3 13.7 %copy-start.1 = (bf16[592,3072]{1,0:T(8,128)(2,1)}, bf16[592,3072]{1,0:T(8,128)(2,1)S(1)}, u32[]{:S(2)}) copy-start(bf16[592,3072]{1,0:T(8,128)(2,1)S(1)} %add_convert_fusion.query_a.key_a.value_a.query_b.key_b.value_b) | copy-start | bytes 10911748
  300.3 13.7 %copy-start.51 = (bf16[4,2,2,64,1024]{4,3,2,1,0:T(8,128)(2,1)S(1)}, bf16[4,2,2,64,1024]{4,3,2,1,0:T(8,128)(2,1)}, u32[]{:S(2)}) copy-start(bf16[4,2,2,64,1024]{4,3,2,1,0:T(8,128)(2,1)} %get-tuple-element.35) | copy-start | bytes 6291460
  315.7 35.5 %copy-start.6 = (f32[592,1024]{1,0:T(8,128)}, f32[592,1024]{1,0:T(8,128)S(1)}, u32[]{:S(2)}) copy-start(f32[592,1024]{1,0:T(8,128)S(1)} %get-tuple-element.128) | copy-start | bytes 7274500
  316.1 12.0 %copy-start.12 = (bf16[592,1024]{1,0:T(8,128)(2,1)}, bf16[592,1024]{1,0:T(8,128)(2,1)S(1)}, u32[]{:S(2)}) copy-start(bf16[592,1024]{1,0:T(8,128)(2,1)S(1)} %add_convert_fusion.3.refs_6_) | copy-start | bytes 3637252
  391.1 15.4 %slice-start.2 = ((s8[8388608]{0:T(1024)(128)(4,1)}), s8[4194304]{0:T(1024)(128)(4,1)S(1)}, s32[]{:S(2)}) async-start(s8[8388608]{0:T(1024)(128)(4,1)} %bitcast.190), calls=%async_computation.2 | async-start | bytes 8388608
  392.1 14.3 %copy-start.14 = (bf16[592,1024]{1,0:T(8,128)(2,1)}, bf16[592,1024]{1,0:T(8,128)(2,1)S(1)}, u32[]{:S(2)}) copy-start(bf16[592,1024]{1,0:T(8,128)(2,1)S(1)} %convert_element_type.218.refs_3_) | copy-start | bytes 3637252
  392.1 14.3 %copy-start.25 = (f32[1,1024]{1,0:T(1,128)S(1)}, f32[1,1024]{1,0:T(1,128)}, u32[]{:S(2)}) copy-start(f32[1,1024]{1,0:T(1,128)} %copy-done.24) | copy-start | bytes 12292
  392.1 14.3 %copy-start.27 = (f32[592]{0:T(1024)S(1)}, f32[592]{0:T(1024)}, u32[]{:S(2)}) copy-start(f32[592]{0:T(1024)} %copy-done.26) | copy-start | bytes 7108
  392.2 14.3 %copy-start.29 = (f32[592]{0:T(1024)S(1)}, f32[592]{0:T(1024)}, u32[]{:S(2)}) copy-start(f32[592]{0:T(1024)} %copy-done.28) | copy-start | bytes 7108
  392.2 14.3 %slice-start.3 = ((s8[8388608]{0:T(1024)(128)(4,1)}), s8[4194304]{0:T(1024)(128)(4,1)S(1)}, s32[]{:S(2)}) async-start(s8[8388608]{0:T(1024)(128)(4,1)} %bitcast.190), calls=%async_computation.3 | async-start | bytes 8388608
  447.1 11.4 %copy-start.3 = (bf16[592,3072]{1,0:T(8,128)(2,1)}, bf16[592,3072]{1,0:T(8,128)(2,1)S(1)}, u32[]{:S(2)}) copy-start(bf16[592,3072]{1,0:T(8,128)(2,1)S(1)} %mix_heads_backward.3.refs_8_) | copy-start | bytes 10911748
  737.1 16.4 %collective-permute-start.3 = (bf16[577,512]{1,0:T(8,128)(2,1)S(1)}, bf16[577,512]{1,0:T(8,128)(2,1)S(1)}, u32[]{:S(2)}, u32[]{:S(2)}) collective-permute-start(bf16[577,512]{1,0:T(8,128)(2,1)S(1)} %bitcast.145), channel_id=1, source_target_pairs={{0,1},{1,0},{2,3},{3,2},{4,5},{5,4},{6,7},{7,6},{8,9},{9,8},{10,11... | collective-permute-start | bytes 1772552 | tf_op jit(solution)/shard_map/ppermute | solution.py:731
  738.2 27.5 %collective-permute-start.2 = (bf16[577,512]{1,0:T(8,128)(2,1)S(1)}, bf16[577,512]{1,0:T(8,128)(2,1)S(1)}, u32[]{:S(2)}, u32[]{:S(2)}) collective-permute-start(bf16[577,512]{1,0:T(8,128)(2,1)S(1)} %bitcast.144), channel_id=1, source_target_pairs={{0,1},{1,0},{2,3},{3,2},{4,5},{5,4},{6,7},{7,6},{8,9},{9,8},{10,11... | collective-permute-start | bytes 1772552 | tf_op jit(solution)/shard_map/ppermute | solution.py:731
  (40 other events, 172.6 us)

commit v4 on v3

--- a/solution.py
+++ b/solution.py
@@ -461,17 +461,109 @@
     pl.semaphore_wait(barrier, len(LINKS))
 
 
+def dot_rows(left, right):
+    return lax.dot_general(
+        left, right, (((1,), (0,)), ((), ())), preferred_element_type=jnp.float32
+    )
+
+
+def dot_cols(left, right):
+    return lax.dot_general(
+        left, right, (((1,), (1,)), ((), ())), preferred_element_type=jnp.float32
+    )
+
+
+def dot_tokens(left, right):
+    return lax.dot_general(
+        left, right, (((0,), (0,)), ((), ())), preferred_element_type=jnp.float32
+    )
+
+
+PAIR = 2 * HEAD_DIM
+
+
+def turned_softmax(keys_here, queries):
+    scores = dot_cols(keys_here, queries)
+    exponent = jnp.exp(scores - jnp.max(scores, axis=0, keepdims=True))
+    return exponent * (1.0 / jnp.sum(exponent, axis=0, keepdims=True))
+
+
+def store_rows(ref, at, pieces):
+    full = SEQ // 16 * 16
+    ref[pl.ds(full, ROWS - full), pl.ds(at, PAIR)] = jnp.zeros((ROWS - full, PAIR), LOW)
+    ref[pl.ds(0, SEQ), pl.ds(at, PAIR)] = jnp.concatenate(pieces, axis=1)
+
+
+def projected_specs(blocks):
+    def spec(offset):
+        return pl.BlockSpec((ROWS, PAIR), lambda step: (0, offset + step))
+
+    return [spec(t * 3 * blocks + part * blocks) for t in range(2) for part in range(3)]
+
+
+def heads_backward_kernel(
+    query_a, key_a, value_a, query_b, key_b, value_b, grad_a, grad_b, out_ref
+):
+    step = pl.program_id(0)
+    scale = jnp.asarray(HEAD_DIM**-0.5, LOW)
+    part_width = out_ref.shape[1] // 6
+    for t, (query_ref, key_ref, value_ref, grad_ref) in enumerate(
+        ((query_a, key_a, value_a, grad_a), (query_b, key_b, value_b, grad_b))
+    ):
+        pieces = ([], [], [])
+        for head in range(2):
+            cols = slice(head * HEAD_DIM, (head + 1) * HEAD_DIM)
+            keys_here, values_here = key_ref[:SEQ, cols], value_ref[:SEQ, cols]
+            grads = grad_ref[:SEQ, cols]
+            queries = query_ref[:SEQ, cols] * scale
+            soft = turned_softmax(keys_here, queries)
+            soft_grad = dot_cols(values_here, grads)
+            delta = jnp.sum(soft_grad * soft, axis=0, keepdims=True)
+            score_grad = (soft * (soft_grad - delta)).astype(LOW)
+            pieces[0].append((dot_tokens(score_grad, keys_here) * HEAD_DIM**-0.5).astype(LOW))
+            pieces[1].append(dot_rows(score_grad, queries).astype(LOW))
+            pieces[2].append(dot_rows(soft.astype(LOW), grads).astype(LOW))
+        for part in range(3):
+            at = pl.multiple_of((t * 3 + part) * part_width + step * PAIR, PAIR)
+            store_rows(out_ref, at, pieces[part])
+
+
+def mix_heads_backward(projected, mixed_grad):
+    width = mixed_grad.shape[1]
+    blocks = width // 2 // PAIR
+
+    def grad_spec(offset):
+        return pl.BlockSpec((ROWS, PAIR), lambda step: (0, offset + step))
+
+    return pl.pallas_call(
+        heads_backward_kernel,
+        grid=(blocks,),
+        in_specs=projected_specs(blocks) + [grad_spec(0), grad_spec(blocks)],
+        out_specs=pl.BlockSpec((ROWS, 3 * width), lambda step: (0, 0)),
+        out_shape=jax.ShapeDtypeStruct((ROWS, 3 * width), LOW),
+        compiler_params=pltpu.CompilerParams(vmem_limit_bytes=48 * 1024 * 1024),
+        cost_estimate=pl.CostEstimate(
+            flops=10 * SEQ * SEQ * width, bytes_accessed=90 * 1024 * 1024, transcendentals=0
+        ),
+        name="mix_heads_backward",
+    )(*[projected] * 6, mixed_grad, mixed_grad)
+
+
+def pick(block, at, axis):
+    return lax.dynamic_index_in_dim(block, at, axis, keepdims=False)
+
+
 def gather_parts(width):
     last = 256 if width >= 1024 else 0
     share = (width - last) // 2
-    return ((0, share), (share, share), (2 * share, last))
-
-
-def gather_stages(z, x, c, y, width):
-    (_, share), _, (last_at, last) = gather_parts(width)
-
-    def cols(t, start, size):
-        return pl.ds(pl.multiple_of(t * width + start, 128), size)
+    return share, last
+
+
+def gather_stages(z, x, c, y, whole, start, width):
+    share, last = gather_parts(width)
+
+    def cols(t, at, size):
+        return pl.ds(pl.multiple_of(t * whole + start + at, 128), size)
 
     all_rows = pl.ds(0, BLOCK)
     pair = pl.ds(lax.div(z, 2) * 2, 2)
@@ -488,7 +580,7 @@
         return cols(t, 0, 2 * share)
 
     def part_c(t):
-        return cols(t, last_at, last)
+        return cols(t, 2 * share, last)
 
     stages = [
         [("z1", (z, x, c, all_rows, part_ab(y)))],
@@ -522,219 +614,447 @@
 
 
 GATHER_COPIES = 21
-
-
-def gather_kernel(layers, kinds, *refs):
-    shard_refs = refs[:kinds]
-    count = layers * kinds
-    whole_refs = refs[kinds : kinds + count]
-    send_sem, recv_sem, local_sem = refs[kinds + count :]
-    z, x, c, y = place()
-    partners = neighbours()
-    own, plans = [], []
-    for chunk in range(count):
-        layer, kind = divmod(chunk, kinds)
-        width = shard_refs[kind].shape[2]
-        plans.append(gather_stages(z, x, c, y, width))
-        mine = pl.ds(pl.multiple_of(y * width, 128), width)
-        copy = pltpu.make_async_copy(
-            shard_refs[kind].at[layer],
-            whole_refs[chunk].at[z, x, c, pl.ds(0, BLOCK), mine],
-            local_sem.at[chunk],
-        )
-        copy.start()
-        own.append(copy)
-    greet(partners)
-    depth = len(plans[0])
-    flying = {}
-    for tick in range(count + depth):
-        for stage_idx in range(depth, -1, -1):
+GATHER_DEPTH = 5
+
+
+class Gather:
+    def __init__(self, chunks):
+        self.chunks = chunks
+
+    def scratch(self):
+        count = len(self.chunks)
+        return dict(
+            gather_send=pltpu.SemaphoreType.DMA((count, GATHER_COPIES)),
+            gather_recv=pltpu.SemaphoreType.DMA((count, GATHER_COPIES)),
+            gather_own=pltpu.SemaphoreType.DMA((count,)),
+        )
+
+    def bind(self, shards, wholes, refs):
+        self.wholes = wholes
+        self.send_sem, self.recv_sem, own_sem = refs
+        z, x, c, y = place()
+        self.partners = neighbours()
+        self.plans, self.own, self.flying = [], [], {}
+        for chunk, (matrix, start, width) in enumerate(self.chunks):
+            whole = shards[matrix].shape[1]
+            self.plans.append(gather_stages(z, x, c, y, whole, start, width))
+            mine = pl.ds(pl.multiple_of(y * whole + start, 128), width)
+            copy = pltpu.make_async_copy(
+                shards[matrix].at[:, pl.ds(start, width)],
+                wholes[matrix].at[z, x, c, pl.ds(0, BLOCK), mine],
+                own_sem.at[chunk],
+            )
+            copy.start()
+            self.own.append(copy)
+
+    def tick(self, tick):
+        done = None
+        for stage_idx in range(GATHER_DEPTH, -1, -1):
             chunk = tick - stage_idx
-            if chunk < 0 or chunk >= count:
+            if chunk < 0 or chunk >= len(self.chunks):
                 continue
             if stage_idx == 0:
-                own[chunk].wait()
-            for copy in flying.get((chunk, stage_idx - 1), ()):
+                self.own[chunk].wait()
+            for copy in self.flying.get((chunk, stage_idx - 1), ()):
                 copy.wait_recv()
-            if stage_idx == depth:
+            if stage_idx == GATHER_DEPTH:
+                done = chunk
                 continue
             started = []
-            base = sum(len(stage) for stage in plans[chunk][:stage_idx])
-            for entry, (link, index) in enumerate(plans[chunk][stage_idx]):
+            plan = self.plans[chunk]
+            base = sum(len(stage) for stage in plan[:stage_idx])
+            whole = self.wholes[self.chunks[chunk][0]]
+            for entry, (link, index) in enumerate(plan[stage_idx]):
                 copy = pltpu.make_async_remote_copy(
-                    src_ref=whole_refs[chunk].at[index],
-                    dst_ref=whole_refs[chunk].at[index],
-                    send_sem=send_sem.at[chunk, base + entry],
-                    recv_sem=recv_sem.at[chunk, base + entry],
-                    device_id=partners[link],
+                    src_ref=whole.at[index],
+                    dst_ref=whole.at[index],
+                    send_sem=self.send_sem.at[chunk, base + entry],
+                    recv_sem=self.recv_sem.at[chunk, base + entry],
+                    device_id=self.partners[link],
                     device_id_type=MESH_IDS,
                 )
                 copy.start()
                 started.append(copy)
-            flying[(chunk, stage_idx)] = started
-    for started in flying.values():
-        for copy in started:
+            self.flying[(chunk, stage_idx)] = started
+        return done
+
+    def finish(self):
+        for started in self.flying.values():
+            for copy in started:
+                copy.wait_send()
+
+
+BIAS_ROWS = 9
+SAVED = ("normed", "projected", "heads", "normed_two", "hidden", "slope", "middle", "incoming")
+
+
+class Forward:
+    def __init__(self, layers, widths):
+        self.layers, self.widths = layers, widths
+        chunks = []
+        for layer in range(layers):
+            base = layer * len(widths)
+            for kind, width in enumerate(widths):
+                split = 2 if layer == layers - 1 and kind == len(widths) - 1 else 1
+                part = width // split
+                chunks += [(base + kind, k * part, part) for k in range(split)]
+        self.gather = Gather(chunks)
+
+    def scratch(self):
+        project, out, up, down = self.widths
+        low, full = (lambda cols: pltpu.VMEM((ROWS, cols), LOW)), pltpu.VMEM((ROWS, 1024), jnp.float32)
+        sem = pltpu.SemaphoreType.DMA
+        own = dict(
+            weights_project=pltpu.VMEM((4, 2, 2, BLOCK, 2 * project), LOW),
+            weights_out=pltpu.VMEM((4, 2, 2, BLOCK, 2 * out), LOW),
+            weights_up=pltpu.VMEM((4, 2, 2, BLOCK, 2 * up), LOW),
+            weights_down=pltpu.VMEM((4, 2, 2, BLOCK, 2 * down), LOW),
+            stream=full,
+            tokens_in=low(512),
+            biases=pltpu.VMEM((2, 24, 512), jnp.float32),
+            normed=low(1024),
+            projected=low(2 * project),
+            heads=low(2 * out),
+            normed_two=low(1024),
+            hidden=low(2 * up),
+            slope=low(2 * up),
+            weight_sem=sem((self.layers * 4, 1)),
+            split_sem=sem((2, 2)),
+            saved_sem=sem((self.layers, len(SAVED))),
+            swap_send=sem((3,)),
+            swap_recv=sem((3,)),
+            bias_sem=sem((1,)),
+        )
+        return {**own, **self.gather.scratch()}
+
+    def bind(self, inputs, outputs, refs):
+        names = list(self.scratch())
+        for name, ref in zip(names, refs, strict=True):
+            setattr(self, name, ref)
+        shards, self.near, self.far, bias_ref, self.norms = (
+            inputs[:4],
+            inputs[4],
+            inputs[5],
+            inputs[6],
+            inputs[7],
+        )
+        count = self.layers * 4
+        self.wholes, outputs = outputs[:count], outputs[count:]
+        self.cotangent_in, self.activations, outputs = outputs[0], outputs[1], outputs[2:]
+        self.saved_out = [outputs[k * len(SAVED) : (k + 1) * len(SAVED)] for k in range(self.layers)]
+        self.saving, self.loading = {}, {}
+        self.y = lax.axis_index("tensor")
+        copy = pltpu.make_async_copy(bias_ref, self.biases.at[self.y], self.bias_sem.at[0])
+        copy.start()
+        self.gather.bind(
+            [shards[m % 4].at[m // 4] for m in range(count)],
+            self.wholes,
+            [getattr(self, name) for name in self.gather.scratch()],
+        )
+        copy.wait()
+
+    def swap(self):
+        partner = self.gather.partners["y"]
+        pairs = (
+            (self.biases.at[self.y], self.biases.at[self.y]),
+            (self.far.at[0], self.tokens_in),
+            (self.far.at[1], self.cotangent_in),
+        )
+        self.swaps = []
+        for entry, (source, target) in enumerate(pairs):
+            copy = pltpu.make_async_remote_copy(
+                src_ref=source,
+                dst_ref=target,
+                send_sem=self.swap_send.at[entry],
+                recv_sem=self.swap_recv.at[entry],
+                device_id=partner,
+                device_id_type=MESH_IDS,
+            )
+            copy.start()
+            self.swaps.append(copy)
+
+    def save(self, layer, name, source):
+        entry = SAVED.index(name)
+        copy = pltpu.make_async_copy(
+            source, self.saved_out[layer][entry], self.saved_sem.at[layer, entry]
+        )
+        copy.start()
+        self.saving[(layer, name)] = copy
+
+    def saved(self, layer, name):
+        if (layer, name) in self.saving:
+            self.saving.pop((layer, name)).wait()
+
+    def load(self, chunk):
+        matrix, start, width = self.gather.chunks[chunk]
+        whole = self.gather.wholes[matrix]
+        buffer = (self.weights_project, self.weights_out, self.weights_up, self.weights_down)[
+            matrix % 4
+        ]
+        copies = []
+        full = whole.shape[4] // 2
+        if width == full:
+            copies.append((whole, buffer))
+        else:
+            for t in range(2):
+                at = (slice(None),) * 4 + (pl.ds(t * full + start, width),)
+                copies.append((whole.at[at], buffer.at[at]))
+        started = self.loading.setdefault(matrix, [])
+        for entry, (source, target) in enumerate(copies):
+            half = 0 if start == 0 else 1
+            if len(copies) == 2:
+                sem = self.split_sem.at[half, entry]
+            else:
+                sem = self.weight_sem.at[matrix, 0]
+            copy = pltpu.make_async_copy(source, target, sem)
+            copy.start()
+            started.append(copy)
+
+    def wait_weights(self, matrix):
+        for copy in self.loading.pop(matrix):
+            copy.wait()
+
+    def bias_row(self, row):
+        return jnp.concatenate([self.biases[t, pl.ds(row, 1), :] for t in range(2)], axis=1)
+
+    def norm(self, target, gain_row, shift_row, bias_at):
+        gain = self.norms[pl.ds(gain_row, 1), :]
+        shift = self.norms[pl.ds(shift_row, 1), :]
+        bias = None if bias_at is None else self.bias_row(bias_at)
+
+        @pl.loop(0, ROWS // 16)
+        def _(step):
+            rows = pl.ds(pl.multiple_of(step * 16, 16), 16)
+            values = self.stream[rows, :]
+            if bias is not None:
+                values = values + bias
+                self.stream[rows, :] = values
+            mean = jnp.mean(values, axis=1, keepdims=True)
+            square = jnp.mean(values * values, axis=1, keepdims=True)
+            inverse = lax.rsqrt(square - mean * mean + norm_eps)
+            target[rows, :] = ((values - mean) * inverse * gain + shift).astype(LOW)
+
+    def begin(self):
+        for copy in self.swaps:
+            copy.wait_recv()
+        y = self.y
+        near_at = pl.ds(pl.multiple_of(y * 512, 512), 512)
+        far_at = pl.ds(pl.multiple_of((1 - y) * 512, 512), 512)
+        self.stream[:, near_at] = self.near[...].astype(jnp.float32)
+        self.stream[:, far_at] = self.tokens_in[...].astype(jnp.float32)
+
+    def project(self, layer):
+        self.saved(layer - 1, "normed")
+        self.norm(
+            self.normed,
+            layer,
+            self.layers + layer,
+            None if layer == 0 else (layer - 1) * BIAS_ROWS + 4,
+        )
+        self.save(layer, "incoming", self.stream)
+        self.save(layer, "normed", self.normed)
+        self.saved(layer - 1, "projected")
+        self.wait_weights(layer * 4)
+        parts = 6
+
+        @pl.loop(0, parts)
+        def _(part):
+            cols = pl.ds(pl.multiple_of(part * 512, 512), 512)
+            weights = self.weights_project[:, :, :, :, cols].reshape(1024, 512)
+            row = layer * BIAS_ROWS + lax.rem(part, 3)
+            bias = self.biases[lax.div(part, 3), pl.ds(row, 1), :]
+            self.projected[:, cols] = (dot_rows(self.normed[...], weights) + bias).astype(LOW)
+
+        self.save(layer, "projected", self.projected)
+
+    def mix(self, layer, first, last):
+        if first == 0:
+            self.saved(layer - 1, "heads")
+        half = self.heads.shape[1] // 2
+
+        @pl.loop(first, last)
+        def _(step):
+            for t in range(2):
+                def at(part):
+                    start = (t * 3 + part) * half + step * PAIR
+                    return pl.ds(pl.multiple_of(start, PAIR), PAIR)
+
+                queries = self.projected[pl.ds(0, SEQ), at(0)] * jnp.asarray(HEAD_DIM**-0.5, LOW)
+                keys_here = self.projected[pl.ds(0, SEQ), at(1)]
+                values_here = self.projected[pl.ds(0, SEQ), at(2)]
+                pieces = []
+                for head in range(2):
+                    cols = slice(head * HEAD_DIM, (head + 1) * HEAD_DIM)
+                    soft = turned_softmax(keys_here[:, cols], queries[:, cols])
+                    pieces.append(dot_tokens(soft.astype(LOW), values_here[:, cols]).astype(LOW))
+                store_rows(self.heads, pl.multiple_of(t * half + step * PAIR, PAIR), pieces)
+
+        if last * PAIR == half:
+            self.save(layer, "heads", self.heads)
+
+    def attend(self, layer):
+        self.wait_weights(layer * 4 + 1)
+        self.saved(layer, "incoming")
+
+        @pl.loop(0, 4)
+        def _(row):
+            cols = pl.ds(pl.multiple_of(row * 256, 256), 256)
+            weights = self.weights_out[row].reshape(256, -1)
+            self.stream[:, cols] = self.stream[:, cols] + dot_cols(self.heads[...], weights)
+
+        self.saved(layer - 1, "normed_two")
+        self.norm(
+            self.normed_two,
+            2 * self.layers + layer,
+            3 * self.layers + layer,
+            layer * BIAS_ROWS + 3,
+        )
+        self.save(layer, "normed_two", self.normed_two)
+        self.save(layer, "middle", self.stream)
+
+    def feed_up(self, layer, first, last):
+        if first == 0:
+            self.saved(layer - 1, "hidden")
+            self.saved(layer - 1, "slope")
+            self.wait_weights(layer * 4 + 2)
+
+        @pl.loop(first, last)
+        def _(part):
+            cols = pl.ds(pl.multiple_of(part * 512, 512), 512)
+            weights = self.weights_up[:, :, :, :, cols].reshape(1024, 512)
+            row = layer * BIAS_ROWS + 5 + lax.rem(part, 4)
+            bias = self.biases[lax.div(part, 4), pl.ds(row, 1), :]
+            before = dot_rows(self.normed_two[...], weights) + bias
+            normal = 0.5 * (1.0 + lax.erf(before * 0.7071067811865476))
+            self.hidden[:, cols] = (before * normal).astype(LOW)
+            density = jnp.exp(-0.5 * before * before) * 0.3989422804014327
+            self.slope[:, cols] = (normal + before * density).astype(LOW)
+
+        if last * 512 == self.hidden.shape[1]:
+            self.save(layer, "hidden", self.hidden)
+            self.save(layer, "slope", self.slope)
+
+    def feed_down(self, layer, first, last):
+        if first == 0:
+            self.saved(layer, "middle")
+            self.wait_weights(layer * 4 + 3)
+
+        @pl.loop(first, last)
+        def _(row):
+            cols = pl.ds(pl.multiple_of(row * 256, 256), 256)
+            weights = self.weights_down[row].reshape(256, -1)
+            self.stream[:, cols] = self.stream[:, cols] + dot_cols(self.hidden[...], weights)
+
+    def end(self):
+        bias = self.bias_row((self.layers - 1) * BIAS_ROWS + 4)
+
+        @pl.loop(0, ROWS // 16)
+        def _(step):
+            rows = pl.ds(pl.multiple_of(step * 16, 16), 16)
+            self.activations[rows, :] = (self.stream[rows, :] + bias).astype(LOW)
+
+    def work(self):
+        steps = [(0, 1, self.begin)]
+        for layer in range(self.layers):
+            base = layer * 4
+            steps += [
+                (base, 6, lambda layer=layer: self.project(layer)),
+                (base, 7, lambda layer=layer: self.mix(layer, 0, 2)),
+                (base, 7, lambda layer=layer: self.mix(layer, 2, 4)),
+                (base + 1, 4, lambda layer=layer: self.attend(layer)),
+                (base + 2, 6, lambda layer=layer: self.feed_up(layer, 0, 4)),
+                (base + 2, 6, lambda layer=layer: self.feed_up(layer, 4, 8)),
+                (base + 3, 4, lambda layer=layer: self.feed_down(layer, 0, 2)),
+                (base + 3, 4, lambda layer=layer: self.feed_down(layer, 2, 4)),
+            ]
+        return steps + [(self.layers * 4 - 1, 1, self.end)]
+
+    def run(self):
+        greet(self.gather.partners)
+        self.swap()
+        steps = self.work()
+        ready = set()
+        remaining = {}
+        for matrix, _, _ in self.gather.chunks:
+            remaining[matrix] = remaining.get(matrix, 0) + 1
+        ticks = len(self.gather.chunks) + GATHER_DEPTH
+        for tick in range(ticks):
+            budget = WORK_A_TICK
+            done = self.gather.tick(tick)
+            while steps and steps[0][0] in ready and budget > 0:
+                _, cost, step = steps.pop(0)
+                budget -= cost
+                step()
+            if done is not None:
+                self.free_buffer(done, steps)
+                matrix = self.gather.chunks[done][0]
+                self.load(done)
+                remaining[matrix] -= 1
+                if remaining[matrix] == 0:
+                    ready.add(matrix)
+        for _, _, step in steps:
+            step()
+        self.gather.finish()
+        for copy in self.swaps:
             copy.wait_send()
-
-
-def gather_weights(shards):
-    layers, kinds = shards[0].shape[0], len(shards)
-    count = layers * kinds
-    whole = pl.pallas_call(
-        lambda *refs: gather_kernel(layers, kinds, *refs),
-        out_shape=[
-            jax.ShapeDtypeStruct((4, 2, 2, BLOCK, 2 * shards[chunk % kinds].shape[2]), LOW)
-            for chunk in range(count)
-        ],
-        in_specs=[pl.BlockSpec(memory_space=pl.ANY)] * kinds,
-        out_specs=[pl.BlockSpec(memory_space=pl.ANY)] * count,
-        scratch_shapes=[
-            pltpu.SemaphoreType.DMA((count, GATHER_COPIES)),
-            pltpu.SemaphoreType.DMA((count, GATHER_COPIES)),
-            pltpu.SemaphoreType.DMA((count,)),
-        ],
-        compiler_params=pltpu.CompilerParams(collective_id=0, has_side_effects=True),
+        for copy in self.saving.values():
+            copy.wait()
+
+    def free_buffer(self, chunk, steps):
+        matrix = self.gather.chunks[chunk][0]
+        while steps and any(entry[0] == matrix - 4 for entry in steps):
+            steps.pop(0)[2]()
+
+
+WORK_A_TICK = 12
+
+
+def forward(shards, near, far, biases, norms):
+    layers = shards[0].shape[0]
+    widths = [shard.shape[2] for shard in shards]
+    plan = Forward(layers, widths)
+    project, out, up, down = widths
+    low = lambda cols: jax.ShapeDtypeStruct((ROWS, cols), LOW)
+    full = jax.ShapeDtypeStruct((ROWS, 1024), jnp.float32)
+    saved = [
+        low(1024), low(2 * project), low(2 * out), low(1024), low(2 * up), low(2 * up), full, full
+    ]
+    wholes = [
+        jax.ShapeDtypeStruct((4, 2, 2, BLOCK, 2 * width), LOW) for width in widths
+    ] * layers
+    outs = [*wholes, low(512), low(1024), *(saved * layers)]
+    any_spec, vmem_spec = pl.BlockSpec(memory_space=pl.ANY), pl.BlockSpec(memory_space=pltpu.VMEM)
+    out_specs = [any_spec] * len(outs)
+    out_specs[len(wholes) + 1] = vmem_spec
+
+    def kernel(*refs):
+        outputs = refs[8 : 8 + len(outs)]
+        plan.bind(refs[:8], outputs, refs[8 + len(outs) :])
+        plan.run()
+
+    results = pl.pallas_call(
+        kernel,
+        out_shape=outs,
+        in_specs=[any_spec] * 4 + [vmem_spec, any_spec, any_spec, vmem_spec],
+        out_specs=out_specs,
+        scratch_shapes=list(plan.scratch().values()),
+        compiler_params=pltpu.CompilerParams(
+            collective_id=0, has_side_effects=True, vmem_limit_bytes=60 * 1024 * 1024
+        ),
         cost_estimate=pl.CostEstimate(
-            flops=0, bytes_accessed=600 * 1024 * 1024, transcendentals=0
+            flops=60 * 1024**3, bytes_accessed=700 * 1024 * 1024, transcendentals=0
         ),
-        name="gather_weights",
-    )(*shards)
-    return [
-        [whole[layer * kinds + kind].reshape(1024, -1) for kind in range(kinds)]
-        for layer in range(layers)
+        name="forward",
+    )(*shards, near, far, biases, norms)
+    whole, results = results[: len(wholes)], results[len(wholes) :]
+    weights = [
+        [whole[layer * 4 + kind].reshape(1024, -1) for kind in range(4)] for layer in range(layers)
     ]
-
-
-def dot_rows(left, right):
-    return lax.dot_general(
-        left, right, (((1,), (0,)), ((), ())), preferred_element_type=jnp.float32
-    )
-
-
-def dot_cols(left, right):
-    return lax.dot_general(
-        left, right, (((1,), (1,)), ((), ())), preferred_element_type=jnp.float32
-    )
-
-
-def dot_tokens(left, right):
-    return lax.dot_general(
-        left, right, (((0,), (0,)), ((), ())), preferred_element_type=jnp.float32
-    )
-
-
-PAIR = 2 * HEAD_DIM
-
-
-def turned_softmax(keys_here, queries):
-    scores = dot_cols(keys_here, queries)
-    exponent = jnp.exp(scores - jnp.max(scores, axis=0, keepdims=True))
-    return exponent * (1.0 / jnp.sum(exponent, axis=0, keepdims=True))
-
-
-def store_rows(ref, at, pieces):
-    full = SEQ // 16 * 16
-    ref[pl.ds(full, ROWS - full), pl.ds(at, PAIR)] = jnp.zeros((ROWS - full, PAIR), LOW)
-    ref[pl.ds(0, SEQ), pl.ds(at, PAIR)] = jnp.concatenate(pieces, axis=1)
-
-
-def heads_kernel(query_a, key_a, value_a, query_b, key_b, value_b, mixed_ref):
-    step = pl.program_id(0)
-    scale = jnp.asarray(HEAD_DIM**-0.5, LOW)
-    half_width = mixed_ref.shape[1] // 2
-    for t, (query_ref, key_ref, value_ref) in enumerate(
-        ((query_a, key_a, value_a), (query_b, key_b, value_b))
-    ):
-        pieces = []
-        for head in range(2):
-            cols = slice(head * HEAD_DIM, (head + 1) * HEAD_DIM)
-            soft = turned_softmax(key_ref[:SEQ, cols], query_ref[:SEQ, cols] * scale)
-            pieces.append(dot_tokens(soft.astype(LOW), value_ref[:SEQ, cols]).astype(LOW))
-        at = pl.multiple_of(t * half_width + step * PAIR, PAIR)
-        store_rows(mixed_ref, at, pieces)
-
-
-def projected_specs(blocks):
-    def spec(offset):
-        return pl.BlockSpec((ROWS, PAIR), lambda step: (0, offset + step))
-
-    return [spec(t * 3 * blocks + part * blocks) for t in range(2) for part in range(3)]
-
-
-def mix_heads(projected):
-    width = projected.shape[1] // 3
-    blocks = width // 2 // PAIR
-    return pl.pallas_call(
-        heads_kernel,
-        grid=(blocks,),
-        in_specs=projected_specs(blocks),
-        out_specs=pl.BlockSpec((ROWS, width), lambda step: (0, 0)),
-        out_shape=jax.ShapeDtypeStruct((ROWS, width), LOW),
-        compiler_params=pltpu.CompilerParams(vmem_limit_bytes=40 * 1024 * 1024),
-        cost_estimate=pl.CostEstimate(
-            flops=4 * SEQ * SEQ * width, bytes_accessed=45 * 1024 * 1024, transcendentals=0
-        ),
-        name="mix_heads",
-    )(*[projected] * 6)
-
-
-def heads_backward_kernel(
-    query_a, key_a, value_a, query_b, key_b, value_b, grad_a, grad_b, out_ref
-):
-    step = pl.program_id(0)
-    scale = jnp.asarray(HEAD_DIM**-0.5, LOW)
-    part_width = out_ref.shape[1] // 6
-    for t, (query_ref, key_ref, value_ref, grad_ref) in enumerate(
-        ((query_a, key_a, value_a, grad_a), (query_b, key_b, value_b, grad_b))
-    ):
-        pieces = ([], [], [])
-        for head in range(2):
-            cols = slice(head * HEAD_DIM, (head + 1) * HEAD_DIM)
-            keys_here, values_here = key_ref[:SEQ, cols], value_ref[:SEQ, cols]
-            grads = grad_ref[:SEQ, cols]
-            queries = query_ref[:SEQ, cols] * scale
-            soft = turned_softmax(keys_here, queries)
-            soft_grad = dot_cols(values_here, grads)
-            delta = jnp.sum(soft_grad * soft, axis=0, keepdims=True)
-            score_grad = (soft * (soft_grad - delta)).astype(LOW)
-            pieces[0].append((dot_tokens(score_grad, keys_here) * HEAD_DIM**-0.5).astype(LOW))
-            pieces[1].append(dot_rows(score_grad, queries).astype(LOW))
-            pieces[2].append(dot_rows(soft.astype(LOW), grads).astype(LOW))
-        for part in range(3):
-            at = pl.multiple_of((t * 3 + part) * part_width + step * PAIR, PAIR)
-            store_rows(out_ref, at, pieces[part])
-
-
-def mix_heads_backward(projected, mixed_grad):
-    width = mixed_grad.shape[1]
-    blocks = width // 2 // PAIR
-
-    def grad_spec(offset):
-        return pl.BlockSpec((ROWS, PAIR), lambda step: (0, offset + step))
-
-    return pl.pallas_call(
-        heads_backward_kernel,
-        grid=(blocks,),
-        in_specs=projected_specs(blocks) + [grad_spec(0), grad_spec(blocks)],
-        out_specs=pl.BlockSpec((ROWS, 3 * width), lambda step: (0, 0)),
-        out_shape=jax.ShapeDtypeStruct((ROWS, 3 * width), LOW),
-        compiler_params=pltpu.CompilerParams(vmem_limit_bytes=48 * 1024 * 1024),
-        cost_estimate=pl.CostEstimate(
-            flops=10 * SEQ * SEQ * width, bytes_accessed=90 * 1024 * 1024, transcendentals=0
-        ),
-        name="mix_heads_backward",
-    )(*[projected] * 6, mixed_grad, mixed_grad)
-
-
-def swap_link(block, link):
-    if link == "y":
-        return lax.ppermute(block, "tensor", [(0, 1), (1, 0)])
-    flip = {"core": 1, "x": 2, "z1": 4, "z2": 8}[link]
-    return lax.ppermute(block, "wide", [(i, i ^ flip) for i in range(16)])
-
-
-def pick(block, at, axis):
-    return lax.dynamic_index_in_dim(block, at, axis, keepdims=False)
+    cotangent_in, activations, results = results[0], results[1], results[2:]
+    kept = [
+        dict(zip(SAVED, results[k * len(SAVED) : (k + 1) * len(SAVED)])) for k in range(layers)
+    ]
+    return weights, cotangent_in, activations, kept
 
 
 COLS = 256
@@ -932,15 +1252,24 @@
 def settle_kernel(plan, kinds, layers, *refs):
     matrices = kinds * layers
     lefts, rights = refs[:matrices], refs[matrices : 2 * matrices]
-    small_ref = refs[2 * matrices]
-    refs = refs[2 * matrices + 1 :]
-    outs, total_ref, refs = refs[:kinds], refs[kinds], refs[kinds + 1 :]
-    sums, sums_in, sums_send, sums_recv = refs[:4]
+    small_ref, leaving_ref = refs[2 * matrices : 2 * matrices + 2]
+    refs = refs[2 * matrices + 2 :]
+    outs, total_ref, arriving_ref, refs = refs[:kinds], refs[kinds], refs[kinds + 1], refs[kinds + 2 :]
+    sums, sums_in, sums_send, sums_recv, swap_send, swap_recv = refs[:6]
     plan.bind(
-        lefts, rights, [(outs[m % kinds], m // kinds) for m in range(matrices)], refs[4:]
+        lefts, rights, [(outs[m % kinds], m // kinds) for m in range(matrices)], refs[6:]
     )
     plan.load(0)
     greet(plan.partners)
+    swap = pltpu.make_async_remote_copy(
+        src_ref=leaving_ref,
+        dst_ref=arriving_ref,
+        send_sem=swap_send.at[0],
+        recv_sem=swap_recv.at[0],
+        device_id=plan.partners["y"],
+        device_id_type=MESH_IDS,
+    )
+    swap.start()
     sums[0] = small_ref[...]
     flying = None
     for pair in range(len(plan.pairs) + SETTLE_DEPTH):
@@ -960,6 +1289,7 @@
             flying.start()
         plan.tick(pair)
     total_ref[...] = sums[len(TOTAL_LINKS)]
+    swap.wait()
 
 
 def layer_pairs(base, widths):
@@ -969,7 +1299,7 @@
     return feed + [(rest[k], rest[k + 1]) for k in range(0, len(rest), 2)]
 
 
-def settle_all(layer_terms, small):
+def settle_all(layer_terms, small, leaving):
     layers, kinds = len(layer_terms), len(layer_terms[0])
     widths = [right.shape[1] // 2 for _, right in layer_terms[0]]
     pairs = []
@@ -983,14 +1313,19 @@
     return pl.pallas_call(
         lambda *refs: settle_kernel(plan, kinds, layers, *refs),
         out_shape=[jax.ShapeDtypeStruct((layers, 2, BLOCK, width // 2), jnp.float32) for width in widths]
-        + [jax.ShapeDtypeStruct(small.shape, jnp.float32)],
-        in_specs=[any_spec] * (2 * kinds * layers) + [vmem_spec],
-        out_specs=[vmem_spec] * (kinds + 1),
+        + [
+            jax.ShapeDtypeStruct(small.shape, jnp.float32),
+            jax.ShapeDtypeStruct(leaving.shape, leaving.dtype),
+        ],
+        in_specs=[any_spec] * (2 * kinds * layers) + [vmem_spec, any_spec],
+        out_specs=[vmem_spec] * (kinds + 1) + [any_spec],
         scratch_shapes=[
             pltpu.VMEM((steps + 1, *small.shape), jnp.float32),
             pltpu.VMEM((steps, *small.shape), jnp.float32),
             pltpu.SemaphoreType.DMA((steps,)),
             pltpu.SemaphoreType.DMA((steps,)),
+            pltpu.SemaphoreType.DMA((1,)),
+            pltpu.SemaphoreType.DMA((1,)),
             *plan.scratch().values(),
         ],
         compiler_params=pltpu.CompilerParams(
@@ -1000,7 +1335,7 @@
             flops=24 * 4 * 1024 * 1024 * ROWS, bytes_accessed=700 * 1024 * 1024, transcendentals=0
         ),
         name="settle_all",
-    )(*lefts, *rights, small)
+    )(*lefts, *rights, small, leaving)
 
 
 def in_order(own, other, index, axis):
@@ -1009,12 +1344,11 @@
     return jnp.concatenate((first, second), axis=axis)
 
 
-def whole_norm(stream, gain, shift):
+def centre(stream):
     row_mean = jnp.mean(stream, axis=1, keepdims=True)
     square_mean = jnp.mean(stream * stream, axis=1, keepdims=True)
     inverse_std = lax.rsqrt(square_mean - row_mean * row_mean + norm_eps)
-    centred = (stream - row_mean) * inverse_std
-    return (centred * gain + shift).astype(LOW), centred, inverse_std
+    return (stream - row_mean) * inverse_std, inverse_std
 
 
 def whole_norm_backward(upstream, centred, inverse_std, gain):
@@ -1051,84 +1385,48 @@
     y = lax.axis_index("tensor")
     far = 1 - y
 
-    whole = gather_weights(
+    def own_rows(block, image):
+        rows = lax.dynamic_slice_in_dim(block, image * SEQ, SEQ)
+        return jnp.pad(rows, ((0, ROWS - SEQ), (0, 0)))
+
+    biases = jnp.concatenate(
+        (query_bias, jnp.zeros_like(query_bias), value_bias, out_bias, down_bias, up_bias), axis=1
+    )
+    biases = biases.astype(jnp.float32).reshape(layers * BIAS_ROWS, -1)
+    biases = jnp.pad(biases, ((0, 24 - layers * BIAS_ROWS), (0, 0)))
+    norms = jnp.concatenate((first_gain, first_shift, second_gain, second_shift))
+    weights, cotangent_in, activations, kept = forward(
         (
             jnp.concatenate((query_weight, key_weight, value_weight), axis=2),
             jnp.swapaxes(out_weight, 1, 2),
             up_weight,
             jnp.swapaxes(down_weight, 1, 2),
-        )
-    )
-
-    tokens = jnp.stack((images.reshape(2, SEQ, half), cotangent.reshape(2, SEQ, half)))
-    near_tokens = pick(tokens, y, 1)
-    far_tokens = swap_link(pick(tokens, far, 1), "y")
-    tokens = in_order(near_tokens, far_tokens, y, 2)
-    tokens = jnp.pad(tokens, ((0, 0), (0, ROWS - SEQ), (0, 0)))
-    biases = jnp.concatenate(
-        (query_bias, jnp.zeros_like(query_bias), value_bias, out_bias, down_bias, up_bias), axis=1
-    )
-    both = in_order(biases[None], swap_link(biases, "y")[None], y, 0)
-
-    def whole_bias(start, size, layer):
-        return both[:, layer, start : start + size].reshape(1, -1).astype(jnp.float32)
+        ),
+        own_rows(images, y),
+        jnp.stack((own_rows(images, far), own_rows(cotangent, far))),
+        biases,
+        norms.astype(jnp.float32),
+    )
 
     def row(table, layer):
         return table[layer][None].astype(jnp.float32)
 
-    stream = tokens[0].astype(jnp.float32)
-    saved = []
-    for layer in range(layers):
-        project_w, out_w, up_w, down_w = whole[layer]
-        normed, centred, inverse = whole_norm(
-            stream, row(first_gain, layer), row(first_shift, layer)
-        )
-        projected = (dot_rows(normed, project_w) + whole_bias(0, 3 * half, layer)).astype(LOW)
-        heads = mix_heads(projected)
-        middle = stream + dot_cols(heads, out_w) + whole_bias(3 * half, half, layer)
-        normed_two, centred_two, inverse_two = whole_norm(
-            middle, row(second_gain, layer), row(second_shift, layer)
-        )
-        before = dot_rows(normed_two, up_w) + whole_bias(5 * half, hidden_width // 2, layer)
-        hidden = (before * (0.5 * (1.0 + lax.erf(before * 0.7071067811865476)))).astype(LOW)
-        saved.append(
-            (
-                normed,
-                centred,
-                inverse,
-                projected,
-                heads,
-                normed_two,
-                centred_two,
-                inverse_two,
-                before,
-                hidden,
-            )
-        )
-        stream = middle + dot_cols(hidden, down_w) + whole_bias(4 * half, half, layer)
-    activations = stream.astype(LOW)
-
-    upstream = tokens[1].astype(jnp.float32)
+    upstream = in_order(own_rows(cotangent, y), cotangent_in, y, 1).astype(jnp.float32)
     small = [None] * layers
     terms = [None] * layers
     for layer in reversed(range(layers)):
-        project_w, out_w, up_w, down_w = whole[layer]
-        (
-            normed,
-            centred,
-            inverse,
-            projected,
-            heads,
-            normed_two,
-            centred_two,
-            inverse_two,
-            before,
-            hidden,
-        ) = saved[layer]
+        project_w, out_w, up_w, down_w = weights[layer]
+        values = kept[layer]
+        normed, projected, heads = values["normed"], values["projected"], values["heads"]
+        normed_two, hidden = values["normed_two"], values["hidden"]
+        centred_two, inverse_two = centre(values["middle"])
+        centred, inverse = centre(values["incoming"])
         down_bias_sum = jnp.sum(upstream, axis=0)
         upstream_low = upstream.astype(LOW)
         down_term = (upstream_low, hidden)
-        hidden_grad = (dot_rows(upstream_low, down_w) * gelu_slope(before)).astype(LOW)
+        hidden_grad = (dot_rows(upstream_low, down_w) * values["slope"].astype(jnp.float32)).astype(
+            LOW
+        )
         up_bias_sum = jnp.sum(hidden_grad.astype(jnp.float32), axis=0)
         up_term = (normed_two, hidden_grad)
         normed_two_grad = dot_cols(hidden_grad, up_w)
@@ -1166,8 +1464,13 @@
         terms[layer] = (project_term, out_term, up_term, down_term)
 
     width = 2 * half
-    project_out, out_out, up_out, down_out, totals = settle_all(
-        terms, jnp.stack(small).reshape(-1, width)
+
+    def columns(rows, t):
+        return lax.dynamic_slice_in_dim(rows, t * half, half, axis=1)
+
+    leaving = jnp.stack((columns(activations, far), columns(upstream, far).astype(LOW)))
+    project_out, out_out, up_out, down_out, totals, arriving = settle_all(
+        terms, jnp.stack(small).reshape(-1, width), leaving
     )
     totals = totals.reshape(layers, -1)
     project_out, out_out, up_out, down_out = [
@@ -1178,15 +1481,12 @@
     for size in (width, width, width, hidden_width, width, width, width, width, width):
         small_outs.append(totals[:, at : at + size])
         at += size
-    def to_owner(rows):
-        parts = rows[:SEQ].reshape(SEQ, 2, half)
-        near = pick(parts, y, 1)
-        moved = swap_link(pick(parts, far, 1).astype(LOW), "y")
-        return in_order(near, moved.astype(near.dtype), y, 0)
+    def to_owner(rows, arrived):
+        return in_order(columns(rows, y)[:SEQ], arrived[:SEQ].astype(rows.dtype), y, 0)
 
     return (
-        to_owner(activations),
-        to_owner(upstream),
+        to_owner(activations, arriving[0]),
+        to_owner(upstream, arriving[1]),
         project_out[:, :, :half],
         project_out[:, :, half : 2 * half],
         project_out[:, :, 2 * half :],

time: 773 us -> 680 us (0.88)
  matrix products: 118 us -> 50.4 us
  Pallas kernels: 559 us -> 588 us
  local copies, waits for them, and re-layouts: 40.3 us -> 14.4 us
  waiting for transfers between devices: 21.8 us -> 0 us
    dot_general x8 -> x4, matrix products: 60 us -> 23.5 us  [dot_rows(): lax.dot_general(left, right, (((1,), (0,)), ((), ())), preferred_element_...]
    dot_general x8 -> x4, matrix products: 57.8 us -> 26.9 us  [dot_cols(): lax.dot_general(left, right, (((1,), (1,)), ((), ())), preferred_element_...]
    ppermute x4 -> x0, waiting for transfers between devices: 21.8 us -> none  [swap_link(): return lax.ppermute(block, 'tensor', [(0, 1), (1, 0)])]
    pallas_call x1, Pallas kernels: 239 us -> 257 us  [settle_all(): pl.pallas_call(lambda *refs: settle_kernel(plan, kinds, layers, *refs), o...]
    pallas_call x3 -> x1, Pallas kernels: 263 us -> 274 us  [forward(): pl.pallas_call(kernel, out_shape=outs, in_specs=[any_spec] * 4 + [vmem_sp...]
    reshape x2 -> x0, local copies, waits for them, and re-layouts: 8.13 us -> none  [to_owner(): parts = rows[:SEQ].reshape(SEQ, 2, half)]
  transfers between devices with their start and end apart: 4 -> 0, of which waited for: 2 -> 0; matrix products, arithmetic and copies ran while one was open for 1% -> 0% of each run, Pallas kernels for 31% -> 0%
where the time goes in v4:
time: 680 us; the launch traced here: 677 us
  Pallas kernels  588 us (86%)
  matrix products  50.4 us (7%)
  other arithmetic  23 us (3%)
  local copies, waits for them, and re-layouts  14.4 us (2%)
    pallas_call x1, Pallas kernels, forward(): pl.pallas_call(kernel, out_shape=outs, in_specs=[any_spec] * 4 + [vmem_sp...  274 us
    pallas_call x1, Pallas kernels, settle_all(): pl.pallas_call(lambda *refs: settle_kernel(plan, kinds, layers, *refs), o...  257 us
    pallas_call x2, Pallas kernels, mix_heads_backward(): pl.pallas_call(heads_backward_kernel, grid=(blocks,), in_specs=projected_...  56.3 us
    dot_general x4, matrix products, dot_cols(): lax.dot_general(left, right, (((1,), (1,)), ((), ())), preferred_element_...  26.9 us
    dot_general x4, matrix products, dot_rows(): lax.dot_general(left, right, (((1,), (0,)), ((), ())), preferred_element_...  23.5 us

profile of v4, /device:TPU:0, one launch (start us, length us, event | category | flops | bytes accessed | tf_op | source)
XLA Modules:
  0.0 677.4 jit_solution(16442527829613812728)
XLA Ops:
  0.7 2.2 constant_dynamic-slice_fusion
  7.3 274.5 %forward.1 = (bf16[4,2,2,64,3072]{4,3,2,1,0:T(8,128)(2,1)}, bf16[4,2,2,64,1024]{4,3,2,1,0:T(8,128)(2,1)}, bf16[4,2,2,64,4096]{4,3,2,1,0:T(8,128)(2,1)}, bf16[4,2...) custom-call(bf16[2,64,1536]{2,1,0:T(8,128)(2,1)} %pad_maximum_fusion, ...), custom_call_target="tpu_custom_call" | custom-call | flops 64424509440 | bytes 734003200 | tf_op jit(solution)/shard_map/forward/pallas_call | solution.py:1035
  281.8 1.3 broadcast_select_fusion.1
  283.1 10.1 %convert_reduce_fusion = (f32[4096]{0:T(1024)S(1)}, bf16[592,4096]{1,0:T(8,128)(2,1)S(1)}) fusion(bf16[592,4096]{1,0:T(8,128)(2,1)} %get-tuple-element.54, bf16[1024,4096]{1,0:T(8,128)(2,1)} %bitcast.97, bf16[592,512]{1,0:T(8,128)(2,1)S(1)} %get-tuple-element.117, bf16[592,512]{1,0:T(8,128)(2,1)S(1)} %get-tuple-element.116), kind=kOutput, calls=%fused_computation | convolution fusion | flops 4980600832 | bytes 19316736 | tf_op jit(solution)/shard_map/dot_general | solution.py:465
  293.6 5.7 multiply_reduce_fusion.1
  299.4 1.3 fusion.4
  300.9 1.8 copy-done.29
  302.7 1.4 convolution_convert_fusion.1.grad_a.grad_b
  304.1 28.2 %mix_heads_backward.2.refs_12_ = bf16[592,3072]{1,0:T(8,128)(2,1)S(1)} custom-call(bf16[592,3072]{1,0:T(8,128)(2,1)} %get-tuple-element.57.query_a.key_a.value_a.query_b.key_b.value_b, bf16[592,3072]{1,0:T(8,128)(2,1)} %get-tuple-element.57.query_a.key_a.value_a.query_b.key_b.value_b, ...), custom_call_target="tpu_custom_call" | custom-call | flops 3409192960 | bytes 94371840 | tf_op jit(solution)/shard_map/mix_heads_backward/pallas_call | solution.py:538
  332.7 7.7 %multiply_reduce_fusion.2 = (f32[1024]{0:T(1024)S(1)}, f32[592]{0:T(1024)S(1)}, f32[592]{0:T(1024)S(1)}, f32[1024]{0:T(1024)S(1)}, f32[592,1024]{1,0:T(8,128)S(1)}) fusion(f32[592,1024]{1,0:T(8,128)S(1)} %copy-done.6, f32[592]{0:T(1024)S(1)} %get-tuple-element.146, f32[592]{0:T(1024)S(1)} %get-tuple-element.145, f32[1024]{0:T(1024)S(1)} %bitcast.82, ...), kind=kOutput, calls=%fused_computation.11 | convolution fusion | flops 3729994752 | bytes 14800128 | tf_op jit(solution)/shard_map/dot_general | solution.py:471
  341.6 10.5 %convert_reduce_fusion.1 = (f32[4096]{0:T(1024)S(1)}, bf16[592,4096]{1,0:T(8,128)(2,1)S(1)}) fusion(bf16[592,4096]{1,0:T(8,128)(2,1)} %get-tuple-element.62, bf16[592,1024]{1,0:T(8,128)(2,1)S(1)} %convert_element_type.78.refs_3_, bf16[1024,4096]{1,0:T(8,128)(2,1)} %bitcast.93), kind=kOutput, calls=%fused_computation.1 | convolution fusion | flops 4978176000 | bytes 19316736 | tf_op jit(solution)/shard_map/dot_general | solution.py:465
  352.5 5.7 multiply_reduce_fusion.3
  359.3 1.8 copy-done.28
  361.1 1.4 convolution_convert_fusion.grad_a.grad_b
  362.6 28.1 %mix_heads_backward.3.refs_8_ = bf16[592,3072]{1,0:T(8,128)(2,1)S(1)} custom-call(bf16[592,3072]{1,0:T(8,128)(2,1)} %get-tuple-element.67.query_a.key_a.value_a.query_b.key_b.value_b, bf16[592,3072]{1,0:T(8,128)(2,1)} %get-tuple-element.67.query_a.key_a.value_a.query_b.key_b.value_b, ...), custom_call_target="tpu_custom_call" | custom-call | flops 3409192960 | bytes 94371840 | tf_op jit(solution)/shard_map/mix_heads_backward/pallas_call | solution.py:538
  391.2 7.8 %multiply_reduce_fusion = (f32[592]{0:T(1024)S(1)}, f32[1024]{0:T(1024)S(1)}, f32[592]{0:T(1024)S(1)}, f32[1024]{0:T(1024)S(1)}, f32[592,1024]{1,0:T(8,128)S(1)}) fusion(f32[592,1024]{1,0:T(8,128)S(1)} %copy-done.4, f32[1024]{0:T(1024)S(1)} %bitcast.78, f32[592]{0:T(1024)S(1)} %get-tuple-element.138, f32[592]{0:T(1024)S(1)} %get-tuple-element.137, ...), kind=kOutput, calls=%fused_computation.9 | convolution fusion | flops 3729994752 | bytes 14800128 | tf_op jit(solution)/shard_map/dot_general | solution.py:471
  400.0 1.3 dynamic-slice_bitcast_fusion
  403.3 2.8 convert_reduce_fusion.2
  407.0 2.2 pad_maximum_fusion.2.refs_7_
  409.2 256.9 %settle_all.1 = (f32[2,2,64,768]{3,2,1,0:T(8,128)}, f32[2,2,64,256]{3,2,1,0:T(8,128)}, f32[2,2,64,1024]{3,2,1,0:T(8,128)}, f32[2,2,64,1024]{3,2,1,0:T(8,128)}, f...) custom-call(bf16[592,1024]{1,0:T(8,128)(2,1)} %get-tuple-element.50.refs_0_, bf16[592,1024]{1,0:T(8,128)(2,1)} %copy-done.10, ...), custom_call_target="tpu_custom_call" | custom-call | flops 59592671232 | bytes 734003200 | tf_op jit(solution)/shard_map/settle_all/pallas_call | solution.py:1313
  666.1 1.4 convert_select_fusion.1
  667.5 1.7 pad_maximum_fusion
  669.2 1.5 bitcast_select_fusion.1
  670.7 1.2 pad_maximum_fusion.4
  (145 shorter events, 17.0 us)
Async XLA Ops:
  3.0 2.9 copy-start.26
  3.0 2.9 copy-start.27
  3.0 2.9 copy-start.21
  3.0 3.6 copy-start.19
  3.1 3.6 copy-start.20
  3.1 3.6 copy-start.22
  3.1 3.6 copy-start.23
  283.1 16.3 %copy-start.7 = (bf16[592,512]{1,0:T(8,128)(2,1)}, bf16[592,512]{1,0:T(8,128)(2,1)S(1)}, u32[]{:S(2)}) copy-start(bf16[592,512]{1,0:T(8,128)(2,1)S(1)} %get-tuple-element.117) | copy-start | bytes 1818628
  283.1 10.5 %slice-start.2 = ((s8[8388608]{0:T(1024)(128)(4,1)}), s8[4194304]{0:T(1024)(128)(4,1)S(1)}, s32[]{:S(2)}) async-start(s8[8388608]{0:T(1024)(128)(4,1)} %bitcast.94), calls=%async_computation.2 | async-start | bytes 8388608
  283.1 10.2 %copy-start.3 = (f32[592,1024]{1,0:T(8,128)S(1)}, f32[592,1024]{1,0:T(8,128)}, u32[]{:S(2)}) copy-start(f32[592,1024]{1,0:T(8,128)} %get-tuple-element.52) | copy-start | bytes 7274500
  283.1 10.5 %slice-start.3 = ((s8[8388608]{0:T(1024)(128)(4,1)}), s8[4194304]{0:T(1024)(128)(4,1)S(1)}, s32[]{:S(2)}) async-start(s8[8388608]{0:T(1024)(128)(4,1)} %bitcast.94), calls=%async_computation.3 | async-start | bytes 8388608
  293.2 6.1 copy-start.31
  300.9 3.3 copy-start.8
  304.1 28.2 %copy-start.6 = (f32[592,1024]{1,0:T(8,128)S(1)}, f32[592,1024]{1,0:T(8,128)}, u32[]{:S(2)}) copy-start(f32[592,1024]{1,0:T(8,128)} %get-tuple-element.56) | copy-start | bytes 7274500
  332.3 8.1 %copy-start = (bf16[592,3072]{1,0:T(8,128)(2,1)}, bf16[592,3072]{1,0:T(8,128)(2,1)S(1)}, u32[]{:S(2)}) copy-start(bf16[592,3072]{1,0:T(8,128)(2,1)S(1)} %mix_heads_backward.2.refs_12_) | copy-start | bytes 10911748
  341.5 10.6 %copy-start.9 = (bf16[592,1024]{1,0:T(8,128)(2,1)}, bf16[592,1024]{1,0:T(8,128)(2,1)S(1)}, u32[]{:S(2)}) copy-start(bf16[592,1024]{1,0:T(8,128)(2,1)S(1)} %convert_element_type.78.refs_3_) | copy-start | bytes 3637252
  341.5 11.0 %slice-start = ((s8[8388608]{0:T(1024)(128)(4,1)}), s8[4194304]{0:T(1024)(128)(4,1)S(1)}, s32[]{:S(2)}) async-start(s8[8388608]{0:T(1024)(128)(4,1)} %bitcast.90), calls=%async_computation | async-start | bytes 8388608
  341.5 10.6 %copy-start.5 = (f32[592,1024]{1,0:T(8,128)S(1)}, f32[592,1024]{1,0:T(8,128)}, u32[]{:S(2)}) copy-start(f32[592,1024]{1,0:T(8,128)} %get-tuple-element.60) | copy-start | bytes 7274500
  341.5 10.9 %slice-start.1 = ((s8[8388608]{0:T(1024)(128)(4,1)}), s8[4194304]{0:T(1024)(128)(4,1)S(1)}, s32[]{:S(2)}) async-start(s8[8388608]{0:T(1024)(128)(4,1)} %bitcast.90), calls=%async_computation.1 | async-start | bytes 8388608
  352.1 6.1 copy-start.30
  359.3 3.3 copy-start.10
  362.6 28.2 %copy-start.4 = (f32[592,1024]{1,0:T(8,128)S(1)}, f32[592,1024]{1,0:T(8,128)}, u32[]{:S(2)}) copy-start(f32[592,1024]{1,0:T(8,128)} %get-tuple-element.74) | copy-start | bytes 7274500
  390.7 8.3 %copy-start.1 = (bf16[592,3072]{1,0:T(8,128)(2,1)}, bf16[592,3072]{1,0:T(8,128)(2,1)S(1)}, u32[]{:S(2)}) copy-start(bf16[592,3072]{1,0:T(8,128)(2,1)S(1)} %mix_heads_backward.3.refs_8_) | copy-start | bytes 10911748
  672.9 2.9 copy-start.18
  (12 other events, 28.1 us)

commit v5 on v4

--- a/solution.py
+++ b/solution.py
@@ -492,65 +492,6 @@
     full = SEQ // 16 * 16
     ref[pl.ds(full, ROWS - full), pl.ds(at, PAIR)] = jnp.zeros((ROWS - full, PAIR), LOW)
     ref[pl.ds(0, SEQ), pl.ds(at, PAIR)] = jnp.concatenate(pieces, axis=1)
-
-
-def projected_specs(blocks):
-    def spec(offset):
-        return pl.BlockSpec((ROWS, PAIR), lambda step: (0, offset + step))
-
-    return [spec(t * 3 * blocks + part * blocks) for t in range(2) for part in range(3)]
-
-
-def heads_backward_kernel(
-    query_a, key_a, value_a, query_b, key_b, value_b, grad_a, grad_b, out_ref
-):
-    step = pl.program_id(0)
-    scale = jnp.asarray(HEAD_DIM**-0.5, LOW)
-    part_width = out_ref.shape[1] // 6
-    for t, (query_ref, key_ref, value_ref, grad_ref) in enumerate(
-        ((query_a, key_a, value_a, grad_a), (query_b, key_b, value_b, grad_b))
-    ):
-        pieces = ([], [], [])
-        for head in range(2):
-            cols = slice(head * HEAD_DIM, (head + 1) * HEAD_DIM)
-            keys_here, values_here = key_ref[:SEQ, cols], value_ref[:SEQ, cols]
-            grads = grad_ref[:SEQ, cols]
-            queries = query_ref[:SEQ, cols] * scale
-            soft = turned_softmax(keys_here, queries)
-            soft_grad = dot_cols(values_here, grads)
-            delta = jnp.sum(soft_grad * soft, axis=0, keepdims=True)
-            score_grad = (soft * (soft_grad - delta)).astype(LOW)
-            pieces[0].append((dot_tokens(score_grad, keys_here) * HEAD_DIM**-0.5).astype(LOW))
-            pieces[1].append(dot_rows(score_grad, queries).astype(LOW))
-            pieces[2].append(dot_rows(soft.astype(LOW), grads).astype(LOW))
-        for part in range(3):
-            at = pl.multiple_of((t * 3 + part) * part_width + step * PAIR, PAIR)
-            store_rows(out_ref, at, pieces[part])
-
-
-def mix_heads_backward(projected, mixed_grad):
-    width = mixed_grad.shape[1]
-    blocks = width // 2 // PAIR
-
-    def grad_spec(offset):
-        return pl.BlockSpec((ROWS, PAIR), lambda step: (0, offset + step))
-
-    return pl.pallas_call(
-        heads_backward_kernel,
-        grid=(blocks,),
-        in_specs=projected_specs(blocks) + [grad_spec(0), grad_spec(blocks)],
-        out_specs=pl.BlockSpec((ROWS, 3 * width), lambda step: (0, 0)),
-        out_shape=jax.ShapeDtypeStruct((ROWS, 3 * width), LOW),
-        compiler_params=pltpu.CompilerParams(vmem_limit_bytes=48 * 1024 * 1024),
-        cost_estimate=pl.CostEstimate(
-            flops=10 * SEQ * SEQ * width, bytes_accessed=90 * 1024 * 1024, transcendentals=0
-        ),
-        name="mix_heads_backward",
-    )(*[projected] * 6, mixed_grad, mixed_grad)
-
-
-def pick(block, at, axis):
-    return lax.dynamic_index_in_dim(block, at, axis, keepdims=False)
 
 
 def gather_parts(width):
@@ -1048,7 +989,7 @@
     )(*shards, near, far, biases, norms)
     whole, results = results[: len(wholes)], results[len(wholes) :]
     weights = [
-        [whole[layer * 4 + kind].reshape(1024, -1) for kind in range(4)] for layer in range(layers)
+        [whole[layer * 4 + kind] for kind in range(4)] for layer in range(layers)
     ]
     cotangent_in, activations, results = results[0], results[1], results[2:]
     kept = [
@@ -1059,7 +1000,7 @@
 
 COLS = 256
 SETTLE_DEPTH = 6
-VAL_SLOTS, ARRIVAL_SLOTS = 6, 3
+VAL_SLOTS, ARRIVAL_SLOTS, REST_SLOTS, TURNED_SLOTS = 2, 2, 4, 3
 
 
 class Settle:
@@ -1068,25 +1009,28 @@
 
     def scratch(self):
         rows = (4, 2, 2, BLOCK, COLS)
-        pairs, vals, slots = len(self.pairs), VAL_SLOTS, ARRIVAL_SLOTS
+        pairs, slots = len(self.pairs), ARRIVAL_SLOTS
         sem = pltpu.SemaphoreType.DMA
         return dict(
-            left_in=pltpu.VMEM((2, ROWS, 1024), LOW),
-            left_turned=pltpu.VMEM((4, 1024, DEEP), LOW),
+            left_in=pltpu.VMEM((ROWS, 1024), LOW),
+            left_turned=pltpu.VMEM((TURNED_SLOTS, 1024, DEEP), LOW),
             right_in=pltpu.VMEM((2, 2, 4, DEEP, COLS), LOW),
-            core_out=pltpu.VMEM((2, 2, 2, *rows), LOW),
+            core_out=pltpu.VMEM((2, 2, *rows), LOW),
             core_in=pltpu.VMEM((slots, 2, 2, *rows), LOW),
-            val=pltpu.VMEM((vals, 2, 2, *rows), LOW),
+            val=pltpu.VMEM((VAL_SLOTS, 2, 2, *rows), LOW),
+            rest=pltpu.VMEM((REST_SLOTS, 2, 4, 2, BLOCK, COLS), LOW),
             first_a=pltpu.VMEM((slots, *rows), LOW),
             first_b=pltpu.VMEM((slots, 2, 4, 2, BLOCK, COLS), LOW),
             second=pltpu.VMEM((slots, 2, 4, 2, BLOCK, COLS), LOW),
             third=pltpu.VMEM((slots, 2, 2, 2, BLOCK, COLS), LOW),
             fourth=pltpu.VMEM((slots, 2, 2, BLOCK, COLS), LOW),
             fifth=pltpu.VMEM((slots, 2, BLOCK, COLS), LOW),
+            result=pltpu.VMEM((2, 2, 2, BLOCK, COLS), jnp.float32),
+            result_sem=sem((2, 2, 2)),
             send_sem=sem((pairs, 2, SETTLE_DEPTH)),
             recv_sem=sem((pairs, 2, SETTLE_DEPTH)),
             right_sem=sem((pairs, 2, 4)),
-            left_sem=sem((len(self.widths),)),
+            left_sem=sem((1,)),
         )
 
     def bind(self, lefts, rights, outs, refs):
@@ -1095,29 +1039,17 @@
             setattr(self, name, ref)
         self.z, self.x, self.c, self.y = place()
         self.partners = neighbours()
-        self.copies = {}
-        self.left_copies = {}
-        self.turned = {}
-        self.loaded = []
+        self.copies, self.turned, self.results = {}, {}, {}
         tail = ROWS // 128 * 128
-        self.left_turned[:, :, pl.ds(tail, DEEP - tail)] = jnp.zeros((4, 1024, DEEP - tail), LOW)
+        self.left_turned[:, :, pl.ds(tail, DEEP - tail)] = jnp.zeros(
+            (TURNED_SLOTS, 1024, DEEP - tail), LOW
+        )
         self.right_in[:, :, :, pl.ds(ROWS, DEEP - ROWS)] = jnp.zeros(
             (2, 2, 4, DEEP - ROWS, COLS), LOW
         )
 
     def load(self, pair):
-        if pair >= len(self.pairs):
-            return
         for unit, (matrix, step) in enumerate(self.pairs[pair]):
-            if matrix not in self.left_copies:
-                copy = pltpu.make_async_copy(
-                    self.lefts[matrix],
-                    self.left_in.at[len(self.loaded) % 2],
-                    self.left_sem.at[len(self.loaded)],
-                )
-                copy.start()
-                self.left_copies[matrix] = (copy, len(self.loaded))
-                self.loaded.append(matrix)
             width = self.widths[matrix]
             for t in range(2):
                 for core in range(2):
@@ -1130,13 +1062,24 @@
                     copy.start()
                     self.copies[(pair, unit, "right", 2 * t + core)] = copy
 
+    def turn(self, matrix):
+        if matrix in self.turned:
+            return
+        source, here = self.lefts[matrix]
+        if not here:
+            copy = pltpu.make_async_copy(source, self.left_in, self.left_sem.at[0])
+            copy.start()
+            copy.wait()
+            source = self.left_in
+        slot = len(self.turned) % TURNED_SLOTS
+        for quarter in range(4):
+            cols = pl.ds(quarter * 256, 256)
+            self.left_turned[slot, cols, pl.ds(0, ROWS)] = source[:, cols].T
+        self.turned[matrix] = slot
+
     def wait_load(self, pair):
         for unit, (matrix, _) in enumerate(self.pairs[pair]):
-            if matrix not in self.turned:
-                copy, at = self.left_copies[matrix]
-                copy.wait()
-                self.left_turned[at % 4, :, pl.ds(0, ROWS)] = self.left_in[at % 2].T
-                self.turned[matrix] = at % 4
+            self.turn(matrix)
             for entry in range(4):
                 self.copies.pop((pair, unit, "right", entry)).wait()
 
@@ -1164,13 +1107,13 @@
         if pair < 0 or pair >= len(self.pairs):
             return
         z, x, c, y = self.z, self.x, self.c, self.y
-        slot, arrival = pair % VAL_SLOTS, pair % ARRIVAL_SLOTS
+        arrival = pair % ARRIVAL_SLOTS
         high, lower = lax.div(z, 2), lax.rem(z, 2)
-        near_pair, far_pair = pl.ds(2 * high, 2), pl.ds(2 * (1 - high), 2)
+        far_pair = pl.ds(2 * (1 - high), 2)
         far_z = z + 1 - 2 * lower
-        val = self.val.at[slot, unit]
+        val, rest = self.val.at[pair % VAL_SLOTS, unit], self.rest.at[pair % REST_SLOTS, unit]
         if stage == 0:
-            out = self.core_out.at[pair % 2, unit]
+            out = self.core_out.at[unit]
 
             @pl.loop(0, 4)
             def _(row):
@@ -1214,32 +1157,45 @@
 
             @pl.loop(0, 4)
             def _(row):
-                val[y, row, x] = val[y, row, x] + self.second[arrival, unit, row]
-
-            target = self.third.at[arrival, unit]
-            self.send(pair, unit, 3, val.at[y, far_pair, x], target, "z2")
+                rest[row] = val[y, row, x] + self.second[arrival, unit, row]
+
+            self.send(pair, unit, 3, rest.at[far_pair], self.third.at[arrival, unit], "z2")
         elif stage == 4:
             for row in range(2):
                 at = 2 * high + row
-                val[y, at, x] = val[y, at, x] + self.third[arrival, unit, row]
-            target = self.fourth.at[arrival, unit]
-            self.send(pair, unit, 4, val.at[y, far_z, x], target, "z1")
+                rest[at] = rest[at] + self.third[arrival, unit, row]
+            self.send(pair, unit, 4, rest.at[far_z], self.fourth.at[arrival, unit], "z1")
         elif stage == 5:
-            val[y, z, x] = val[y, z, x] + self.fourth[arrival, unit]
-            target = self.fifth.at[arrival, unit]
-            self.send(pair, unit, 5, val.at[y, z, x, 1 - c], target, "core")
+            rest[z] = rest[z] + self.fourth[arrival, unit]
+            self.send(pair, unit, 5, rest.at[z, 1 - c], self.fifth.at[arrival, unit], "core")
         else:
             matrix, step = self.pairs[pair][unit]
             out_ref, layer = self.outs[matrix]
-            cols = pl.ds(step * COLS, COLS)
-            out_ref[layer, c, :, cols] = val[y, z, x, c].astype(jnp.float32)
-            out_ref[layer, 1 - c, :, cols] = self.fifth[arrival, unit].astype(jnp.float32)
+            slot = pair % 2
+            for copy in self.results.pop((slot, unit), ()):
+                copy.wait()
+            result = self.result.at[slot, unit]
+            result[c] = rest[z, c].astype(jnp.float32)
+            result[1 - c] = self.fifth[arrival, unit].astype(jnp.float32)
+            self.results[(slot, unit)] = []
+            for core in range(2):
+                copy = pltpu.make_async_copy(
+                    result.at[core],
+                    out_ref.at[layer, core, :, pl.ds(step * COLS, COLS)],
+                    self.result_sem.at[slot, unit, core],
+                )
+                copy.start()
+                self.results[(slot, unit)].append(copy)
+
+    def finish(self):
+        for copies in self.results.values():
+            for copy in copies:
+                copy.wait()
 
     def tick(self, pair):
         for stage in range(SETTLE_DEPTH, 0, -1):
             for unit in range(2):
                 self.stage(pair - stage, unit, stage)
-        self.load(pair + 1)
         if pair < len(self.pairs):
             self.wait_load(pair)
             for unit in range(2):
@@ -1247,117 +1203,454 @@
 
 
 TOTAL_LINKS = ("x", "y", "z1", "z2", "core")
-
-
-def settle_kernel(plan, kinds, layers, *refs):
-    matrices = kinds * layers
-    lefts, rights = refs[:matrices], refs[matrices : 2 * matrices]
-    small_ref, leaving_ref = refs[2 * matrices : 2 * matrices + 2]
-    refs = refs[2 * matrices + 2 :]
-    outs, total_ref, arriving_ref, refs = refs[:kinds], refs[kinds], refs[kinds + 1], refs[kinds + 2 :]
-    sums, sums_in, sums_send, sums_recv, swap_send, swap_recv = refs[:6]
-    plan.bind(
-        lefts, rights, [(outs[m % kinds], m // kinds) for m in range(matrices)], refs[6:]
-    )
-    plan.load(0)
-    greet(plan.partners)
-    swap = pltpu.make_async_remote_copy(
-        src_ref=leaving_ref,
-        dst_ref=arriving_ref,
-        send_sem=swap_send.at[0],
-        recv_sem=swap_recv.at[0],
-        device_id=plan.partners["y"],
-        device_id_type=MESH_IDS,
-    )
-    swap.start()
-    sums[0] = small_ref[...]
-    flying = None
-    for pair in range(len(plan.pairs) + SETTLE_DEPTH):
-        if flying is not None:
-            flying.wait()
-            sums[pair] = sums[pair - 1] + sums_in[pair - 1]
-            flying = None
-        if pair < len(TOTAL_LINKS):
-            flying = pltpu.make_async_remote_copy(
-                src_ref=sums.at[pair],
-                dst_ref=sums_in.at[pair],
-                send_sem=sums_send.at[pair],
-                recv_sem=sums_recv.at[pair],
-                device_id=plan.partners[TOTAL_LINKS[pair]],
+SUM_ROWS = 12
+TILE = 512
+KEPT = ("normed", "projected", "heads", "normed_two", "hidden", "slope", "middle", "incoming")
+
+
+class Backward:
+    def __init__(self, layers, widths):
+        self.layers, self.widths = layers, widths
+        pairs, self.needs = [], []
+        for layer in reversed(range(layers)):
+            base = layer * 4
+            feed = widths[2] // 2 // COLS
+            for kind, fact in ((3, "arrived"), (2, "fed")):
+                for k in range(0, feed, 2):
+                    pairs.append(((base + kind, k), (base + kind, k + 1)))
+                    self.needs.append((layer, fact))
+            rest = [(base + 1, k) for k in range(widths[1] // 2 // COLS)]
+            rest += [(base, k) for k in range(widths[0] // 2 // COLS)]
+            for k in range(0, len(rest), 2):
+                pairs.append((rest[k], rest[k + 1]))
+                self.needs.append((layer, "mixed"))
+        self.settle = Settle(widths * layers, pairs)
+
+    def scratch(self):
+        sem = pltpu.SemaphoreType.DMA
+        full = pltpu.VMEM((ROWS, 1024), jnp.float32)
+        low = pltpu.VMEM((ROWS, 1024), LOW)
+        steps = len(TOTAL_LINKS)
+        rows = self.layers * SUM_ROWS
+        own = dict(
+            grad=full,
+            delta=full,
+            values=full,
+            feed_grad=low,
+            mix_grad=low,
+            heads_grad=low,
+            projected=pltpu.VMEM((ROWS, 2 * self.widths[0]), LOW),
+            joined=pltpu.VMEM((ROWS, 2 * self.widths[0]), LOW),
+            tile_a=pltpu.VMEM((2, 4, 2, 2, BLOCK, TILE), LOW),
+            tile_b=pltpu.VMEM((2, 4, 2, 2, BLOCK, TILE), LOW),
+            slope_in=pltpu.VMEM((2, ROWS, TILE), LOW),
+            hidden_out=pltpu.VMEM((2, ROWS, TILE), LOW),
+            column_sums=pltpu.VMEM((8, 1, TILE), jnp.float32),
+            sums_part=pltpu.VMEM((3, 16, 1024), jnp.float32),
+            sums=pltpu.VMEM((steps + 1, rows, 1024), jnp.float32),
+            sums_in=pltpu.VMEM((steps, rows, 1024), jnp.float32),
+            leave=pltpu.VMEM((ROWS, 512), LOW),
+            tile_sem=sem((2, 3)),
+            hidden_sem=sem((2,)),
+            value_sem=sem((3,)),
+            sums_send=sem((steps,)),
+            sums_recv=sem((steps,)),
+            swap_send=sem((2,)),
+            swap_recv=sem((2,)),
+        )
+        return {**own, **self.settle.scratch()}
+
+    def bind(self, inputs, outputs, refs):
+        for name, ref in zip(self.scratch(), refs, strict=True):
+            setattr(self, name, ref)
+        layers = self.layers
+        count = layers * 4
+        self.weights, inputs = inputs[:count], inputs[count:]
+        self.kept = [
+            dict(zip(KEPT, inputs[k * len(KEPT) : (k + 1) * len(KEPT)])) for k in range(layers)
+        ]
+        self.upstream, self.gains, self.leaving = inputs[layers * len(KEPT) :]
+        outs, outputs = outputs[:4], outputs[4:]
+        self.total_out, self.near_out, self.arriving, outputs = (*outputs[:3], outputs[3:])
+        self.hidden_grads = outputs
+        self.facts = set()
+        lefts, rights = [], []
+        for layer in range(layers):
+            kept = self.kept[layer]
+            lefts += [
+                (kept["normed"], False),
+                (self.mix_grad, True),
+                (kept["normed_two"], False),
+                (self.feed_grad, True),
+            ]
+            rights += [self.joined, kept["heads"], self.hidden_grads[layer], kept["hidden"]]
+        self.settle.bind(
+            lefts,
+            rights,
+            [(outs[m % 4], m // 4) for m in range(count)],
+            [getattr(self, name) for name in self.settle.scratch()],
+        )
+        self.loaded_pair = -1
+
+    def fetch(self, entry, source, target):
+        copy = pltpu.make_async_copy(source, target, self.value_sem.at[entry])
+        copy.start()
+        return copy
+
+    def swap(self, entry, source):
+        copy = pltpu.make_async_remote_copy(
+            src_ref=source,
+            dst_ref=self.arriving.at[entry],
+            send_sem=self.swap_send.at[entry],
+            recv_sem=self.swap_recv.at[entry],
+            device_id=self.settle.partners["y"],
+            device_id_type=MESH_IDS,
+        )
+        copy.start()
+        return copy
+
+    def row_loop(self, body):
+        @pl.loop(0, ROWS // 16)
+        def _(step):
+            body(pl.ds(pl.multiple_of(step * 16, 16), 16))
+
+    def put_sum(self, layer, row, values):
+        self.sums[0, pl.ds(layer * SUM_ROWS + row, 1), :] = values
+
+    def begin(self):
+        self.fetch(0, self.upstream, self.feed_grad).wait()
+        self.facts.add((self.layers - 1, "arrived"))
+
+    def widen(self):
+        self.sums_part[...] = jnp.zeros_like(self.sums_part)
+
+        def body(rows):
+            values = self.feed_grad[rows, :].astype(jnp.float32)
+            self.grad[rows, :] = values
+            self.sums_part[2] += values
+
+        self.row_loop(body)
+        self.put_sum(self.layers - 1, 7, jnp.sum(self.sums_part[2], axis=0, keepdims=True))
+
+    def tiles(self, first, last, sources, targets, body):
+        def copies(part, slot):
+            cols = pl.ds(pl.multiple_of(part * TILE, TILE), TILE)
+            return [
+                pltpu.make_async_copy(
+                    source.at[(slice(None),) * (len(source.shape) - 1) + (cols,)],
+                    target.at[slot],
+                    self.tile_sem.at[slot, entry],
+                )
+                for entry, (source, target) in enumerate(zip(sources, targets))
+            ]
+
+        for copy in copies(first, first % 2):
+            copy.start()
+
+        @pl.loop(first, last)
+        def _(part):
+            slot = lax.rem(part, 2)
+
+            @pl.when(part + 1 < last)
+            def _():
+                for copy in copies(part + 1, 1 - slot):
+                    copy.start()
+
+            for copy in copies(part, slot):
+                copy.wait()
+            body(part, slot)
+
+    def add_delta(self, is_first, grads, weights):
+        for half in range(2):
+            cols = slice(half * 512, (half + 1) * 512)
+            product = dot_cols(grads, weights[2 * half : 2 * half + 2].reshape(512, TILE))
+            before = jnp.where(is_first, 0.0, self.delta[:, cols])
+            self.delta[:, cols] = before + product
+
+    def feed(self, layer, first, last):
+        out_ref = self.hidden_grads[layer]
+        if first == 0:
+            self.value_copy = self.fetch(1, self.kept[layer]["middle"], self.values)
+
+        def out_copy(part, slot):
+            cols = pl.ds(pl.multiple_of(part * TILE, TILE), TILE)
+            return pltpu.make_async_copy(
+                self.hidden_out.at[slot], out_ref.at[:, cols], self.hidden_sem.at[slot]
+            )
+
+        def body(part, slot):
+            @pl.when(part >= first + 2)
+            def _():
+                out_copy(part - 2, slot).wait()
+
+            down = self.tile_a[slot].reshape(1024, TILE)
+            slope = self.slope_in[slot].astype(jnp.float32)
+            grads = (dot_rows(self.feed_grad[...], down) * slope).astype(LOW)
+            self.hidden_out[slot] = grads
+            out_copy(part, slot).start()
+            self.column_sums[part] = jnp.sum(grads.astype(jnp.float32), axis=0, keepdims=True)
+            self.add_delta(part == 0, grads, self.tile_b.at[slot])
+
+        self.tiles(
+            first,
+            last,
+            (self.weights[layer * 4 + 3], self.weights[layer * 4 + 2], self.kept[layer]["slope"]),
+            (self.tile_a, self.tile_b, self.slope_in),
+            body,
+        )
+        for part in (last - 2, last - 1):
+            out_copy(part, part % 2).wait()
+        if last * TILE == out_ref.shape[1]:
+            for row in range(4):
+                pieces = [self.column_sums[2 * row], self.column_sums[2 * row + 1]]
+                self.put_sum(layer, 3 + row, jnp.concatenate(pieces, axis=1))
+            self.facts.add((layer, "fed"))
+
+    def norm_back(self, layer, gain_row, sum_row, low_ref, total_at):
+        self.value_copy.wait()
+        gain = self.gains[pl.ds(gain_row, 1), :]
+        self.sums_part[...] = jnp.zeros_like(self.sums_part)
+
+        def body(rows):
+            stream, delta = self.values[rows, :], self.delta[rows, :]
+            mean = jnp.mean(stream, axis=1, keepdims=True)
+            square = jnp.mean(stream * stream, axis=1, keepdims=True)
+            inverse = lax.rsqrt(square - mean * mean + norm_eps)
+            centred = (stream - mean) * inverse
+            weighted = delta * centred
+            self.sums_part[0] += weighted
+            self.sums_part[1] += delta
+            scaled = delta * gain
+            grad = self.grad[rows, :] + inverse * (
+                scaled
+                - jnp.mean(scaled, axis=1, keepdims=True)
+                - centred * jnp.mean(weighted * gain, axis=1, keepdims=True)
+            )
+            self.grad[rows, :] = grad
+            self.sums_part[2] += grad
+            if low_ref is not None:
+                low_ref[rows, :] = grad.astype(LOW)
+
+        self.row_loop(body)
+        for entry in range(2):
+            total = jnp.sum(self.sums_part[entry], axis=0, keepdims=True)
+            self.put_sum(layer, sum_row + entry, total)
+        if total_at is not None:
+            total = jnp.sum(self.sums_part[2], axis=0, keepdims=True)
+            self.put_sum(*total_at, total)
+
+    def out_back(self, layer):
+        self.norm_back(layer, self.layers + layer, 10, self.mix_grad, (layer, 2))
+        self.value_copy = self.fetch(1, self.kept[layer]["incoming"], self.values)
+        self.projected_copy = self.fetch(2, self.kept[layer]["projected"], self.projected)
+
+        def body(part, slot):
+            cols = pl.ds(pl.multiple_of(part * TILE, TILE), TILE)
+            weights = self.tile_a[slot].reshape(1024, TILE)
+            self.heads_grad[:, cols] = dot_rows(self.mix_grad[...], weights).astype(LOW)
+
+        self.tiles(0, 2, (self.weights[layer * 4 + 1],), (self.tile_a,), body)
+
+    def mix_back(self, layer, first, last):
+        if first == 0:
+            self.projected_copy.wait()
+        half = self.heads_grad.shape[1] // 2
+
+        @pl.loop(2 * first, 2 * last)
+        def _(turn):
+            step, t = lax.div(turn, 2), lax.rem(turn, 2)
+
+            def at(part):
+                start = (t * 3 + part) * half + step * PAIR
+                return pl.ds(pl.multiple_of(start, PAIR), PAIR)
+
+            here = pl.ds(pl.multiple_of(t * half + step * PAIR, PAIR), PAIR)
+            rows = pl.ds(0, SEQ)
+            all_queries = self.projected[rows, at(0)] * jnp.asarray(HEAD_DIM**-0.5, LOW)
+            all_keys, all_values = self.projected[rows, at(1)], self.projected[rows, at(2)]
+            all_grads = self.heads_grad[rows, here]
+            pieces = ([], [], [])
+            for head in range(2):
+                cols = slice(head * HEAD_DIM, (head + 1) * HEAD_DIM)
+                keys_here, queries = all_keys[:, cols], all_queries[:, cols]
+                grads = all_grads[:, cols]
+                soft = turned_softmax(keys_here, queries)
+                soft_grad = dot_cols(all_values[:, cols], grads)
+                delta = jnp.sum(soft_grad * soft, axis=0, keepdims=True)
+                score_grad = (soft * (soft_grad - delta)).astype(LOW)
+                pieces[0].append(
+                    (dot_tokens(score_grad, keys_here) * HEAD_DIM**-0.5).astype(LOW)
+                )
+                pieces[1].append(dot_rows(score_grad, queries).astype(LOW))
+                pieces[2].append(dot_rows(soft.astype(LOW), grads).astype(LOW))
+            for part in range(3):
+                start = (t * 3 + part) * half + step * PAIR
+                store_rows(self.joined, pl.multiple_of(start, PAIR), pieces[part])
+
+        if last * PAIR == half:
+            self.facts.add((layer, "mixed"))
+
+    def project_back(self, layer):
+        def body(part, slot):
+            cols = pl.ds(pl.multiple_of(part * TILE, TILE), TILE)
+            grads = self.joined[:, cols]
+            self.column_sums[part] = jnp.sum(grads.astype(jnp.float32), axis=0, keepdims=True)
+            self.add_delta(part == 0, grads, self.tile_a.at[slot])
+
+        self.tiles(0, 6, (self.weights[layer * 4],), (self.tile_a,), body)
+        for row, part in ((0, 0), (1, 2)):
+            pieces = [self.column_sums[part], self.column_sums[3 + part]]
+            self.put_sum(layer, row, jnp.concatenate(pieces, axis=1))
+
+    def first_back(self, layer):
+        last = layer == 0
+        low_ref = None if last else self.feed_grad
+        self.norm_back(layer, layer, 8, low_ref, None if last else (layer - 1, 7))
+        if not last:
+            self.facts.add((layer - 1, "arrived"))
+
+    def end(self):
+        y = self.y
+        near_at = pl.ds(pl.multiple_of(y * 512, 512), 512)
+        far_at = pl.ds(pl.multiple_of((1 - y) * 512, 512), 512)
+        self.leave[...] = self.grad[:, far_at].astype(LOW)
+        self.swaps.append(self.swap(1, self.leave))
+        copy = self.fetch(0, self.grad.at[:, near_at], self.near_out)
+        copy.wait()
+        self.facts.add("summed")
+
+    def chain(self):
+        steps = [(1, self.begin, ()), (2, self.widen, ())]
+        for layer in reversed(range(self.layers)):
+            steps += [
+                (9, lambda layer=layer: self.feed(layer, 0, 4), ()),
+                (9, lambda layer=layer: self.feed(layer, 4, 8), ()),
+                (4, lambda layer=layer: self.out_back(layer), ((layer + 1, 1),)),
+            ]
+            for k in range(4):
+                needs = ((layer + 1, 0),)
+                steps.append((7, lambda layer=layer, k=k: self.mix_back(layer, k, k + 1), needs))
+            steps += [
+                (8, lambda layer=layer: self.project_back(layer), ()),
+                (3, lambda layer=layer: self.first_back(layer), ((layer, 3),)),
+            ]
+        return steps + [(1, self.end, ())]
+
+    def add_sums(self, step):
+        if step > 0:
+            self.sums_copy.wait()
+            self.sums[step] = self.sums[step - 1] + self.sums_in[step - 1]
+        if step < len(TOTAL_LINKS):
+            copy = pltpu.make_async_remote_copy(
+                src_ref=self.sums.at[step],
+                dst_ref=self.sums_in.at[step],
+                send_sem=self.sums_send.at[step],
+                recv_sem=self.sums_recv.at[step],
+                device_id=self.settle.partners[TOTAL_LINKS[step]],
                 device_id_type=MESH_IDS,
             )
-            flying.start()
-        plan.tick(pair)
-    total_ref[...] = sums[len(TOTAL_LINKS)]
-    swap.wait()
-
-
-def layer_pairs(base, widths):
-    feed = [((base + 2, k), (base + 3, k)) for k in range(widths[2] // 2 // COLS)]
-    rest = [(base, k) for k in range(widths[0] // 2 // COLS)]
-    rest.insert(1, (base + 1, 0))
-    return feed + [(rest[k], rest[k + 1]) for k in range(0, len(rest), 2)]
-
-
-def settle_all(layer_terms, small, leaving):
-    layers, kinds = len(layer_terms), len(layer_terms[0])
-    widths = [right.shape[1] // 2 for _, right in layer_terms[0]]
-    pairs = []
-    for layer in reversed(range(layers)):
-        pairs += layer_pairs(layer * kinds, widths)
-    plan = Settle(widths * layers, pairs)
-    lefts = [left for terms in layer_terms for left, _ in terms]
-    rights = [right for terms in layer_terms for _, right in terms]
-    steps = len(TOTAL_LINKS)
+            copy.start()
+            self.sums_copy = copy
+
+    def run(self):
+        self.y = lax.axis_index("tensor")
+        settle = self.settle
+        greet(settle.partners)
+        self.swaps = [self.swap(0, self.leaving)]
+        chain = self.chain()
+        last_pair = {}
+        for pair, units in enumerate(settle.pairs):
+            for matrix, _ in units:
+                last_pair[matrix] = pair
+        pairs, loaded, sum_step = len(settle.pairs), set(), 0
+        passed = -1
+
+        def free(needs):
+            for layer, kind in needs:
+                if layer < self.layers and passed < last_pair[layer * 4 + kind]:
+                    return False
+            return True
+
+        def advance():
+            _, step, _ = chain.pop(0)
+            step()
+
+        pair = 0
+        while pair < pairs + SETTLE_DEPTH or sum_step <= len(TOTAL_LINKS):
+            if pair < pairs:
+                while self.needs[pair] not in self.facts:
+                    advance()
+                if pair not in loaded:
+                    settle.load(pair)
+                    loaded.add(pair)
+            settle.tick(pair)
+            passed = pair
+            if "summed" in self.facts and sum_step <= len(TOTAL_LINKS):
+                self.add_sums(sum_step)
+                sum_step += 1
+            if pair + 1 < pairs and self.needs[pair + 1] in self.facts:
+                settle.load(pair + 1)
+                loaded.add(pair + 1)
+            budget = CHAIN_A_TICK
+            while chain and budget > 0 and free(chain[0][2]):
+                budget -= chain[0][0]
+                advance()
+            pair += 1
+        self.total_out[...] = self.sums[len(TOTAL_LINKS)]
+        settle.finish()
+        for copy in self.swaps:
+            copy.wait()
+
+
+CHAIN_A_TICK = 10
+
+
+def backward(weights, kept, upstream, gains, leaving):
+    layers = len(weights)
+    widths = [block.shape[-1] // 2 for block in weights[0]]
+    plan = Backward(layers, widths)
     any_spec, vmem_spec = pl.BlockSpec(memory_space=pl.ANY), pl.BlockSpec(memory_space=pltpu.VMEM)
-    return pl.pallas_call(
-        lambda *refs: settle_kernel(plan, kinds, layers, *refs),
-        out_shape=[jax.ShapeDtypeStruct((layers, 2, BLOCK, width // 2), jnp.float32) for width in widths]
-        + [
-            jax.ShapeDtypeStruct(small.shape, jnp.float32),
-            jax.ShapeDtypeStruct(leaving.shape, leaving.dtype),
-        ],
-        in_specs=[any_spec] * (2 * kinds * layers) + [vmem_spec, any_spec],
-        out_specs=[vmem_spec] * (kinds + 1) + [any_spec],
-        scratch_shapes=[
-            pltpu.VMEM((steps + 1, *small.shape), jnp.float32),
-            pltpu.VMEM((steps, *small.shape), jnp.float32),
-            pltpu.SemaphoreType.DMA((steps,)),
-            pltpu.SemaphoreType.DMA((steps,)),
-            pltpu.SemaphoreType.DMA((1,)),
-            pltpu.SemaphoreType.DMA((1,)),
-            *plan.scratch().values(),
-        ],
+    operands = [block for layer in weights for block in layer]
+    operands += [values[name] for values in kept for name in KEPT]
+    operands += [upstream, gains, leaving]
+    in_specs = [any_spec] * len(operands)
+    in_specs[-2] = vmem_spec
+    outs = [jax.ShapeDtypeStruct((layers, 2, BLOCK, width // 2), jnp.float32) for width in widths]
+    outs += [
+        jax.ShapeDtypeStruct((layers * SUM_ROWS, 1024), jnp.float32),
+        jax.ShapeDtypeStruct((ROWS, 512), jnp.float32),
+        jax.ShapeDtypeStruct((2, ROWS, 512), LOW),
+    ]
+    outs += [jax.ShapeDtypeStruct((ROWS, 2 * widths[2]), LOW)] * layers
+    out_specs = [any_spec] * len(outs)
+    out_specs[4] = vmem_spec
+
+    def kernel(*refs):
+        ins, refs = refs[: len(operands)], refs[len(operands) :]
+        plan.bind(ins, refs[: len(outs)], refs[len(outs) :])
+        plan.run()
+
+    results = pl.pallas_call(
+        kernel,
+        out_shape=outs,
+        in_specs=in_specs,
+        out_specs=out_specs,
+        scratch_shapes=list(plan.scratch().values()),
         compiler_params=pltpu.CompilerParams(
-            collective_id=1, has_side_effects=True, vmem_limit_bytes=58 * 1024 * 1024
+            collective_id=1, has_side_effects=True, vmem_limit_bytes=60 * 1024 * 1024
         ),
         cost_estimate=pl.CostEstimate(
-            flops=24 * 4 * 1024 * 1024 * ROWS, bytes_accessed=700 * 1024 * 1024, transcendentals=0
+            flops=120 * 1024**3, bytes_accessed=700 * 1024 * 1024, transcendentals=0
         ),
-        name="settle_all",
-    )(*lefts, *rights, small, leaving)
+        name="backward",
+    )(*operands)
+    return results[:4], results[4], results[5], results[6]
 
 
 def in_order(own, other, index, axis):
     first = jnp.where(index == 0, own, other)
     second = jnp.where(index == 0, other, own)
     return jnp.concatenate((first, second), axis=axis)
-
-
-def centre(stream):
-    row_mean = jnp.mean(stream, axis=1, keepdims=True)
-    square_mean = jnp.mean(stream * stream, axis=1, keepdims=True)
-    inverse_std = lax.rsqrt(square_mean - row_mean * row_mean + norm_eps)
-    return (stream - row_mean) * inverse_std, inverse_std
-
-
-def whole_norm_backward(upstream, centred, inverse_std, gain):
-    scaled = upstream * gain
-    return inverse_std * (
-        scaled
-        - jnp.mean(scaled, axis=1, keepdims=True)
-        - centred * jnp.mean(scaled * centred, axis=1, keepdims=True)
-    )
 
 
 def image_body(
@@ -1408,85 +1701,27 @@
         norms.astype(jnp.float32),
     )
 
-    def row(table, layer):
-        return table[layer][None].astype(jnp.float32)
-
-    upstream = in_order(own_rows(cotangent, y), cotangent_in, y, 1).astype(jnp.float32)
-    small = [None] * layers
-    terms = [None] * layers
-    for layer in reversed(range(layers)):
-        project_w, out_w, up_w, down_w = weights[layer]
-        values = kept[layer]
-        normed, projected, heads = values["normed"], values["projected"], values["heads"]
-        normed_two, hidden = values["normed_two"], values["hidden"]
-        centred_two, inverse_two = centre(values["middle"])
-        centred, inverse = centre(values["incoming"])
-        down_bias_sum = jnp.sum(upstream, axis=0)
-        upstream_low = upstream.astype(LOW)
-        down_term = (upstream_low, hidden)
-        hidden_grad = (dot_rows(upstream_low, down_w) * values["slope"].astype(jnp.float32)).astype(
-            LOW
-        )
-        up_bias_sum = jnp.sum(hidden_grad.astype(jnp.float32), axis=0)
-        up_term = (normed_two, hidden_grad)
-        normed_two_grad = dot_cols(hidden_grad, up_w)
-        second_gain_sum = jnp.sum(normed_two_grad * centred_two, axis=0)
-        second_shift_sum = jnp.sum(normed_two_grad, axis=0)
-        upstream = upstream + whole_norm_backward(
-            normed_two_grad, centred_two, inverse_two, row(second_gain, layer)
-        )
-        out_bias_sum = jnp.sum(upstream, axis=0)
-        upstream_low = upstream.astype(LOW)
-        out_term = (upstream_low, heads)
-        heads_grad = dot_rows(upstream_low, out_w).astype(LOW)
-        joined = mix_heads_backward(projected, heads_grad)
-        joined_sums = jnp.sum(joined.astype(jnp.float32), axis=0).reshape(2, 3, half)
-        project_term = (normed, joined)
-        normed_grad = dot_cols(joined, project_w)
-        first_gain_sum = jnp.sum(normed_grad * centred, axis=0)
-        first_shift_sum = jnp.sum(normed_grad, axis=0)
-        upstream = upstream + whole_norm_backward(
-            normed_grad, centred, inverse, row(first_gain, layer)
-        )
-        small[layer] = jnp.concatenate(
-            (
-                joined_sums[:, 0].reshape(-1),
-                joined_sums[:, 2].reshape(-1),
-                out_bias_sum,
-                up_bias_sum,
-                down_bias_sum,
-                first_gain_sum,
-                first_shift_sum,
-                second_gain_sum,
-                second_shift_sum,
-            )
-        )
-        terms[layer] = (project_term, out_term, up_term, down_term)
-
-    width = 2 * half
-
     def columns(rows, t):
         return lax.dynamic_slice_in_dim(rows, t * half, half, axis=1)
 
-    leaving = jnp.stack((columns(activations, far), columns(upstream, far).astype(LOW)))
-    project_out, out_out, up_out, down_out, totals, arriving = settle_all(
-        terms, jnp.stack(small).reshape(-1, width), leaving
+    upstream = in_order(own_rows(cotangent, y), cotangent_in, y, 1)
+    gains = jnp.concatenate((first_gain, second_gain)).astype(jnp.float32)
+    (project_out, out_out, up_out, down_out), totals, near_gradient, arriving = backward(
+        weights, kept, upstream, gains, columns(activations, far)
     )
     totals = totals.reshape(layers, -1)
     project_out, out_out, up_out, down_out = [
         jnp.swapaxes(block, 1, 2).reshape(layers, BLOCK, -1)
         for block in (project_out, out_out, up_out, down_out)
     ]
+    width = 2 * half
     small_outs, at = [], 0
     for size in (width, width, width, hidden_width, width, width, width, width, width):
         small_outs.append(totals[:, at : at + size])
         at += size
-    def to_owner(rows, arrived):
-        return in_order(columns(rows, y)[:SEQ], arrived[:SEQ].astype(rows.dtype), y, 0)
-
     return (
-        to_owner(activations, arriving[0]),
-        to_owner(upstream, arriving[1]),
+        in_order(columns(activations, y)[:SEQ], arriving[0, :SEQ], y, 0),
+        in_order(near_gradient[:SEQ], arriving[1, :SEQ].astype(jnp.float32), y, 0),
         project_out[:, :, :half],
         project_out[:, :, half : 2 * half],
         project_out[:, :, 2 * half :],

time: 680 us -> 617 us (0.907)
  matrix products: 50.4 us -> 0 us
  other arithmetic: 23 us -> 13.3 us
    dot_general x8 -> x0, matrix products: 50.4 us -> none  [the longest x4 26.9 us: dot_cols(): lax.dot_general(left, right, (((1,), (1,)), ((), ())), preferred_element_...]
    reduce_sum x9 -> x0, other arithmetic: 7.94 us -> none  [the longest x2 3.55 us: image_body(): jnp.sum(joined.astype(jnp.float32), axis=0).reshape(2, 3, half)]
    pallas_call x3 -> x1, Pallas kernels: 313 us -> 310 us  [backward(): pl.pallas_call(kernel, out_shape=outs, in_specs=in_specs, out_specs=out_s...]
where the time goes in v5:
time: 617 us; the launch traced here: 613 us
  Pallas kernels  584 us (95%)
  local copies, waits for them, and re-layouts  14.3 us (2%)
  other arithmetic  13.3 us (2%)
    pallas_call x1, Pallas kernels, backward(): pl.pallas_call(kernel, out_shape=outs, in_specs=in_specs, out_specs=out_s...  310 us
    pallas_call x1, Pallas kernels, forward(): pl.pallas_call(kernel, out_shape=outs, in_specs=[any_spec] * 4 + [vmem_sp...  274 us

profile of v5, /device:TPU:0, one launch (start us, length us, event | category | flops | bytes accessed | tf_op | source)
XLA Modules:
  0.0 613.0 jit_solution(246336586801436144)
XLA Ops:
  0.7 1.3 maximum_convert_fusion.1.refs_25_
  2.0 0.7 constant_dynamic-update-slice_fusion.5
  2.7 0.7 constant_dynamic-update-slice_fusion.3
  3.4 0.7 constant_dynamic-update-slice_fusion.2
  4.1 0.7 constant_dynamic-update-slice_fusion.1
  4.8 0.7 constant_dynamic-update-slice_fusion
  6.1 1.4 maximum_convert_fusion.refs_7_
  7.5 1.8 pad_maximum_fusion.4.refs_0_
  9.3 2.2 constant_dynamic-slice_fusion.1
  11.5 0.9 pad.19.refs_4_
  12.4 1.1 pad_maximum_fusion.1.refs_5_
  13.6 274.4 %forward.1 = (bf16[4,2,2,64,3072]{4,3,2,1,0:T(8,128)(2,1)}, bf16[4,2,2,64,1024]{4,3,2,1,0:T(8,128)(2,1)}, bf16[4,2,2,64,4096]{4,3,2,1,0:T(8,128)(2,1)}, bf16[4,2...) custom-call(bf16[2,64,1536]{2,1,0:T(8,128)(2,1)} %pad_maximum_fusion, ...), custom_call_target="tpu_custom_call" | custom-call | flops 64424509440 | bytes 734003200 | tf_op jit(solution)/shard_map/forward/pallas_call | solution.py:976
  288.0 2.0 constant_dynamic-slice_fusion.refs_26_
  290.2 1.2 pad_maximum_fusion.2.refs_24_
  291.4 309.9 %backward.1 = (f32[2,2,64,768]{3,2,1,0:T(8,128)}, f32[2,2,64,256]{3,2,1,0:T(8,128)}, f32[2,2,64,1024]{3,2,1,0:T(8,128)}, f32[2,2,64,1024]{3,2,1,0:T(8,128)}, f32...) custom-call(bf16[4,2,2,64,3072]{4,3,2,1,0:T(8,128)(2,1)} %get-tuple-, ...), custom_call_target="tpu_custom_call" | custom-call | flops 128849018880 | bytes 734003200 | tf_op jit(solution)/shard_map/backward/pallas_call | solution.py:1633
  601.3 1.5 bitcast_select_fusion.1
  602.8 1.2 pad_maximum_fusion.3
  604.5 1.4 convert_select_fusion.1
  605.9 1.7 pad_maximum_fusion
  607.6 0.9 fusion
  609.2 0.6 fusion.1
  609.9 0.7 copy.39
  610.6 1.0 copy.40
  611.7 1.1 copy.41
  (23 shorter events, 2.3 us)
Async XLA Ops:
  288.0 2.0 copy-start.4
  602.8 1.7 copy-start
  605.9 1.7 copy-start.3
  607.5 1.0 copy-start.6
  607.6 2.3 copy-start.5
  607.6 3.0 copy-start.2
  609.9 1.8 copy-start.1

commit v6 on v5

--- a/solution.py
+++ b/solution.py
@@ -494,14 +494,8 @@
     ref[pl.ds(0, SEQ), pl.ds(at, PAIR)] = jnp.concatenate(pieces, axis=1)
 
 
-def gather_parts(width):
-    last = 256 if width >= 1024 else 0
+def gather_stages(z, x, c, y, whole, start, width, last):
     share = (width - last) // 2
-    return share, last
-
-
-def gather_stages(z, x, c, y, whole, start, width):
-    share, last = gather_parts(width)
 
     def cols(t, at, size):
         return pl.ds(pl.multiple_of(t * whole + start + at, 128), size)
@@ -556,6 +550,8 @@
 
 GATHER_COPIES = 21
 GATHER_DEPTH = 5
+GATHER_LAG = 2
+CHUNK = 512
 
 
 class Gather:
@@ -576,12 +572,14 @@
         z, x, c, y = place()
         self.partners = neighbours()
         self.plans, self.own, self.flying = [], [], {}
-        for chunk, (matrix, start, width) in enumerate(self.chunks):
-            whole = shards[matrix].shape[1]
-            self.plans.append(gather_stages(z, x, c, y, whole, start, width))
+        for chunk, (matrix, start, width, last) in enumerate(self.chunks):
+            whole = wholes[matrix].shape[4] // 2
+            self.plans.append(gather_stages(z, x, c, y, whole, start, width, last))
             mine = pl.ds(pl.multiple_of(y * whole + start, 128), width)
+            size = shards[matrix][0].shape[1]
+            shard = shards[matrix][start // size]
             copy = pltpu.make_async_copy(
-                shards[matrix].at[:, pl.ds(start, width)],
+                shard.at[:, pl.ds(start % size, width)],
                 wholes[matrix].at[z, x, c, pl.ds(0, BLOCK), mine],
                 own_sem.at[chunk],
             )
@@ -591,7 +589,7 @@
     def tick(self, tick):
         done = None
         for stage_idx in range(GATHER_DEPTH, -1, -1):
-            chunk = tick - stage_idx
+            chunk = tick - GATHER_LAG * stage_idx
             if chunk < 0 or chunk >= len(self.chunks):
                 continue
             if stage_idx == 0:
@@ -634,11 +632,10 @@
         self.layers, self.widths = layers, widths
         chunks = []
         for layer in range(layers):
-            base = layer * len(widths)
             for kind, width in enumerate(widths):
-                split = 2 if layer == layers - 1 and kind == len(widths) - 1 else 1
-                part = width // split
-                chunks += [(base + kind, k * part, part) for k in range(split)]
+                for start in range(0, width, CHUNK):
+                    last = CHUNK // 2 if len(chunks) % 4 == 3 else 0
+                    chunks.append((layer * len(widths) + kind, start, CHUNK, last))
         self.gather = Gather(chunks)
 
     def scratch(self):
@@ -652,47 +649,48 @@
             weights_down=pltpu.VMEM((4, 2, 2, BLOCK, 2 * down), LOW),
             stream=full,
             tokens_in=low(512),
-            biases=pltpu.VMEM((2, 24, 512), jnp.float32),
+            biases=pltpu.VMEM((2, self.layers * BIAS_ROWS, 512), jnp.float32),
             normed=low(1024),
             projected=low(2 * project),
             heads=low(2 * out),
             normed_two=low(1024),
             hidden=low(2 * up),
             slope=low(2 * up),
-            weight_sem=sem((self.layers * 4, 1)),
-            split_sem=sem((2, 2)),
+            weight_sem=sem((len(self.gather.chunks), 2)),
             saved_sem=sem((self.layers, len(SAVED))),
             swap_send=sem((3,)),
             swap_recv=sem((3,)),
-            bias_sem=sem((1,)),
         )
         return {**own, **self.gather.scratch()}
 
     def bind(self, inputs, outputs, refs):
-        names = list(self.scratch())
-        for name, ref in zip(names, refs, strict=True):
+        for name, ref in zip(self.scratch(), refs, strict=True):
             setattr(self, name, ref)
-        shards, self.near, self.far, bias_ref, self.norms = (
-            inputs[:4],
-            inputs[4],
-            inputs[5],
-            inputs[6],
-            inputs[7],
-        )
+        shards, inputs = inputs[:6], inputs[6:]
+        self.near, self.far, self.norm_refs, bias_refs = inputs[0], inputs[1], inputs[2:6], inputs[6:]
         count = self.layers * 4
         self.wholes, outputs = outputs[:count], outputs[count:]
         self.cotangent_in, self.activations, outputs = outputs[0], outputs[1], outputs[2:]
         self.saved_out = [outputs[k * len(SAVED) : (k + 1) * len(SAVED)] for k in range(self.layers)]
         self.saving, self.loading = {}, {}
         self.y = lax.axis_index("tensor")
-        copy = pltpu.make_async_copy(bias_ref, self.biases.at[self.y], self.bias_sem.at[0])
-        copy.start()
+        kinds = (shards[:3], shards[3:4], shards[4:5], shards[5:6])
         self.gather.bind(
-            [shards[m % 4].at[m // 4] for m in range(count)],
+            [[shard.at[m // 4] for shard in kinds[m % 4]] for m in range(count)],
             self.wholes,
             [getattr(self, name) for name in self.gather.scratch()],
         )
-        copy.wait()
+        zeros = jnp.zeros((1, 512), jnp.float32)
+        for layer in range(self.layers):
+            row = layer * BIAS_ROWS
+            for ref in bias_refs:
+                line = ref[layer : layer + 1, :].astype(jnp.float32)
+                for start in range(0, ref.shape[1], 512):
+                    self.biases[self.y, row : row + 1, :] = line[:, start : start + 512]
+                    row += 1
+                if ref is bias_refs[0]:
+                    self.biases[self.y, row : row + 1, :] = zeros
+                    row += 1
 
     def swap(self):
         partner = self.gather.partners["y"]
@@ -727,29 +725,16 @@
             self.saving.pop((layer, name)).wait()
 
     def load(self, chunk):
-        matrix, start, width = self.gather.chunks[chunk]
+        matrix, start, width, _ = self.gather.chunks[chunk]
         whole = self.gather.wholes[matrix]
         buffer = (self.weights_project, self.weights_out, self.weights_up, self.weights_down)[
             matrix % 4
         ]
-        copies = []
-        full = whole.shape[4] // 2
-        if width == full:
-            copies.append((whole, buffer))
-        else:
-            for t in range(2):
-                at = (slice(None),) * 4 + (pl.ds(t * full + start, width),)
-                copies.append((whole.at[at], buffer.at[at]))
-        started = self.loading.setdefault(matrix, [])
-        for entry, (source, target) in enumerate(copies):
-            half = 0 if start == 0 else 1
-            if len(copies) == 2:
-                sem = self.split_sem.at[half, entry]
-            else:
-                sem = self.weight_sem.at[matrix, 0]
-            copy = pltpu.make_async_copy(source, target, sem)
+        for t in range(2):
+            at = (slice(None),) * 4 + (pl.ds(t * (whole.shape[4] // 2) + start, width),)
+            copy = pltpu.make_async_copy(whole.at[at], buffer.at[at], self.weight_sem.at[chunk, t])
             copy.start()
-            started.append(copy)
+            self.loading.setdefault(matrix, []).append(copy)
 
     def wait_weights(self, matrix):
         for copy in self.loading.pop(matrix):
@@ -758,9 +743,9 @@
     def bias_row(self, row):
         return jnp.concatenate([self.biases[t, pl.ds(row, 1), :] for t in range(2)], axis=1)
 
-    def norm(self, target, gain_row, shift_row, bias_at):
-        gain = self.norms[pl.ds(gain_row, 1), :]
-        shift = self.norms[pl.ds(shift_row, 1), :]
+    def norm(self, target, gain_ref, shift_ref, layer, bias_at):
+        gain = gain_ref[layer : layer + 1, :].astype(jnp.float32)
+        shift = shift_ref[layer : layer + 1, :].astype(jnp.float32)
         bias = None if bias_at is None else self.bias_row(bias_at)
 
         @pl.loop(0, ROWS // 16)
@@ -788,8 +773,8 @@
         self.saved(layer - 1, "normed")
         self.norm(
             self.normed,
+            *self.norm_refs[:2],
             layer,
-            self.layers + layer,
             None if layer == 0 else (layer - 1) * BIAS_ROWS + 4,
         )
         self.save(layer, "incoming", self.stream)
@@ -846,8 +831,8 @@
         self.saved(layer - 1, "normed_two")
         self.norm(
             self.normed_two,
-            2 * self.layers + layer,
-            3 * self.layers + layer,
+            *self.norm_refs[2:],
+            layer,
             layer * BIAS_ROWS + 3,
         )
         self.save(layer, "normed_two", self.normed_two)
@@ -916,9 +901,9 @@
         steps = self.work()
         ready = set()
         remaining = {}
-        for matrix, _, _ in self.gather.chunks:
+        for matrix, _, _, _ in self.gather.chunks:
             remaining[matrix] = remaining.get(matrix, 0) + 1
-        ticks = len(self.gather.chunks) + GATHER_DEPTH
+        ticks = len(self.gather.chunks) + GATHER_LAG * GATHER_DEPTH
         for tick in range(ticks):
             budget = WORK_A_TICK
             done = self.gather.tick(tick)
@@ -947,12 +932,12 @@
             steps.pop(0)[2]()
 
 
-WORK_A_TICK = 12
-
-
-def forward(shards, near, far, biases, norms):
+WORK_A_TICK = 5
+
+
+def forward(shards, near, far, norms, biases):
     layers = shards[0].shape[0]
-    widths = [shard.shape[2] for shard in shards]
+    widths = [3 * shards[0].shape[2], *[shard.shape[2] for shard in shards[3:]]]
     plan = Forward(layers, widths)
     project, out, up, down = widths
     low = lambda cols: jax.ShapeDtypeStruct((ROWS, cols), LOW)
@@ -968,15 +953,17 @@
     out_specs = [any_spec] * len(outs)
     out_specs[len(wholes) + 1] = vmem_spec
 
+    operands = [*shards, near, far, *norms, *biases]
+
     def kernel(*refs):
-        outputs = refs[8 : 8 + len(outs)]
-        plan.bind(refs[:8], outputs, refs[8 + len(outs) :])
+        ins, refs = refs[: len(operands)], refs[len(operands) :]
+        plan.bind(ins, refs[: len(outs)], refs[len(outs) :])
         plan.run()
 
     results = pl.pallas_call(
         kernel,
         out_shape=outs,
-        in_specs=[any_spec] * 4 + [vmem_spec, any_spec, any_spec, vmem_spec],
+        in_specs=[any_spec] * 6 + [vmem_spec, any_spec] + [vmem_spec] * 9,
         out_specs=out_specs,
         scratch_shapes=list(plan.scratch().values()),
         compiler_params=pltpu.CompilerParams(
@@ -986,7 +973,7 @@
             flops=60 * 1024**3, bytes_accessed=700 * 1024 * 1024, transcendentals=0
         ),
         name="forward",
-    )(*shards, near, far, biases, norms)
+    )(*operands)
     whole, results = results[: len(wholes)], results[len(wholes) :]
     weights = [
         [whole[layer * 4 + kind] for kind in range(4)] for layer in range(layers)
@@ -998,9 +985,11 @@
     return weights, cotangent_in, activations, kept
 
 
-COLS = 256
-SETTLE_DEPTH = 6
-VAL_SLOTS, ARRIVAL_SLOTS, REST_SLOTS, TURNED_SLOTS = 2, 2, 4, 3
+COLS = 128
+STAGE_AT = (0, 1, 3, 5, 6, 7, 8)
+SETTLE_DEPTH = len(STAGE_AT) - 1
+SLOTS = dict(core_in=2, val=5, first_a=4, first_b=4, second=4, third=2, fourth=2, fifth=2, rest=4)
+TURNED_SLOTS = 3
 
 
 class Settle:
@@ -1008,23 +997,24 @@
         self.widths, self.pairs = widths, pairs
 
     def scratch(self):
-        rows = (4, 2, 2, BLOCK, COLS)
-        pairs, slots = len(self.pairs), ARRIVAL_SLOTS
-        sem = pltpu.SemaphoreType.DMA
+        shapes = dict(
+            core_in=(2, 2, 4, 2, 2, BLOCK, COLS),
+            val=(2, 2, 4, 2, 2, BLOCK, COLS),
+            first_a=(4, 2, 2, BLOCK, COLS),
+            first_b=(2, 4, 2, BLOCK, COLS),
+            second=(2, 4, 2, BLOCK, COLS),
+            third=(2, 2, 2, BLOCK, COLS),
+            fourth=(2, 2, BLOCK, COLS),
+            fifth=(2, BLOCK, COLS),
+            rest=(2, 4, 2, BLOCK, COLS),
+        )
+        pairs, sem = len(self.pairs), pltpu.SemaphoreType.DMA
         return dict(
             left_in=pltpu.VMEM((ROWS, 1024), LOW),
             left_turned=pltpu.VMEM((TURNED_SLOTS, 1024, DEEP), LOW),
-            right_in=pltpu.VMEM((2, 2, 4, DEEP, COLS), LOW),
-            core_out=pltpu.VMEM((2, 2, *rows), LOW),
-            core_in=pltpu.VMEM((slots, 2, 2, *rows), LOW),
-            val=pltpu.VMEM((VAL_SLOTS, 2, 2, *rows), LOW),
-            rest=pltpu.VMEM((REST_SLOTS, 2, 4, 2, BLOCK, COLS), LOW),
-            first_a=pltpu.VMEM((slots, *rows), LOW),
-            first_b=pltpu.VMEM((slots, 2, 4, 2, BLOCK, COLS), LOW),
-            second=pltpu.VMEM((slots, 2, 4, 2, BLOCK, COLS), LOW),
-            third=pltpu.VMEM((slots, 2, 2, 2, BLOCK, COLS), LOW),
-            fourth=pltpu.VMEM((slots, 2, 2, BLOCK, COLS), LOW),
-            fifth=pltpu.VMEM((slots, 2, BLOCK, COLS), LOW),
+            right_in=pltpu.VMEM((2, 2, 2, DEEP, 2 * COLS), LOW),
+            core_out=pltpu.VMEM((2, 2, 4, 2, 2, BLOCK, COLS), LOW),
+            **{name: pltpu.VMEM((SLOTS[name], *shape), LOW) for name, shape in shapes.items()},
             result=pltpu.VMEM((2, 2, 2, BLOCK, COLS), jnp.float32),
             result_sem=sem((2, 2, 2)),
             send_sem=sem((pairs, 2, SETTLE_DEPTH)),
@@ -1045,22 +1035,25 @@
             (TURNED_SLOTS, 1024, DEEP - tail), LOW
         )
         self.right_in[:, :, :, pl.ds(ROWS, DEEP - ROWS)] = jnp.zeros(
-            (2, 2, 4, DEEP - ROWS, COLS), LOW
+            (2, 2, 2, DEEP - ROWS, 2 * COLS), LOW
         )
 
     def load(self, pair):
         for unit, (matrix, step) in enumerate(self.pairs[pair]):
             width = self.widths[matrix]
             for t in range(2):
-                for core in range(2):
-                    at = t * width + core * (width // 2) + step * COLS
+                for near in range(2):
+                    core = self.c if near else 1 - self.c
+                    at = pl.multiple_of(t * width + core * (width // 2) + step * COLS, COLS)
                     copy = pltpu.make_async_copy(
                         self.rights[matrix].at[:, pl.ds(at, COLS)],
-                        self.right_in.at[pair % 2, unit, 2 * t + core, pl.ds(0, ROWS)],
-                        self.right_sem.at[pair, unit, 2 * t + core],
+                        self.right_in.at[
+                            pair % 2, unit, t, pl.ds(0, ROWS), pl.ds(near * COLS, COLS)
+                        ],
+                        self.right_sem.at[pair, unit, 2 * t + near],
                     )
                     copy.start()
-                    self.copies[(pair, unit, "right", 2 * t + core)] = copy
+                    self.copies[(pair, unit, "right", 2 * t + near)] = copy
 
     def turn(self, matrix):
         if matrix in self.turned:
@@ -1095,54 +1088,61 @@
         copy.start()
         self.copies[(pair, unit, stage)] = copy
 
-    def product(self, pair, unit, t, core, z):
+    def product(self, pair, unit, t, z):
         matrix, _ = self.pairs[pair][unit]
         at = pl.multiple_of(z * 256, 256)
         left = self.left_turned[self.turned[matrix], pl.ds(at, 256), :]
-        right = self.right_in[pair % 2, unit, 2 * t + core]
+        right = self.right_in[pair % 2, unit, t]
         total = dot_rows(left[:, :512], right[:512]) + dot_rows(left[:, 512:], right[512:])
-        return total.reshape(2, 2, BLOCK, COLS)
+        return total.astype(LOW)
 
     def stage(self, pair, unit, stage):
         if pair < 0 or pair >= len(self.pairs):
             return
         z, x, c, y = self.z, self.x, self.c, self.y
-        arrival = pair % ARRIVAL_SLOTS
         high, lower = lax.div(z, 2), lax.rem(z, 2)
         far_pair = pl.ds(2 * (1 - high), 2)
         far_z = z + 1 - 2 * lower
-        val, rest = self.val.at[pair % VAL_SLOTS, unit], self.rest.at[pair % REST_SLOTS, unit]
+
+        def buffer(name):
+            return getattr(self, name).at[pair % SLOTS[name], unit]
+
+        val, rest = buffer("val"), buffer("rest")
+        first_a = self.first_a.at[pair % SLOTS["first_a"]]
+        first_b = self.first_b.at[pair % SLOTS["first_b"]]
+        shape = (2, 2, BLOCK, COLS)
         if stage == 0:
             out = self.core_out.at[unit]
 
             @pl.loop(0, 4)
             def _(row):
                 for t in range(2):
-                    out[t, row] = self.product(pair, unit, t, 1 - c, row).astype(LOW)
-
-            self.send(pair, unit, 0, out, self.core_in.at[arrival, unit], "core")
+                    total = self.product(pair, unit, t, row)
+                    out[t, row] = total[:, :COLS].reshape(shape)
+                    val[t, row] = total[:, COLS:].reshape(shape)
+
+            self.send(pair, unit, 0, out, buffer("core_in"), "core")
             return
         self.copies.pop((pair, unit, stage - 1)).wait()
         if stage == 1:
-            other = self.core_in.at[arrival, unit]
+            other = buffer("core_in")
 
             @pl.loop(0, 4)
             def _(row):
                 for t in range(2):
-                    total = self.product(pair, unit, t, c, row)
-                    val[t, row] = (total + other[t, row].astype(jnp.float32)).astype(LOW)
+                    val[t, row] = val[t, row] + other[t, row]
 
             if unit == 0:
-                self.send(pair, unit, 1, val.at[1 - y], self.first_a.at[arrival], "y")
+                self.send(pair, unit, 1, val.at[1 - y], first_a, "y")
             else:
-                self.send(pair, unit, 1, val.at[:, :, 1 - x], self.first_b.at[arrival], "x")
+                self.send(pair, unit, 1, val.at[:, :, 1 - x], first_b, "x")
         elif stage == 2:
-            target = self.second.at[arrival, unit]
+            target = buffer("second")
             if unit == 0:
 
                 @pl.loop(0, 4)
                 def _(row):
-                    val[y, row] = val[y, row] + self.first_a[arrival, row]
+                    val[y, row] = val[y, row] + first_a[row]
 
                 self.send(pair, unit, 2, val.at[y, :, 1 - x], target, "x")
             else:
@@ -1150,24 +1150,27 @@
                 @pl.loop(0, 4)
                 def _(row):
                     for t in range(2):
-                        val[t, row, x] = val[t, row, x] + self.first_b[arrival, t, row]
+                        val[t, row, x] = val[t, row, x] + first_b[t, row]
 
                 self.send(pair, unit, 2, val.at[1 - y, :, x], target, "y")
         elif stage == 3:
 
+            second = buffer("second")
+
             @pl.loop(0, 4)
             def _(row):
-                rest[row] = val[y, row, x] + self.second[arrival, unit, row]
-
-            self.send(pair, unit, 3, rest.at[far_pair], self.third.at[arrival, unit], "z2")
+                rest[row] = val[y, row, x] + second[row]
+
+            self.send(pair, unit, 3, rest.at[far_pair], buffer("third"), "z2")
         elif stage == 4:
+            third = buffer("third")
             for row in range(2):
                 at = 2 * high + row
-                rest[at] = rest[at] + self.third[arrival, unit, row]
-            self.send(pair, unit, 4, rest.at[far_z], self.fourth.at[arrival, unit], "z1")
+                rest[at] = rest[at] + third[row]
+            self.send(pair, unit, 4, rest.at[far_z], buffer("fourth"), "z1")
         elif stage == 5:
-            rest[z] = rest[z] + self.fourth[arrival, unit]
-            self.send(pair, unit, 5, rest.at[z, 1 - c], self.fifth.at[arrival, unit], "core")
+            rest[z] = rest[z] + buffer("fourth")[...]
+            self.send(pair, unit, 5, rest.at[z, 1 - c], buffer("fifth"), "core")
         else:
             matrix, step = self.pairs[pair][unit]
             out_ref, layer = self.outs[matrix]
@@ -1176,7 +1179,7 @@
                 copy.wait()
             result = self.result.at[slot, unit]
             result[c] = rest[z, c].astype(jnp.float32)
-            result[1 - c] = self.fifth[arrival, unit].astype(jnp.float32)
+            result[1 - c] = buffer("fifth")[...].astype(jnp.float32)
             self.results[(slot, unit)] = []
             for core in range(2):
                 copy = pltpu.make_async_copy(
@@ -1195,7 +1198,7 @@
     def tick(self, pair):
         for stage in range(SETTLE_DEPTH, 0, -1):
             for unit in range(2):
-                self.stage(pair - stage, unit, stage)
+                self.stage(pair - STAGE_AT[stage], unit, stage)
         if pair < len(self.pairs):
             self.wait_load(pair)
             for unit in range(2):
@@ -1269,11 +1272,11 @@
         self.kept = [
             dict(zip(KEPT, inputs[k * len(KEPT) : (k + 1) * len(KEPT)])) for k in range(layers)
         ]
-        self.upstream, self.gains, self.leaving = inputs[layers * len(KEPT) :]
+        self.upstream, self.leaving, *self.gains = inputs[layers * len(KEPT) :]
         outs, outputs = outputs[:4], outputs[4:]
         self.total_out, self.near_out, self.arriving, outputs = (*outputs[:3], outputs[3:])
         self.hidden_grads = outputs
-        self.facts = set()
+        self.facts, self.hidden_copies = set(), []
         lefts, rights = [], []
         for layer in range(layers):
             kept = self.kept[layer]
@@ -1332,83 +1335,66 @@
         self.row_loop(body)
         self.put_sum(self.layers - 1, 7, jnp.sum(self.sums_part[2], axis=0, keepdims=True))
 
-    def tiles(self, first, last, sources, targets, body):
-        def copies(part, slot):
-            cols = pl.ds(pl.multiple_of(part * TILE, TILE), TILE)
-            return [
-                pltpu.make_async_copy(
-                    source.at[(slice(None),) * (len(source.shape) - 1) + (cols,)],
-                    target.at[slot],
-                    self.tile_sem.at[slot, entry],
-                )
-                for entry, (source, target) in enumerate(zip(sources, targets))
-            ]
-
-        for copy in copies(first, first % 2):
+    def tile_copies(self, part, sources, targets):
+        cols = pl.ds(part * TILE, TILE)
+        slot = part % 2
+        copies = []
+        for entry, (source, target) in enumerate(zip(sources, targets)):
+            at = (slice(None),) * (len(source.shape) - 1) + (cols,)
+            copy = pltpu.make_async_copy(
+                source.at[at], target.at[slot], self.tile_sem.at[slot, entry]
+            )
             copy.start()
-
-        @pl.loop(first, last)
-        def _(part):
-            slot = lax.rem(part, 2)
-
-            @pl.when(part + 1 < last)
-            def _():
-                for copy in copies(part + 1, 1 - slot):
-                    copy.start()
-
-            for copy in copies(part, slot):
-                copy.wait()
-            body(part, slot)
+            copies.append(copy)
+        return copies
+
+    def tile(self, part, parts, sources, targets):
+        if part == 0:
+            self.coming = self.tile_copies(0, sources, targets)
+        for copy in self.coming:
+            copy.wait()
+        if part + 1 < parts:
+            self.coming = self.tile_copies(part + 1, sources, targets)
 
     def add_delta(self, is_first, grads, weights):
         for half in range(2):
             cols = slice(half * 512, (half + 1) * 512)
             product = dot_cols(grads, weights[2 * half : 2 * half + 2].reshape(512, TILE))
-            before = jnp.where(is_first, 0.0, self.delta[:, cols])
-            self.delta[:, cols] = before + product
-
-    def feed(self, layer, first, last):
+            self.delta[:, cols] = product if is_first else self.delta[:, cols] + product
+
+    def feed(self, layer, part):
         out_ref = self.hidden_grads[layer]
-        if first == 0:
+        parts, slot = out_ref.shape[1] // TILE, part % 2
+        if part == 0:
             self.value_copy = self.fetch(1, self.kept[layer]["middle"], self.values)
-
-        def out_copy(part, slot):
-            cols = pl.ds(pl.multiple_of(part * TILE, TILE), TILE)
-            return pltpu.make_async_copy(
-                self.hidden_out.at[slot], out_ref.at[:, cols], self.hidden_sem.at[slot]
-            )
-
-        def body(part, slot):
-            @pl.when(part >= first + 2)
-            def _():
-                out_copy(part - 2, slot).wait()
-
-            down = self.tile_a[slot].reshape(1024, TILE)
-            slope = self.slope_in[slot].astype(jnp.float32)
-            grads = (dot_rows(self.feed_grad[...], down) * slope).astype(LOW)
-            self.hidden_out[slot] = grads
-            out_copy(part, slot).start()
-            self.column_sums[part] = jnp.sum(grads.astype(jnp.float32), axis=0, keepdims=True)
-            self.add_delta(part == 0, grads, self.tile_b.at[slot])
-
-        self.tiles(
-            first,
-            last,
-            (self.weights[layer * 4 + 3], self.weights[layer * 4 + 2], self.kept[layer]["slope"]),
-            (self.tile_a, self.tile_b, self.slope_in),
-            body,
-        )
-        for part in (last - 2, last - 1):
-            out_copy(part, part % 2).wait()
-        if last * TILE == out_ref.shape[1]:
+        sources = (self.weights[layer * 4 + 3], self.weights[layer * 4 + 2], self.kept[layer]["slope"])
+        self.tile(part, parts, sources, (self.tile_a, self.tile_b, self.slope_in))
+        if part >= 2:
+            self.hidden_copies.pop(0).wait()
+        down = self.tile_a[slot].reshape(1024, TILE)
+        slope = self.slope_in[slot].astype(jnp.float32)
+        grads = (dot_rows(self.feed_grad[...], down) * slope).astype(LOW)
+        self.hidden_out[slot] = grads
+        copy = pltpu.make_async_copy(
+            self.hidden_out.at[slot],
+            out_ref.at[:, pl.ds(part * TILE, TILE)],
+            self.hidden_sem.at[slot],
+        )
+        copy.start()
+        self.hidden_copies.append(copy)
+        self.column_sums[part] = jnp.sum(grads.astype(jnp.float32), axis=0, keepdims=True)
+        self.add_delta(part == 0, grads, self.tile_b.at[slot])
+        if part == parts - 1:
+            while self.hidden_copies:
+                self.hidden_copies.pop(0).wait()
             for row in range(4):
                 pieces = [self.column_sums[2 * row], self.column_sums[2 * row + 1]]
                 self.put_sum(layer, 3 + row, jnp.concatenate(pieces, axis=1))
             self.facts.add((layer, "fed"))
 
-    def norm_back(self, layer, gain_row, sum_row, low_ref, total_at):
+    def norm_back(self, layer, gain_ref, sum_row, low_ref, total_at):
         self.value_copy.wait()
-        gain = self.gains[pl.ds(gain_row, 1), :]
+        gain = gain_ref[layer : layer + 1, :].astype(jnp.float32)
         self.sums_part[...] = jnp.zeros_like(self.sums_part)
 
         def body(rows):
@@ -1440,16 +1426,15 @@
             self.put_sum(*total_at, total)
 
     def out_back(self, layer):
-        self.norm_back(layer, self.layers + layer, 10, self.mix_grad, (layer, 2))
+        self.norm_back(layer, self.gains[1], 10, self.mix_grad, (layer, 2))
         self.value_copy = self.fetch(1, self.kept[layer]["incoming"], self.values)
         self.projected_copy = self.fetch(2, self.kept[layer]["projected"], self.projected)
 
-        def body(part, slot):
-            cols = pl.ds(pl.multiple_of(part * TILE, TILE), TILE)
-            weights = self.tile_a[slot].reshape(1024, TILE)
+        for part in range(2):
+            self.tile(part, 2, (self.weights[layer * 4 + 1],), (self.tile_a,))
+            cols = pl.ds(part * TILE, TILE)
+            weights = self.tile_a[part].reshape(1024, TILE)
             self.heads_grad[:, cols] = dot_rows(self.mix_grad[...], weights).astype(LOW)
-
-        self.tiles(0, 2, (self.weights[layer * 4 + 1],), (self.tile_a,), body)
 
     def mix_back(self, layer, first, last):
         if first == 0:
@@ -1490,22 +1475,20 @@
         if last * PAIR == half:
             self.facts.add((layer, "mixed"))
 
-    def project_back(self, layer):
-        def body(part, slot):
-            cols = pl.ds(pl.multiple_of(part * TILE, TILE), TILE)
-            grads = self.joined[:, cols]
-            self.column_sums[part] = jnp.sum(grads.astype(jnp.float32), axis=0, keepdims=True)
-            self.add_delta(part == 0, grads, self.tile_a.at[slot])
-
-        self.tiles(0, 6, (self.weights[layer * 4],), (self.tile_a,), body)
-        for row, part in ((0, 0), (1, 2)):
-            pieces = [self.column_sums[part], self.column_sums[3 + part]]
-            self.put_sum(layer, row, jnp.concatenate(pieces, axis=1))
+    def project_back(self, layer, part):
+        self.tile(part, 6, (self.weights[layer * 4],), (self.tile_a,))
+        grads = self.joined[:, pl.ds(part * TILE, TILE)]
+        self.column_sums[part] = jnp.sum(grads.astype(jnp.float32), axis=0, keepdims=True)
+        self.add_delta(part == 0, grads, self.tile_a.at[part % 2])
+        if part == 5:
+            for row, at in ((0, 0), (1, 2)):
+                pieces = [self.column_sums[at], self.column_sums[3 + at]]
+                self.put_sum(layer, row, jnp.concatenate(pieces, axis=1))
 
     def first_back(self, layer):
         last = layer == 0
         low_ref = None if last else self.feed_grad
-        self.norm_back(layer, layer, 8, low_ref, None if last else (layer - 1, 7))
+        self.norm_back(layer, self.gains[0], 8, low_ref, None if last else (layer - 1, 7))
         if not last:
             self.facts.add((layer - 1, "arrived"))
 
@@ -1522,18 +1505,17 @@
     def chain(self):
         steps = [(1, self.begin, ()), (2, self.widen, ())]
         for layer in reversed(range(self.layers)):
-            steps += [
-                (9, lambda layer=layer: self.feed(layer, 0, 4), ()),
-                (9, lambda layer=layer: self.feed(layer, 4, 8), ()),
-                (4, lambda layer=layer: self.out_back(layer), ((layer + 1, 1),)),
-            ]
+            for part in range(2 * self.widths[2] // TILE):
+                steps.append((2.5, lambda layer=layer, part=part: self.feed(layer, part), ()))
+            steps.append((4, lambda layer=layer: self.out_back(layer), ((layer + 1, 1),)))
             for k in range(4):
                 needs = ((layer + 1, 0),)
                 steps.append((7, lambda layer=layer, k=k: self.mix_back(layer, k, k + 1), needs))
-            steps += [
-                (8, lambda layer=layer: self.project_back(layer), ()),
-                (3, lambda layer=layer: self.first_back(layer), ((layer, 3),)),
-            ]
+            for part in range(6):
+                steps.append(
+                    (1.5, lambda layer=layer, part=part: self.project_back(layer, part), ())
+                )
+            steps.append((3, lambda layer=layer: self.first_back(layer), ((layer, 3),)))
         return steps + [(1, self.end, ())]
 
     def add_sums(self, step):
@@ -1576,7 +1558,7 @@
             step()
 
         pair = 0
-        while pair < pairs + SETTLE_DEPTH or sum_step <= len(TOTAL_LINKS):
+        while pair < pairs + STAGE_AT[-1] or sum_step <= len(TOTAL_LINKS):
             if pair < pairs:
                 while self.needs[pair] not in self.facts:
                     advance()
@@ -1602,7 +1584,7 @@
             copy.wait()
 
 
-CHAIN_A_TICK = 10
+CHAIN_A_TICK = 5
 
 
 def backward(weights, kept, upstream, gains, leaving):
@@ -1612,9 +1594,9 @@
     any_spec, vmem_spec = pl.BlockSpec(memory_space=pl.ANY), pl.BlockSpec(memory_space=pltpu.VMEM)
     operands = [block for layer in weights for block in layer]
     operands += [values[name] for values in kept for name in KEPT]
-    operands += [upstream, gains, leaving]
-    in_specs = [any_spec] * len(operands)
-    in_specs[-2] = vmem_spec
+    operands += [upstream, leaving]
+    in_specs = [any_spec] * len(operands) + [vmem_spec] * len(gains)
+    operands += gains
     outs = [jax.ShapeDtypeStruct((layers, 2, BLOCK, width // 2), jnp.float32) for width in widths]
     outs += [
         jax.ShapeDtypeStruct((layers * SUM_ROWS, 1024), jnp.float32),
@@ -1682,32 +1664,27 @@
         rows = lax.dynamic_slice_in_dim(block, image * SEQ, SEQ)
         return jnp.pad(rows, ((0, ROWS - SEQ), (0, 0)))
 
-    biases = jnp.concatenate(
-        (query_bias, jnp.zeros_like(query_bias), value_bias, out_bias, down_bias, up_bias), axis=1
-    )
-    biases = biases.astype(jnp.float32).reshape(layers * BIAS_ROWS, -1)
-    biases = jnp.pad(biases, ((0, 24 - layers * BIAS_ROWS), (0, 0)))
-    norms = jnp.concatenate((first_gain, first_shift, second_gain, second_shift))
     weights, cotangent_in, activations, kept = forward(
         (
-            jnp.concatenate((query_weight, key_weight, value_weight), axis=2),
+            query_weight,
+            key_weight,
+            value_weight,
             jnp.swapaxes(out_weight, 1, 2),
             up_weight,
             jnp.swapaxes(down_weight, 1, 2),
         ),
         own_rows(images, y),
         jnp.stack((own_rows(images, far), own_rows(cotangent, far))),
-        biases,
-        norms.astype(jnp.float32),
+        (first_gain, first_shift, second_gain, second_shift),
+        (query_bias, value_bias, out_bias, down_bias, up_bias),
     )
 
     def columns(rows, t):
         return lax.dynamic_slice_in_dim(rows, t * half, half, axis=1)
 
     upstream = in_order(own_rows(cotangent, y), cotangent_in, y, 1)
-    gains = jnp.concatenate((first_gain, second_gain)).astype(jnp.float32)
     (project_out, out_out, up_out, down_out), totals, near_gradient, arriving = backward(
-        weights, kept, upstream, gains, columns(activations, far)
+        weights, kept, upstream, (first_gain, second_gain), columns(activations, far)
     )
     totals = totals.reshape(layers, -1)
     project_out, out_out, up_out, down_out = [

time: 617 us -> 594 us (0.963)
  Pallas kernels: 584 us -> 570 us
    pallas_call x1, Pallas kernels: 274 us -> 252 us  [forward(): pl.pallas_call(kernel, out_shape=outs, in_specs=[any_spec] * 6 + [vmem_sp...]
    pallas_call x1, Pallas kernels: 310 us -> 318 us  [backward(): pl.pallas_call(kernel, out_shape=outs, in_specs=in_specs, out_specs=out_s...]
where the time goes in v6:
time: 594 us; the launch traced here: 590 us
  Pallas kernels  570 us (96%)
  local copies, waits for them, and re-layouts  10.8 us (2%)
  other arithmetic  8.21 us (1%)
    pallas_call x1, Pallas kernels, backward(): pl.pallas_call(kernel, out_shape=outs, in_specs=in_specs, out_specs=out_s...  318 us
    pallas_call x1, Pallas kernels, forward(): pl.pallas_call(kernel, out_shape=outs, in_specs=[any_spec] * 6 + [vmem_sp...  252 us

profile of v6, /device:TPU:0, one launch (start us, length us, event | category | flops | bytes accessed | tf_op | source)
XLA Modules:
  0.0 590.4 jit_solution(13671226780941935902)
XLA Ops:
  0.7 2.2 constant_dynamic-slice_fusion.1
  2.9 0.9 pad.13.refs_6_
  3.8 1.1 pad_maximum_fusion.1.refs_7_
  4.9 252.3 %forward.1 = (bf16[4,2,2,64,3072]{4,3,2,1,0:T(8,128)(2,1)}, bf16[4,2,2,64,1024]{4,3,2,1,0:T(8,128)(2,1)}, bf16[4,2,2,64,4096]{4,3,2,1,0:T(8,128)(2,1)}, bf16[4,2...) custom-call(bf16[2,64,512]{2,1,0:T(8,128)(2,1)} %refs_0_.1, ...), custom_call_target="tpu_custom_call" | custom-call | flops 64424509440 | bytes 734003200 | tf_op jit(solution)/shard_map/forward/pallas_call | solution.py:963
  257.3 2.0 constant_dynamic-slice_fusion.refs_25_
  259.3 0.2 broadcast_select_fusion.1
  259.5 1.2 pad_maximum_fusion.2.refs_24_
  260.6 318.2 %backward.1 = (f32[2,2,64,768]{3,2,1,0:T(8,128)}, f32[2,2,64,256]{3,2,1,0:T(8,128)}, f32[2,2,64,1024]{3,2,1,0:T(8,128)}, f32[2,2,64,1024]{3,2,1,0:T(8,128)}, f32...) custom-call(bf16[4,2,2,64,3072]{4,3,2,1,0:T(8,128)(2,1)} %get-tuple-, ...), custom_call_target="tpu_custom_call" | custom-call | flops 128849018880 | bytes 734003200 | tf_op jit(solution)/shard_map/backward/pallas_call | solution.py:1615
  578.8 1.5 bitcast_select_fusion.1
  580.3 1.2 pad_maximum_fusion.3
  581.5 0.5 copy-done
  582.0 1.4 convert_select_fusion.1
  583.4 0.0 copy-start.3
  583.4 1.7 pad_maximum_fusion
  585.1 0.1 copy.38
  585.2 0.9 fusion
  586.0 0.0 copy-done.6
  586.1 0.1 reshape.55
  586.1 0.6 slice.70
  586.8 0.6 fusion.1
  587.4 0.0 copy-done.5
  587.4 0.7 copy.39
  588.1 1.0 copy.40
  589.2 1.1 copy.41
  (12 shorter events, 0.1 us)
Async XLA Ops:
  257.2 2.0 copy-start.4
  580.3 1.7 copy-start
  583.4 1.7 copy-start.3
  585.1 1.0 copy-start.6
  585.1 2.3 copy-start.5
  585.1 3.0 copy-start.2
  587.4 1.8 copy-start.1

commit v7 on v6

--- a/solution.py
+++ b/solution.py
@@ -494,8 +494,8 @@
     ref[pl.ds(0, SEQ), pl.ds(at, PAIR)] = jnp.concatenate(pieces, axis=1)
 
 
-def gather_stages(z, x, c, y, whole, start, width, last):
-    share = (width - last) // 2
+def gather_stages(z, x, c, y, whole, start, shares):
+    share_a, share_b, last = shares
 
     def cols(t, at, size):
         return pl.ds(pl.multiple_of(t * whole + start + at, 128), size)
@@ -506,16 +506,16 @@
     far_x, far_y = 1 - x, 1 - y
 
     def part_a(t):
-        return cols(t, 0, share)
+        return cols(t, 0, share_a)
 
     def part_b(t):
-        return cols(t, share, share)
+        return cols(t, share_a, share_b)
 
     def part_ab(t):
-        return cols(t, 0, 2 * share)
+        return cols(t, 0, share_a + share_b)
 
     def part_c(t):
-        return cols(t, 2 * share, last)
+        return cols(t, share_a + share_b, last)
 
     stages = [
         [("z1", (z, x, c, all_rows, part_ab(y)))],
@@ -552,6 +552,16 @@
 GATHER_DEPTH = 5
 GATHER_LAG = 2
 CHUNK = 512
+CHUNK_SHARES = (
+    (256, 256, 0),
+    (128, 384, 0),
+    (256, 256, 0),
+    (128, 128, 256),
+    (128, 384, 0),
+    (256, 256, 0),
+    (128, 384, 0),
+    (128, 128, 256),
+)
 
 
 class Gather:
@@ -572,9 +582,10 @@
         z, x, c, y = place()
         self.partners = neighbours()
         self.plans, self.own, self.flying = [], [], {}
-        for chunk, (matrix, start, width, last) in enumerate(self.chunks):
+        for chunk, (matrix, start, shares) in enumerate(self.chunks):
+            width = sum(shares)
             whole = wholes[matrix].shape[4] // 2
-            self.plans.append(gather_stages(z, x, c, y, whole, start, width, last))
+            self.plans.append(gather_stages(z, x, c, y, whole, start, shares))
             mine = pl.ds(pl.multiple_of(y * whole + start, 128), width)
             size = shards[matrix][0].shape[1]
             shard = shards[matrix][start // size]
@@ -624,7 +635,28 @@
 
 
 BIAS_ROWS = 9
-SAVED = ("normed", "projected", "heads", "normed_two", "hidden", "slope", "middle", "incoming")
+SAVED = (
+    "normed",
+    "projected",
+    "heads",
+    "normed_two",
+    "hidden",
+    "slope",
+    "centred",
+    "inverse",
+    "centred_two",
+    "inverse_two",
+)
+
+
+def row_loop(body):
+    @pl.loop(0, ROWS // 32)
+    def _(step):
+        body(pl.ds(pl.multiple_of(step * 32, 32), 32), 32)
+
+    left = ROWS % 32
+    if left:
+        body(pl.ds(ROWS - left, left), left)
 
 
 class Forward:
@@ -634,8 +666,8 @@
         for layer in range(layers):
             for kind, width in enumerate(widths):
                 for start in range(0, width, CHUNK):
-                    last = CHUNK // 2 if len(chunks) % 4 == 3 else 0
-                    chunks.append((layer * len(widths) + kind, start, CHUNK, last))
+                    shares = CHUNK_SHARES[len(chunks) % len(CHUNK_SHARES)]
+                    chunks.append((layer * len(widths) + kind, start, shares))
         self.gather = Gather(chunks)
 
     def scratch(self):
@@ -648,6 +680,8 @@
             weights_up=pltpu.VMEM((4, 2, 2, BLOCK, 2 * up), LOW),
             weights_down=pltpu.VMEM((4, 2, 2, BLOCK, 2 * down), LOW),
             stream=full,
+            centred=full,
+            inverse=pltpu.VMEM((ROWS, 128), jnp.float32),
             tokens_in=low(512),
             biases=pltpu.VMEM((2, self.layers * BIAS_ROWS, 512), jnp.float32),
             normed=low(1024),
@@ -670,9 +704,9 @@
         self.near, self.far, self.norm_refs, bias_refs = inputs[0], inputs[1], inputs[2:6], inputs[6:]
         count = self.layers * 4
         self.wholes, outputs = outputs[:count], outputs[count:]
-        self.cotangent_in, self.activations, outputs = outputs[0], outputs[1], outputs[2:]
+        self.cotangent_in, self.leaving, self.staying, outputs = (*outputs[:3], outputs[3:])
         self.saved_out = [outputs[k * len(SAVED) : (k + 1) * len(SAVED)] for k in range(self.layers)]
-        self.saving, self.loading = {}, {}
+        self.saving, self.loading, self.centred_saves = {}, {}, []
         self.y = lax.axis_index("tensor")
         kinds = (shards[:3], shards[3:4], shards[4:5], shards[5:6])
         self.gather.bind(
@@ -725,7 +759,8 @@
             self.saving.pop((layer, name)).wait()
 
     def load(self, chunk):
-        matrix, start, width, _ = self.gather.chunks[chunk]
+        matrix, start, shares = self.gather.chunks[chunk]
+        width = sum(shares)
         whole = self.gather.wholes[matrix]
         buffer = (self.weights_project, self.weights_out, self.weights_up, self.weights_down)[
             matrix % 4
@@ -743,14 +778,14 @@
     def bias_row(self, row):
         return jnp.concatenate([self.biases[t, pl.ds(row, 1), :] for t in range(2)], axis=1)
 
-    def norm(self, target, gain_ref, shift_ref, layer, bias_at):
+    def norm(self, target, gain_ref, shift_ref, layer, bias_at, names):
         gain = gain_ref[layer : layer + 1, :].astype(jnp.float32)
         shift = shift_ref[layer : layer + 1, :].astype(jnp.float32)
         bias = None if bias_at is None else self.bias_row(bias_at)
-
-        @pl.loop(0, ROWS // 16)
-        def _(step):
-            rows = pl.ds(pl.multiple_of(step * 16, 16), 16)
+        for key in self.centred_saves:
+            self.saved(*key)
+
+        def body(rows, size):
             values = self.stream[rows, :]
             if bias is not None:
                 values = values + bias
@@ -758,7 +793,15 @@
             mean = jnp.mean(values, axis=1, keepdims=True)
             square = jnp.mean(values * values, axis=1, keepdims=True)
             inverse = lax.rsqrt(square - mean * mean + norm_eps)
-            target[rows, :] = ((values - mean) * inverse * gain + shift).astype(LOW)
+            centred = (values - mean) * inverse
+            self.centred[rows, :] = centred
+            self.inverse[rows, :] = jnp.broadcast_to(inverse, (size, 128))
+            target[rows, :] = (centred * gain + shift).astype(LOW)
+
+        row_loop(body)
+        self.save(layer, names[0], self.centred)
+        self.save(layer, names[1], self.inverse)
+        self.centred_saves = [(layer, name) for name in names]
 
     def begin(self):
         for copy in self.swaps:
@@ -776,8 +819,8 @@
             *self.norm_refs[:2],
             layer,
             None if layer == 0 else (layer - 1) * BIAS_ROWS + 4,
+            ("centred", "inverse"),
         )
-        self.save(layer, "incoming", self.stream)
         self.save(layer, "normed", self.normed)
         self.saved(layer - 1, "projected")
         self.wait_weights(layer * 4)
@@ -820,7 +863,6 @@
 
     def attend(self, layer):
         self.wait_weights(layer * 4 + 1)
-        self.saved(layer, "incoming")
 
         @pl.loop(0, 4)
         def _(row):
@@ -834,9 +876,9 @@
             *self.norm_refs[2:],
             layer,
             layer * BIAS_ROWS + 3,
+            ("centred_two", "inverse_two"),
         )
         self.save(layer, "normed_two", self.normed_two)
-        self.save(layer, "middle", self.stream)
 
     def feed_up(self, layer, first, last):
         if first == 0:
@@ -862,7 +904,6 @@
 
     def feed_down(self, layer, first, last):
         if first == 0:
-            self.saved(layer, "middle")
             self.wait_weights(layer * 4 + 3)
 
         @pl.loop(first, last)
@@ -872,12 +913,15 @@
             self.stream[:, cols] = self.stream[:, cols] + dot_cols(self.hidden[...], weights)
 
     def end(self):
-        bias = self.bias_row((self.layers - 1) * BIAS_ROWS + 4)
-
-        @pl.loop(0, ROWS // 16)
-        def _(step):
-            rows = pl.ds(pl.multiple_of(step * 16, 16), 16)
-            self.activations[rows, :] = (self.stream[rows, :] + bias).astype(LOW)
+        row = (self.layers - 1) * BIAS_ROWS + 4
+        for t, ref in ((self.y, self.staying), (1 - self.y, self.leaving)):
+            bias = self.biases[t, pl.ds(row, 1), :]
+            cols = pl.ds(pl.multiple_of(t * 512, 512), 512)
+
+            def body(rows, _, ref=ref, bias=bias, cols=cols):
+                ref[rows, :] = (self.stream[rows, cols] + bias).astype(LOW)
+
+            row_loop(body)
 
     def work(self):
         steps = [(0, 1, self.begin)]
@@ -901,7 +945,7 @@
         steps = self.work()
         ready = set()
         remaining = {}
-        for matrix, _, _, _ in self.gather.chunks:
+        for matrix, _, _ in self.gather.chunks:
             remaining[matrix] = remaining.get(matrix, 0) + 1
         ticks = len(self.gather.chunks) + GATHER_LAG * GATHER_DEPTH
         for tick in range(ticks):
@@ -942,16 +986,18 @@
     project, out, up, down = widths
     low = lambda cols: jax.ShapeDtypeStruct((ROWS, cols), LOW)
     full = jax.ShapeDtypeStruct((ROWS, 1024), jnp.float32)
+    lanes = jax.ShapeDtypeStruct((ROWS, 128), jnp.float32)
     saved = [
-        low(1024), low(2 * project), low(2 * out), low(1024), low(2 * up), low(2 * up), full, full
+        low(1024), low(2 * project), low(2 * out), low(1024), low(2 * up), low(2 * up),
+        full, lanes, full, lanes,
     ]
     wholes = [
         jax.ShapeDtypeStruct((4, 2, 2, BLOCK, 2 * width), LOW) for width in widths
     ] * layers
-    outs = [*wholes, low(512), low(1024), *(saved * layers)]
+    outs = [*wholes, low(512), low(512), low(512), *(saved * layers)]
     any_spec, vmem_spec = pl.BlockSpec(memory_space=pl.ANY), pl.BlockSpec(memory_space=pltpu.VMEM)
     out_specs = [any_spec] * len(outs)
-    out_specs[len(wholes) + 1] = vmem_spec
+    out_specs[len(wholes) + 1 : len(wholes) + 3] = [vmem_spec] * 2
 
     operands = [*shards, near, far, *norms, *biases]
 
@@ -978,11 +1024,11 @@
     weights = [
         [whole[layer * 4 + kind] for kind in range(4)] for layer in range(layers)
     ]
-    cotangent_in, activations, results = results[0], results[1], results[2:]
+    swapped, results = results[:3], results[3:]
     kept = [
         dict(zip(SAVED, results[k * len(SAVED) : (k + 1) * len(SAVED)])) for k in range(layers)
     ]
-    return weights, cotangent_in, activations, kept
+    return weights, swapped, kept
 
 
 COLS = 128
@@ -1088,10 +1134,9 @@
         copy.start()
         self.copies[(pair, unit, stage)] = copy
 
-    def product(self, pair, unit, t, z):
+    def product(self, pair, unit, t):
         matrix, _ = self.pairs[pair][unit]
-        at = pl.multiple_of(z * 256, 256)
-        left = self.left_turned[self.turned[matrix], pl.ds(at, 256), :]
+        left = self.left_turned[self.turned[matrix]]
         right = self.right_in[pair % 2, unit, t]
         total = dot_rows(left[:, :512], right[:512]) + dot_rows(left[:, 512:], right[512:])
         return total.astype(LOW)
@@ -1110,16 +1155,15 @@
         val, rest = buffer("val"), buffer("rest")
         first_a = self.first_a.at[pair % SLOTS["first_a"]]
         first_b = self.first_b.at[pair % SLOTS["first_b"]]
-        shape = (2, 2, BLOCK, COLS)
+        shape = (4, 2, 2, BLOCK, COLS)
         if stage == 0:
             out = self.core_out.at[unit]
 
-            @pl.loop(0, 4)
-            def _(row):
-                for t in range(2):
-                    total = self.product(pair, unit, t, row)
-                    out[t, row] = total[:, :COLS].reshape(shape)
-                    val[t, row] = total[:, COLS:].reshape(shape)
+            @pl.loop(0, 2)
+            def _(t):
+                total = self.product(pair, unit, t)
+                out[t] = total[:, :COLS].reshape(shape)
+                val[t] = total[:, COLS:].reshape(shape)
 
             self.send(pair, unit, 0, out, buffer("core_in"), "core")
             return
@@ -1208,7 +1252,7 @@
 TOTAL_LINKS = ("x", "y", "z1", "z2", "core")
 SUM_ROWS = 12
 TILE = 512
-KEPT = ("normed", "projected", "heads", "normed_two", "hidden", "slope", "middle", "incoming")
+KEPT = SAVED
 
 
 class Backward:
@@ -1238,7 +1282,8 @@
         own = dict(
             grad=full,
             delta=full,
-            values=full,
+            centred=full,
+            inverse=pltpu.VMEM((ROWS, 128), jnp.float32),
             feed_grad=low,
             mix_grad=low,
             heads_grad=low,
@@ -1255,7 +1300,7 @@
             leave=pltpu.VMEM((ROWS, 512), LOW),
             tile_sem=sem((2, 3)),
             hidden_sem=sem((2,)),
-            value_sem=sem((3,)),
+            value_sem=sem((4,)),
             sums_send=sem((steps,)),
             sums_recv=sem((steps,)),
             swap_send=sem((2,)),
@@ -1272,7 +1317,8 @@
         self.kept = [
             dict(zip(KEPT, inputs[k * len(KEPT) : (k + 1) * len(KEPT)])) for k in range(layers)
         ]
-        self.upstream, self.leaving, *self.gains = inputs[layers * len(KEPT) :]
+        *self.upstream, self.leaving, first_gain, second_gain = inputs[layers * len(KEPT) :]
+        self.gains = (first_gain, second_gain)
         outs, outputs = outputs[:4], outputs[4:]
         self.total_out, self.near_out, self.arriving, outputs = (*outputs[:3], outputs[3:])
         self.hidden_grads = outputs
@@ -1300,6 +1346,12 @@
         copy.start()
         return copy
 
+    def fetch_centred(self, layer, centred, inverse):
+        self.centred_copies = [
+            self.fetch(1, self.kept[layer][centred], self.centred),
+            self.fetch(3, self.kept[layer][inverse], self.inverse),
+        ]
+
     def swap(self, entry, source):
         copy = pltpu.make_async_remote_copy(
             src_ref=source,
@@ -1312,27 +1364,31 @@
         copy.start()
         return copy
 
-    def row_loop(self, body):
-        @pl.loop(0, ROWS // 16)
-        def _(step):
-            body(pl.ds(pl.multiple_of(step * 16, 16), 16))
+    def add_sum(self, entry, values):
+        for start in range(0, values.shape[0], 16):
+            self.sums_part[entry] += values[start : start + 16]
 
     def put_sum(self, layer, row, values):
         self.sums[0, pl.ds(layer * SUM_ROWS + row, 1), :] = values
 
     def begin(self):
-        self.fetch(0, self.upstream, self.feed_grad).wait()
+        copies = []
+        for entry, t in enumerate((self.y, 1 - self.y)):
+            cols = pl.ds(pl.multiple_of(t * 512, 512), 512)
+            copies.append(self.fetch(entry, self.upstream[entry], self.feed_grad.at[:, cols]))
+        for copy in copies:
+            copy.wait()
         self.facts.add((self.layers - 1, "arrived"))
 
     def widen(self):
         self.sums_part[...] = jnp.zeros_like(self.sums_part)
 
-        def body(rows):
+        def body(rows, _):
             values = self.feed_grad[rows, :].astype(jnp.float32)
             self.grad[rows, :] = values
-            self.sums_part[2] += values
-
-        self.row_loop(body)
+            self.add_sum(2, values)
+
+        row_loop(body)
         self.put_sum(self.layers - 1, 7, jnp.sum(self.sums_part[2], axis=0, keepdims=True))
 
     def tile_copies(self, part, sources, targets):
@@ -1366,7 +1422,7 @@
         out_ref = self.hidden_grads[layer]
         parts, slot = out_ref.shape[1] // TILE, part % 2
         if part == 0:
-            self.value_copy = self.fetch(1, self.kept[layer]["middle"], self.values)
+            self.fetch_centred(layer, "centred_two", "inverse_two")
         sources = (self.weights[layer * 4 + 3], self.weights[layer * 4 + 2], self.kept[layer]["slope"])
         self.tile(part, parts, sources, (self.tile_a, self.tile_b, self.slope_in))
         if part >= 2:
@@ -1393,31 +1449,28 @@
             self.facts.add((layer, "fed"))
 
     def norm_back(self, layer, gain_ref, sum_row, low_ref, total_at):
-        self.value_copy.wait()
+        for copy in self.centred_copies:
+            copy.wait()
         gain = gain_ref[layer : layer + 1, :].astype(jnp.float32)
         self.sums_part[...] = jnp.zeros_like(self.sums_part)
 
-        def body(rows):
-            stream, delta = self.values[rows, :], self.delta[rows, :]
-            mean = jnp.mean(stream, axis=1, keepdims=True)
-            square = jnp.mean(stream * stream, axis=1, keepdims=True)
-            inverse = lax.rsqrt(square - mean * mean + norm_eps)
-            centred = (stream - mean) * inverse
+        def body(rows, _):
+            centred, delta = self.centred[rows, :], self.delta[rows, :]
             weighted = delta * centred
-            self.sums_part[0] += weighted
-            self.sums_part[1] += delta
+            self.add_sum(0, weighted)
+            self.add_sum(1, delta)
             scaled = delta * gain
-            grad = self.grad[rows, :] + inverse * (
+            grad = self.grad[rows, :] + self.inverse[rows, 0:1] * (
                 scaled
                 - jnp.mean(scaled, axis=1, keepdims=True)
                 - centred * jnp.mean(weighted * gain, axis=1, keepdims=True)
             )
             self.grad[rows, :] = grad
-            self.sums_part[2] += grad
+            self.add_sum(2, grad)
             if low_ref is not None:
                 low_ref[rows, :] = grad.astype(LOW)
 
-        self.row_loop(body)
+        row_loop(body)
         for entry in range(2):
             total = jnp.sum(self.sums_part[entry], axis=0, keepdims=True)
             self.put_sum(layer, sum_row + entry, total)
@@ -1427,7 +1480,7 @@
 
     def out_back(self, layer):
         self.norm_back(layer, self.gains[1], 10, self.mix_grad, (layer, 2))
-        self.value_copy = self.fetch(1, self.kept[layer]["incoming"], self.values)
+        self.fetch_centred(layer, "centred", "inverse")
         self.projected_copy = self.fetch(2, self.kept[layer]["projected"], self.projected)
 
         for part in range(2):
@@ -1594,7 +1647,7 @@
     any_spec, vmem_spec = pl.BlockSpec(memory_space=pl.ANY), pl.BlockSpec(memory_space=pltpu.VMEM)
     operands = [block for layer in weights for block in layer]
     operands += [values[name] for values in kept for name in KEPT]
-    operands += [upstream, leaving]
+    operands += [*upstream, leaving]
     in_specs = [any_spec] * len(operands) + [vmem_spec] * len(gains)
     operands += gains
     outs = [jax.ShapeDtypeStruct((layers, 2, BLOCK, width // 2), jnp.float32) for width in widths]
@@ -1664,7 +1717,7 @@
         rows = lax.dynamic_slice_in_dim(block, image * SEQ, SEQ)
         return jnp.pad(rows, ((0, ROWS - SEQ), (0, 0)))
 
-    weights, cotangent_in, activations, kept = forward(
+    weights, (cotangent_in, leaving, staying), kept = forward(
         (
             query_weight,
             key_weight,
@@ -1679,12 +1732,12 @@
         (query_bias, value_bias, out_bias, down_bias, up_bias),
     )
 
-    def columns(rows, t):
-        return lax.dynamic_slice_in_dim(rows, t * half, half, axis=1)
-
-    upstream = in_order(own_rows(cotangent, y), cotangent_in, y, 1)
     (project_out, out_out, up_out, down_out), totals, near_gradient, arriving = backward(
-        weights, kept, upstream, (first_gain, second_gain), columns(activations, far)
+        weights,
+        kept,
+        (own_rows(cotangent, y), cotangent_in),
+        (first_gain, second_gain),
+        leaving,
     )
     totals = totals.reshape(layers, -1)
     project_out, out_out, up_out, down_out = [
@@ -1697,7 +1750,7 @@
         small_outs.append(totals[:, at : at + size])
         at += size
     return (
-        in_order(columns(activations, y)[:SEQ], arriving[0, :SEQ], y, 0),
+        in_order(staying[:SEQ], arriving[0, :SEQ], y, 0),
         in_order(near_gradient[:SEQ], arriving[1, :SEQ].astype(jnp.float32), y, 0),
         project_out[:, :, :half],
         project_out[:, :, half : 2 * half],

time: 594 us -> 572 us (0.963)
  Pallas kernels: 570 us -> 549 us
    pallas_call x1, Pallas kernels: 318 us -> 290 us  [backward(): pl.pallas_call(kernel, out_shape=outs, in_specs=in_specs, out_specs=out_s...]
    pallas_call x1, Pallas kernels: 252 us -> 259 us  [forward(): pl.pallas_call(kernel, out_shape=outs, in_specs=[any_spec] * 6 + [vmem_sp...]
where the time goes in v7:
time: 572 us; the launch traced here: 567 us
  Pallas kernels  549 us (96%)
  local copies, waits for them, and re-layouts  12.5 us (2%)
    pallas_call x1, Pallas kernels, backward(): pl.pallas_call(kernel, out_shape=outs, in_specs=in_specs, out_specs=out_s...  290 us
    pallas_call x1, Pallas kernels, forward(): pl.pallas_call(kernel, out_shape=outs, in_specs=[any_spec] * 6 + [vmem_sp...  259 us

profile of v7, /device:TPU:0, one launch (start us, length us, event | category | flops | bytes accessed | tf_op | source)
XLA Modules:
  0.0 567.3 jit_solution(16592930736867812298)
XLA Ops:
  0.7 2.2 constant_dynamic-slice_fusion
  2.9 0.9 pad.16.refs_28_
  3.7 0.9 pad.13.refs_6_
  4.7 1.1 pad_maximum_fusion.1.refs_7_
  5.8 259.3 %forward.1 = (bf16[4,2,2,64,3072]{4,3,2,1,0:T(8,128)(2,1)}, bf16[4,2,2,64,1024]{4,3,2,1,0:T(8,128)(2,1)}, bf16[4,2,2,64,4096]{4,3,2,1,0:T(8,128)(2,1)}, bf16[4,2...) custom-call(bf16[2,64,512]{2,1,0:T(8,128)(2,1)} %refs_0_.1, ...), custom_call_target="tpu_custom_call" | custom-call | flops 64424509440 | bytes 734003200 | tf_op jit(solution)/shard_map/forward/pallas_call | solution.py:1009
  265.1 289.9 %backward.1 = (f32[2,2,64,768]{3,2,1,0:T(8,128)}, f32[2,2,64,256]{3,2,1,0:T(8,128)}, f32[2,2,64,1024]{3,2,1,0:T(8,128)}, f32[2,2,64,1024]{3,2,1,0:T(8,128)}, f32...) custom-call(bf16[4,2,2,64,3072]{4,3,2,1,0:T(8,128)(2,1)} %get-tuple-, ...), custom_call_target="tpu_custom_call" | custom-call | flops 128849018880 | bytes 734003200 | tf_op jit(solution)/shard_map/backward/pallas_call | solution.py:1668
  555.0 1.2 copy.38
  556.3 0.0 copy-start.5
  556.3 0.0 copy-start
  556.3 0.0 copy-start.4
  556.3 0.9 fusion
  557.2 0.1 reshape.55
  557.3 0.6 slice.70
  557.9 0.6 fusion.1
  558.5 0.7 copy.39
  559.3 0.1 bitcast_select_fusion.1
  559.4 1.2 copy-done.1
  560.5 0.3 convert_select_fusion.1
  560.9 1.7 pad_maximum_fusion
  562.5 1.2 pad_maximum_fusion.2
  563.7 0.4 copy-done.3
  564.1 1.0 copy.40
  565.1 0.6 copy-done.2
  565.7 1.1 copy.41
  (10 shorter events, 0.1 us)
Async XLA Ops:
  555.0 2.2 copy-start.6
  556.3 2.3 copy-start.5
  556.3 3.0 copy-start
  556.3 3.0 copy-start.4
  559.3 1.3 copy-start.1
  562.5 1.6 copy-start.3
  564.1 1.6 copy-start.2

commit v8 on v7

--- a/solution.py
+++ b/solution.py
@@ -501,7 +501,7 @@
         return pl.ds(pl.multiple_of(t * whole + start + at, 128), size)
 
     all_rows = pl.ds(0, BLOCK)
-    pair = pl.ds(lax.div(z, 2) * 2, 2)
+    met = (z, lax.rem(z + 2, 4))
     every_z, every_x = pl.ds(0, 4), pl.ds(0, 2)
     far_x, far_y = 1 - x, 1 - y
 
@@ -518,8 +518,8 @@
         return cols(t, share_a + share_b, last)
 
     stages = [
-        [("z1", (z, x, c, all_rows, part_ab(y)))],
-        [("z2", (pair, x, c, all_rows, part_ab(y)))],
+        [("z2", (z, x, c, all_rows, part_ab(y)))],
+        [("z1", (row, x, c, all_rows, part_ab(y))) for row in met],
         [
             ("x", (every_z, x, c, all_rows, part_a(y))),
             ("y", (every_z, x, c, all_rows, part_b(y))),
@@ -542,25 +542,22 @@
         stages[0].append(("x", (z, x, c, all_rows, part_c(y))))
         stages[1].append(("y", (z, every_x, c, all_rows, part_c(y))))
         for t in range(2):
-            stages[2].append(("z1", (z, every_x, c, all_rows, part_c(t))))
-            stages[3].append(("z2", (pair, every_x, c, all_rows, part_c(t))))
+            stages[2].append(("z2", (z, every_x, c, all_rows, part_c(t))))
+            stages[3] += [("z1", (row, every_x, c, all_rows, part_c(t))) for row in met]
             stages[4].append(("core", (every_z, every_x, c, all_rows, part_c(t))))
     return stages
 
 
-GATHER_COPIES = 21
+GATHER_COPIES = 24
 GATHER_DEPTH = 5
 GATHER_LAG = 2
 CHUNK = 512
 CHUNK_SHARES = (
+    (128, 256, 128),
+    (256, 128, 128),
     (256, 256, 0),
-    (128, 384, 0),
-    (256, 256, 0),
-    (128, 128, 256),
-    (128, 384, 0),
-    (256, 256, 0),
-    (128, 384, 0),
-    (128, 128, 256),
+    (128, 256, 128),
+    (256, 128, 128),
 )
 
 

time: 572 us -> 557 us (0.974)
  Pallas kernels: 549 us -> 533 us
    pallas_call x1, Pallas kernels: 259 us -> 243 us  [forward(): pl.pallas_call(kernel, out_shape=outs, in_specs=[any_spec] * 6 + [vmem_sp...]
where the time goes in v8:
time: 557 us; the launch traced here: 551 us
  Pallas kernels  533 us (96%)
  local copies, waits for them, and re-layouts  12.5 us (2%)
    pallas_call x1, Pallas kernels, backward(): pl.pallas_call(kernel, out_shape=outs, in_specs=in_specs, out_specs=out_s...  290 us
    pallas_call x1, Pallas kernels, forward(): pl.pallas_call(kernel, out_shape=outs, in_specs=[any_spec] * 6 + [vmem_sp...  243 us

profile of v8, /device:TPU:0, one launch (start us, length us, event | category | flops | bytes accessed | tf_op | source)
XLA Modules:
  0.0 550.8 jit_solution(4916965386661376424)
XLA Ops:
  0.7 2.2 constant_dynamic-slice_fusion
  2.9 0.9 pad.16.refs_28_
  3.7 0.9 pad.13.refs_6_
  4.7 1.1 pad_maximum_fusion.1.refs_7_
  5.8 242.9 %forward.1 = (bf16[4,2,2,64,3072]{4,3,2,1,0:T(8,128)(2,1)}, bf16[4,2,2,64,1024]{4,3,2,1,0:T(8,128)(2,1)}, bf16[4,2,2,64,4096]{4,3,2,1,0:T(8,128)(2,1)}, bf16[4,2...) custom-call(bf16[2,64,512]{2,1,0:T(8,128)(2,1)} %refs_0_.1, ...), custom_call_target="tpu_custom_call" | custom-call | flops 64424509440 | bytes 734003200 | tf_op jit(solution)/shard_map/forward/pallas_call | solution.py:1006
  248.7 290.2 %backward.1 = (f32[2,2,64,768]{3,2,1,0:T(8,128)}, f32[2,2,64,256]{3,2,1,0:T(8,128)}, f32[2,2,64,1024]{3,2,1,0:T(8,128)}, f32[2,2,64,1024]{3,2,1,0:T(8,128)}, f32...) custom-call(bf16[4,2,2,64,3072]{4,3,2,1,0:T(8,128)(2,1)} %get-tuple-, ...), custom_call_target="tpu_custom_call" | custom-call | flops 128849018880 | bytes 734003200 | tf_op jit(solution)/shard_map/backward/pallas_call | solution.py:1665
  538.9 0.0 copy-start.6
  538.9 1.2 copy.38
  540.1 0.0 copy-start.5
  540.1 0.9 fusion
  541.0 0.1 reshape.55
  541.1 0.6 slice.70
  541.7 0.6 fusion.1
  542.4 0.7 copy.39
  543.1 0.0 copy-done.4
  543.1 0.1 bitcast_select_fusion.1
  543.2 1.2 copy-done.1
  544.4 0.3 convert_select_fusion.1
  544.7 1.7 pad_maximum_fusion
  546.4 1.2 pad_maximum_fusion.2
  547.5 0.4 copy-done.3
  547.9 1.0 copy.40
  549.0 0.6 copy-done.2
  549.5 1.1 copy.41
  (10 shorter events, 0.1 us)
Async XLA Ops:
  538.9 2.2 copy-start.6
  540.1 2.3 copy-start.5
  540.1 3.0 copy-start
  540.1 3.0 copy-start.4
  543.1 1.3 copy-start.1
  546.4 1.6 copy-start.3
  547.9 1.6 copy-start.2
